TPU v7x, 32 devices: a whole 2x2x4 slice. The times are simulated.
32 devices in a mesh: seq: 8 (over z, x), tp: 4 (over y, core).
Axes of the slice: x: 2, y: 2, z: 4, core: 2. Of those that a mesh axis runs over, the one named last changes fastest.
Arguments:
- tokens: bfloat16 [2, 4096, 1024], P(None, ('seq', 'tp')), may hold values from -6 to 6
- out_grad: bfloat16 [2, 4096, 1024], P(None, ('seq', 'tp')), may hold values from -6 to 6
- norm_gain: float32 [1024], replicated, may hold values from 0.5 to 1.5
- w_query: bfloat16 [1024, 1024], P(None, 'tp'), may hold values from -0.1875 to 0.1875
- w_key: bfloat16 [1024, 1024], P(None, 'tp'), may hold values from -0.1875 to 0.1875
- w_value: bfloat16 [1024, 1024], P(None, 'tp'), may hold values from -0.1875 to 0.1875
- w_out: bfloat16 [1024, 1024], P('tp'), may hold values from -1.5 to 1.5
- mid_gain: float32 [1024], replicated, may hold values from 0.5 to 1.5
- w_up: bfloat16 [1024, 4096], P(None, 'tp'), may hold values from -0.1875 to 0.1875
- w_down: bfloat16 [4096, 1024], P('tp'), may hold values from -0.09375 to 0.09375
- ssm_rate: float32 [1024, 16], P('tp'), may hold values from 0.00048828125 to 0.1
- ssm_in: float32 [1024, 16], P('tp'), may hold values from -5 to 5
- ssm_out: float32 [1024, 16], P('tp'), may hold values from -1.5 to 1.5
- resets: int32 [2, 8], P(None, 'seq'), may hold values from 0 to 1, as said below
- init_state: float32 [2, 1024, 16], P(None, 'tp'), may hold values from -5 to 5
- states_grad: float32 [2, 8, 1024, 16], P(None, 'seq', 'tp'), may hold values from -6 to 6
Outputs:
- mixed: bfloat16 [2, 4096, 1024], P(None, ('seq', 'tp'))
- block_states: float32 [2, 8, 1024, 16], P(None, 'seq', 'tp')
- tokens_grad: float32 [2, 4096, 1024], P(None, ('seq', 'tp'))
- norm_gain_grad: float32 [1024], P('tp')
- query_grad: float32 [1024, 1024], P(None, 'tp')
- key_grad: float32 [1024, 1024], P(None, 'tp')
- value_grad: float32 [1024, 1024], P(None, 'tp')
- out_proj_grad: float32 [1024, 1024], P('tp')
- mid_gain_grad: float32 [1024], P('tp')
- up_grad: float32 [1024, 4096], P(None, 'tp')
- down_grad: float32 [4096, 1024], P('tp')
- rate_grad: float32 [1024, 16], P('tp')
- ssm_in_grad: float32 [1024, 16], P('tp')
- ssm_out_grad: float32 [1024, 16], P('tp')
Inputs may be any that keep to these rules, and one draw needn't show every extreme that they name: resets is 1 in the first block of every stream; in one stream no later block is 1.
All inputs are finite; a program needn't handle non-finite values.
Results may differ from a plain program's by a relative error of at most 0.012.
Values may be sent and summed in bfloat16 or wider, within the bound.
A program may use at most 192 MiB of HBM per device.

v0:
```python
import jax
import jax.numpy as jnp
from jax import lax
from jax.sharding import PartitionSpec as P

HD = 128
NS = 16
CTX = 128


eps_norm = 1e-06
sub_len = 128
neg_big = -1e30
highest = lax.Precision.HIGHEST


def entering(value, axis, join, neutral, backward):
    count, mine = (lax.axis_size(axis), lax.axis_index(axis))
    pieces = jax.tree.map(lambda part: lax.all_gather(part, axis), value)
    if backward:
        pieces = jax.tree.map(lambda part: part[::-1], pieces)
        mine = count - 1 - mine
    subtotal = jax.tree.map(
        lambda part, zero: jnp.full_like(part, 0) + jnp.asarray(zero, part.dtype), value, neutral
    )

    def lap(position, subtotal):
        longer = join(subtotal, jax.tree.map(lambda part: part[position], pieces))
        return jax.tree.map(lambda new, old: jnp.where(position < mine, new, old), longer, subtotal)

    return lax.fori_loop(0, count - 1, lap, subtotal)


def passed_along(x, axis, by):
    length = lax.axis_size(axis)
    pairs = [(i, i + by) for i in range(length) if 0 <= i + by < length]
    return lax.ppermute(x, axis, pairs)


def rms_norm(values, gain):
    return values * lax.rsqrt(jnp.mean(values * values, axis=-1, keepdims=True) + eps_norm) * gain


def ssm_block(inputs, start, rate, coef_in, coef_out):
    length, channels = inputs.shape
    width = min(sub_len, length)
    decay = jnp.exp(-rate)
    drive = jnp.sqrt(1.0 - decay * decay) * coef_in
    lag_steps = jnp.arange(width).astype(jnp.float32)
    powers = jnp.exp(-rate[:, :, None] * lag_steps)
    kernel = jnp.einsum("cn,cnl->cl", coef_out * drive, powers, precision=highest)
    row_ids = jnp.arange(width)[:, None]
    col_ids = jnp.arange(width)[None, :]
    lag_index = jnp.maximum(row_ids - col_ids, 0)
    toeplitz = jnp.where((row_ids >= col_ids)[None], jnp.take(kernel, lag_index, axis=1), 0.0)
    ahead = jnp.exp(-rate[:, :, None] * (lag_steps + 1.0))
    behind = jnp.flip(powers, axis=2) * drive[:, :, None]
    whole_decay = jnp.exp(-rate * width)
    pieces = inputs.reshape(length // width, width, channels)

    def advance(state, piece):
        inner = jnp.einsum("ctj,jc->tc", toeplitz, piece, precision=highest)
        carried = jnp.einsum("cn,cnt->tc", coef_out * state, ahead, precision=highest)
        state = whole_decay * state + jnp.einsum("cnj,jc->cn", behind, piece, precision=highest)
        return (state, inner + carried)

    final, outputs = lax.scan(advance, start, pieces)
    return (outputs.reshape(length, channels), final)


def project(left, right):
    return jnp.einsum("mtd,dc->mtc", left, right, preferred_element_type=jnp.float32)


def project_back(left, right):
    return jnp.einsum("mtc,dc->mtd", left, right, preferred_element_type=jnp.float32)


def outer_sum(left, right):
    return jnp.einsum("mtd,mtc->dc", left, right, preferred_element_type=jnp.float32)


def chain(earlier, later):
    return (later[0] * earlier[0], later[0] * earlier[1] + later[1])


def visible(flag, block, context):
    row_ids = jnp.arange(block)[:, None]
    col_ids = jnp.arange(context + 2 * block)[None, :]
    outside = col_ids < context + block
    return jnp.where(outside, flag < 0.5, col_ids - context - block <= row_ids)


def body(
    tokens,
    out_grad,
    norm_gain,
    w_query,
    w_key,
    w_value,
    w_out,
    mid_gain,
    w_up,
    w_down,
    ssm_rate,
    ssm_in,
    ssm_out,
    resets,
    init_state,
    states_grad,
):
    tp_index = lax.axis_index("tp")
    seq_index = lax.axis_index("seq")
    rows_blk, grads_blk = (
        lax.all_gather(tokens, "tp", axis=1, tiled=True),
        lax.all_gather(out_grad, "tp", axis=1, tiled=True),
    )
    micro, block, model_width = rows_blk.shape
    context = CTX
    scale = HD ** (-0.5)
    channels = ssm_rate.shape[0]
    x_block = rows_blk.astype(jnp.float32)
    normed = rms_norm(x_block, norm_gain).astype(jnp.bfloat16)
    query = project(normed, w_query).astype(jnp.bfloat16)
    keys_own = project(normed, w_key).astype(jnp.bfloat16)
    vals_own = project(normed, w_value).astype(jnp.bfloat16)
    heads_here = query.shape[2] // HD
    inputs = lax.dynamic_slice_in_dim(normed, tp_index * channels, channels, 2).astype(jnp.float32)
    flags = resets[:, 0].astype(jnp.float32)
    keep_flag = (1.0 - flags)[:, None, None]
    first = (seq_index == 0).astype(jnp.float32)
    zero_start = jnp.zeros((micro, channels, NS), jnp.float32)

    def whole_block(series, start, rate, coef_in, coef_out):
        return jax.vmap(ssm_block, in_axes=(0, 0, None, None, None))(
            series, start, rate, coef_in, coef_out
        )

    local_out, local_end = whole_block(inputs, zero_start, ssm_rate, ssm_in, ssm_out)
    whole_decay = jnp.exp(-ssm_rate * block)
    reach = keep_flag * whole_decay
    offset = local_end + first * whole_decay * init_state
    identity = (jnp.ones_like(reach), jnp.zeros_like(offset))
    carry_parts = entering((reach, offset), "seq", chain, identity, False)
    start = keep_flag * carry_parts[1] + first * init_state
    ahead_full = jnp.exp(-ssm_rate[:, :, None] * (jnp.arange(block).astype(jnp.float32) + 1.0))
    ssm_y = local_out + jnp.einsum("mcn,cnt->mtc", ssm_out * start, ahead_full, precision=highest)
    block_states = (local_end + whole_decay * start)[:, None]
    ctx_own = ssm_y[:, block - context :, :].astype(jnp.bfloat16)
    ctx_full = lax.all_gather(ctx_own, "tp", axis=2, tiled=True)
    keys_prev, vals_prev, ctx_prev = passed_along((keys_own, vals_own, ctx_full), "seq", 1)
    keys_ctx = project(ctx_prev, w_key).astype(jnp.bfloat16)
    vals_ctx = project(ctx_prev, w_value).astype(jnp.bfloat16)
    keys_all = jnp.concatenate([keys_ctx, keys_prev, keys_own], axis=1).reshape(
        micro, context + 2 * block, heads_here, HD
    )
    vals_all = jnp.concatenate([vals_ctx, vals_prev, vals_own], axis=1).reshape(
        micro, context + 2 * block, heads_here, HD
    )
    query_heads = query.reshape(micro, block, heads_here, HD)

    def scores_of(query_part, keys_part, flag):
        scores = (
            jnp.einsum("thd,khd->htk", query_part, keys_part, preferred_element_type=jnp.float32)
            * scale
        )
        return jnp.where(visible(flag, block, context)[None], scores, neg_big)

    def attend(item):
        query_part, keys_part, vals_part, flag = item
        scores = scores_of(query_part, keys_part, flag)
        top = jnp.max(scores, axis=2, keepdims=True)
        expo = jnp.exp(scores - top)
        total = jnp.sum(expo, axis=2, keepdims=True)
        weights = (expo / total).astype(jnp.bfloat16)
        result = jnp.einsum("htk,khd->thd", weights, vals_part, preferred_element_type=jnp.float32)
        return (result.astype(jnp.bfloat16), (top + jnp.log(total))[..., 0])

    attended, log_total = lax.map(attend, (query_heads, keys_all, vals_all, flags))
    attn_flat = attended.reshape(micro, block, heads_here * HD)
    mixed_attn = lax.psum_scatter(project(attn_flat, w_out), "tp", scatter_dimension=1, tiled=True)
    hidden_one = tokens.astype(jnp.float32) + mixed_attn
    hidden_blk = lax.all_gather(hidden_one, "tp", axis=1, tiled=True)
    normed_mid = rms_norm(hidden_blk, mid_gain).astype(jnp.bfloat16)
    pre_act = project(normed_mid, w_up)
    hidden = jax.nn.gelu(pre_act, approximate=True).astype(jnp.bfloat16)
    mlp_mine = lax.psum_scatter(
        project(hidden, w_down).astype(jnp.bfloat16), "tp", scatter_dimension=1, tiled=True
    ).astype(jnp.float32)
    mixed = (hidden_one + mlp_mine).astype(jnp.bfloat16)
    down_grad = jnp.einsum("mtf,mtd->fd", hidden, grads_blk, preferred_element_type=jnp.float32)
    d_hidden = jnp.einsum("mtd,fd->mtf", grads_blk, w_down, preferred_element_type=jnp.float32)
    _, gelu_pull = jax.vjp(lambda value: jax.nn.gelu(value, approximate=True), pre_act)
    d_pre = gelu_pull(d_hidden)[0].astype(jnp.bfloat16)
    up_grad = outer_sum(normed_mid, d_pre)
    d_mid = project_back(d_pre, w_up)
    _, mid_pull = jax.vjp(rms_norm, hidden_blk, mid_gain)
    d_hidden_part, d_mid_gain = mid_pull(d_mid)
    d_hidden_mlp, mid_gain_grad = (
        lax.psum_scatter(d_hidden_part, "tp", scatter_dimension=1, tiled=True),
        lax.psum_scatter(d_mid_gain, "tp", scatter_dimension=0, tiled=True),
    )
    d_hidden_one = out_grad.astype(jnp.float32) + d_hidden_mlp
    d_mixed_attn = lax.all_gather(d_hidden_one.astype(jnp.bfloat16), "tp", axis=1, tiled=True)
    out_proj_grad = outer_sum(attn_flat, d_mixed_attn)
    d_attended = (
        project_back(d_mixed_attn, w_out).astype(jnp.bfloat16).reshape(micro, block, heads_here, HD)
    )

    def attend_back(item):
        query_part, keys_part, vals_part, flag, log_part, grad_part = item
        probs = jnp.exp(scores_of(query_part, keys_part, flag) - log_part[..., None])
        d_probs = jnp.einsum(
            "thd,khd->htk", grad_part, vals_part, preferred_element_type=jnp.float32
        )
        spread = jnp.sum(probs * d_probs, axis=2, keepdims=True)
        d_scores = (probs * (d_probs - spread)).astype(jnp.bfloat16)
        query_back = (
            jnp.einsum("htk,khd->thd", d_scores, keys_part, preferred_element_type=jnp.float32)
            * scale
        )
        keys_back = (
            jnp.einsum("htk,thd->khd", d_scores, query_part, preferred_element_type=jnp.float32)
            * scale
        )
        vals_back = jnp.einsum(
            "htk,thd->khd",
            probs.astype(jnp.bfloat16),
            grad_part,
            preferred_element_type=jnp.float32,
        )
        return (query_back, keys_back, vals_back)

    query_back, keys_back, vals_back = lax.map(
        attend_back, (query_heads, keys_all, vals_all, flags, log_total, d_attended)
    )
    keys_back = keys_back.reshape(micro, context + 2 * block, heads_here * HD)
    vals_back = vals_back.reshape(micro, context + 2 * block, heads_here * HD)
    d_keys_ctx = keys_back[:, :context].astype(jnp.bfloat16)
    d_vals_ctx = vals_back[:, :context].astype(jnp.bfloat16)
    d_ctx_part = project_back(d_keys_ctx, w_key) + project_back(d_vals_ctx, w_value)
    d_ctx_mine = lax.psum_scatter(
        d_ctx_part.astype(jnp.bfloat16), "tp", scatter_dimension=2, tiled=True
    ).astype(jnp.float32)
    keys_next, vals_next, d_ctx_back = passed_along(
        (
            keys_back[:, context : context + block],
            vals_back[:, context : context + block],
            d_ctx_mine,
        ),
        "seq",
        -1,
    )
    d_keys = (keys_back[:, context + block :] + keys_next).astype(jnp.bfloat16)
    d_vals = (vals_back[:, context + block :] + vals_next).astype(jnp.bfloat16)
    d_query = query_back.reshape(micro, block, heads_here * HD).astype(jnp.bfloat16)
    query_grad = outer_sum(normed, d_query)
    key_grad = outer_sum(normed, d_keys) + outer_sum(ctx_prev, d_keys_ctx)
    value_grad = outer_sum(normed, d_vals) + outer_sum(ctx_prev, d_vals_ctx)
    d_normed = (
        project_back(d_query, w_query) + project_back(d_keys, w_key) + project_back(d_vals, w_value)
    )
    end_grad = states_grad[:, 0]
    d_ssm_y = jnp.concatenate(
        [jnp.zeros((micro, block - context, channels), jnp.float32), d_ctx_back], axis=1
    )
    start_term = jnp.einsum("mtc,cnt->mcn", d_ssm_y, ahead_full, precision=highest) * ssm_out
    back_parts = entering(
        (reach, keep_flag * start_term + reach * end_grad), "seq", chain, identity, True
    )
    _, ssm_pull = jax.vjp(whole_block, inputs, start, ssm_rate, ssm_in, ssm_out)
    d_inputs, _, rate_grad, ssm_in_grad, ssm_out_grad = ssm_pull(
        (d_ssm_y, back_parts[1] + end_grad)
    )
    columns = lax.dynamic_slice_in_dim(d_normed, tp_index * channels, channels, 2) + d_inputs
    d_normed = lax.dynamic_update_slice_in_dim(d_normed, columns, tp_index * channels, 2)
    _, norm_pull = jax.vjp(rms_norm, x_block, norm_gain)
    d_x_part, d_gain_part = norm_pull(d_normed)
    d_x_mine, gain_grad = (
        lax.psum_scatter(d_x_part, "tp", scatter_dimension=1, tiled=True),
        lax.psum_scatter(d_gain_part, "tp", scatter_dimension=0, tiled=True),
    )
    tokens_grad = d_hidden_one + d_x_mine
    summed = lax.psum(
        (
            gain_grad,
            query_grad,
            key_grad,
            value_grad,
            out_proj_grad,
            mid_gain_grad,
            up_grad,
            down_grad,
            rate_grad,
            ssm_in_grad,
            ssm_out_grad,
        ),
        "seq",
    )
    return (
        mixed,
        block_states,
        tokens_grad,
        summed[0],
        summed[1],
        summed[2],
        summed[3],
        summed[4],
        summed[5],
        summed[6],
        summed[7],
        summed[8],
        summed[9],
        summed[10],
    )


def solution(mesh):
    return jax.shard_map(
        body,
        mesh=mesh,
        in_specs=(
            P(None, ("seq", "tp"), None),
            P(None, ("seq", "tp"), None),
            P(),
            P(None, "tp"),
            P(None, "tp"),
            P(None, "tp"),
            P("tp", None),
            P(),
            P(None, "tp"),
            P("tp", None),
            P("tp", None),
            P("tp", None),
            P("tp", None),
            P(None, "seq"),
            P(None, "tp", None),
            P(None, "seq", "tp", None),
        ),
        out_specs=(
            P(None, ("seq", "tp"), None),
            P(None, "seq", "tp", None),
            P(None, ("seq", "tp"), None),
            P("tp"),
            P(None, "tp"),
            P(None, "tp"),
            P(None, "tp"),
            P("tp", None),
            P("tp"),
            P(None, "tp"),
            P("tp", None),
            P("tp", None),
            P("tp", None),
            P("tp", None),
        ),
        check_vma=False,
    )
```

profile of v0, /device:TPU:0, one launch (start us, length us, event | category | flops | bytes accessed | tf_op | source)
XLA Modules:
  0.0 1587.9 jit_solution(12313079761893808815)
XLA Ops:
  20.3 62.1 %gather_fusion = f32[16384,256]{1,0:T(8,128)} fusion(f32[256,128]{0,1:T(8,128)S(1)} %bitcast.429, s32[16384]{0:T(1024)S(1)} %broadcast_clamp_fusion), kind=kCustom, calls=%fused_computation | custom fusion | bytes 33619968 | tf_op jit(solution)/shard_map/vmap(jit(_take))/gather | solution.py:55
  82.4 18.0 %copy.210 = f32[128,128,256]{1,0,2:T(8,128)} copy(f32[128,128,256]{2,1,0:T(8,128)} %bitcast.432) | data formatting | bytes 33554432 | tf_op jit(solution)/shard_map/vmap(jit(_take))/gather | solution.py:55
  101.6 34.6 %all_gather.34 = f32[8,2,256,16]{2,3,1,0:T(8,128)} all-gather(f32[1,2,256,16]{2,3,1,0:T(8,128)S(1)} %broadcast_multiply_fusion.3), channel_id=1, replica_groups=mesh['seq'=8,'tp'=4] {'seq'}, dimensions={0}, use_global_device_ids=true | all-gather | bytes 294912 | tf_op jit(solution)/shard_map/all_gather | solution.py:19
  140.3 12.0 select_bitcast_fusion
  165.2 141.3 %while.119 = (s32[]{:T(128)}, f32[2,256,16]{2,0,1:T(2,128)S(1)}, f32[4,2,128,256]{2,1,3,0:T(2,128)}, f32[256,16]{1,0:T(8,128)}, f32[4,2,128,256]{2,1,3,0:T(2,128...) while((s32[]{:T(128)}, f32[2,256,16]{2,0,1:T(2,128)S(1)}, ...), condition=%wide.region_2.3_spmd.clone, body=%wide.region_1.2_spmd.clone.sunk | while | flops 126459904 | bytes 29199108 | solution.py:67
  165.4 28.7 %fusion.299 = f32[256,2,128]{2,1,0:T(2,128)S(1)} fusion(f32[256,128,128]{2,1,0:T(8,128)} %get-tuple-element.1982, f32[4,2,128,256]{2,1,3,0:T(2,128)S(1)} %get-tuple-element.1980, s32[]{:T(128)S(6)} %copy.308), kind=kOutput, calls=%fused_computation.82.clone.1 | convolution fusion | flops 100663296 | bytes 17301508 | tf_op jit(solution)/shard_map/vmap()/while/body/eval_jaxpr/ctj,jc->tc/dot_general | solution.py:62
  200.7 28.7 %fusion.299 = f32[256,2,128]{2,1,0:T(2,128)S(1)} fusion(f32[256,128,128]{2,1,0:T(8,128)} %get-tuple-element.1982, f32[4,2,128,256]{2,1,3,0:T(2,128)S(1)} %get-tuple-element.1980, s32[]{:T(128)S(6)} %copy.308), kind=kOutput, calls=%fused_computation.82.clone.1 | convolution fusion | flops 100663296 | bytes 17301508 | tf_op jit(solution)/shard_map/vmap()/while/body/eval_jaxpr/ctj,jc->tc/dot_general | solution.py:62
  236.0 28.7 %fusion.299 = f32[256,2,128]{2,1,0:T(2,128)S(1)} fusion(f32[256,128,128]{2,1,0:T(8,128)} %get-tuple-element.1982, f32[4,2,128,256]{2,1,3,0:T(2,128)S(1)} %get-tuple-element.1980, s32[]{:T(128)S(6)} %copy.308), kind=kOutput, calls=%fused_computation.82.clone.1 | convolution fusion | flops 100663296 | bytes 17301508 | tf_op jit(solution)/shard_map/vmap()/while/body/eval_jaxpr/ctj,jc->tc/dot_general | solution.py:62
  271.3 28.7 %fusion.299 = f32[256,2,128]{2,1,0:T(2,128)S(1)} fusion(f32[256,128,128]{2,1,0:T(8,128)} %get-tuple-element.1982, f32[4,2,128,256]{2,1,3,0:T(2,128)S(1)} %get-tuple-element.1980, s32[]{:T(128)S(6)} %copy.308), kind=kOutput, calls=%fused_computation.82.clone.1 | convolution fusion | flops 100663296 | bytes 17301508 | tf_op jit(solution)/shard_map/vmap()/while/body/eval_jaxpr/ctj,jc->tc/dot_general | solution.py:62
  311.0 30.8 %all-gather = f32[16,256,16]{1,2,0:T(8,128)S(1)} all-gather(f32[2,256,16]{1,2,0:T(8,128)S(1)} %multiply_add_fusion.4), channel_id=2, replica_groups=mesh['seq'=8,'tp'=4] {'seq'}, dimensions={0}, use_global_device_ids=true | all-gather | bytes 294912 | tf_op jit(solution)/shard_map/all_gather | solution.py:19
  341.8 10.0 while.120
  356.2 6.8 fusion.142
  364.1 7.2 all_gather.37
  388.7 10.8 collective-permute-done.1
  405.5 4.8 collective-permute-done.2
  411.7 26.2 %while.116 = (s32[]{:T(128)}, bf16[2,512,2,128]{1,3,2,0:T(8,128)(2,1)}, f32[2,2,512]{2,1,0:T(2,128)S(1)}, bf16[2,1152,2,128]{3,2,1,0:T(2,128)(2,1)}, f32[2]{0:T(...) while((s32[]{:T(128)}, ...), condition=%wide.region_8.9_spmd, body=%wide.region_5.8_spmd.sunk | while | flops 614728960 | bytes 25997788 | solution.py:179
  442.0 45.8 %reduce-scatter.6.cloned.1.call-done = f32[2,128,1024]{2,1,0:T(8,128)} async-done(((f32[2,512,1024]{2,1,0:T(8,128)}), f32[2,128,1024]{2,1,0:T(8,128)}) %reduce-scatter.6.cloned.1.call-update) | async-done | bytes 1048592 | tf_op jit(solution)/shard_map/reduce_scatter | solution.py:181
  491.4 33.6 %all-gather.9.cloned.1.call-done = f32[2,512,1024]{2,1,0:T(8,128)} async-done(((f32[2,128,1024]{2,1,0:T(8,128)}), f32[2,512,1024]{2,1,0:T(8,128)}) %all-gather.9.cloned.1.call-update) | async-done | bytes 4194320 | tf_op jit(solution)/shard_map/all_gather | solution.py:183
  528.4 4.4 fusion.135
  532.8 16.2 %all-gather.11.cloned.1.call-done = bf16[2,512,1024]{2,1,0:T(8,128)(2,1)} async-done(((bf16[2,128,1024]{2,1,0:T(8,128)(2,1)}), bf16[2,512,1024]{2,1,0:T(8,128)(2,1)}) %all-gather.11.cloned.1.call-update) | async-done | bytes 2097168 | tf_op jit(solution)/shard_map/all_gather | solution.py:116
  549.1 8.1 fusion.123
  563.4 44.6 %reduce-scatter.10.cloned.1.call-done = f32[2,128,1024]{2,1,0:T(8,128)} async-done(((f32[2,512,1024]{2,1,0:T(8,128)}), f32[2,128,1024]{2,1,0:T(8,128)}) %reduce-scatter.10.cloned.1.call-update) | async-done | bytes 1048592 | tf_op jit(solution)/shard_map/reduce_scatter | solution.py:200
  612.3 28.9 %while.118 = (s32[]{:T(128)}, f32[2,256,16]{2,0,1:T(2,128)S(1)}, f32[4,2,256,16]{3,1,2,0:T(2,128)}, f32[4,2,256,16]{3,1,2,0:T(2,128)}, f32[1,256,16]{2,1,0:T(8,1...) while((s32[]{:T(128)}, f32[2,256,16]{2,0,1:T(2,128)S(1)}, ...), condition=%wide.region_21.22_spmd, body=%wide.region_20.21_spmd.sunk | while | flops 12607490 | bytes 3244141 | solution.py:67
  614.2 5.3 fusion.291
  621.5 5.3 fusion.291
  628.7 5.3 fusion.291
  635.9 5.3 fusion.291
  644.4 25.6 %while.117 = (s32[]{:T(128)}, bf16[2,512,2,128]{1,3,2,0:T(8,128)(2,1)}, f32[2,1152,2,128]{1,3,2,0:T(8,128)}, f32[2,1152,2,128]{1,3,2,0:T(8,128)}, bf16[2,1152,2,...) while((s32[]{:T(128)}, ...), condition=%wide.region_16.17_spmd, body=%wide.region_14.16_spmd.sunk | while | flops 1522173184 | bytes 89624192 | solution.py:234
  689.4 6.9 fusion.139
  706.8 8.2 collective-permute-done.3
  717.5 20.0 %collective-permute-done.4 = f32[2,512,256]{2,1,0:T(8,128)} collective-permute-done((f32[2,512,256]{2,1,0:T(8,128)}, f32[2,512,256]{2,1,0:T(8,128)}, u32[]{:S(2)}, u32[]{:S(2)}) %collective-permute-start.4) | collective-permute-done | bytes 1048608 | tf_op jit(solution)/shard_map/ppermute | solution.py:37
  744.6 11.5 fusion.111
  757.2 32.8 %all-gather.1 = f32[16,256,16]{1,2,0:T(8,128)} all-gather(f32[2,256,16]{1,2,0:T(8,128)S(1)} %fusion.180), channel_id=3, replica_groups=mesh['seq'=8,'tp'=4] {'seq'}, dimensions={0}, use_global_device_ids=true | all-gather | bytes 294912 | tf_op jit(solution)/shard_map/all_gather | solution.py:19
  791.8 5.7 while.121
  800.2 299.6 %while.122 = (s32[]{:T(128)}, f32[256,128,128]{2,1,0:T(8,128)}, f32[256,16]{1,0:T(8,128)}, f32[256,16,128]{2,1,0:T(8,128)}, f32[256,16]{1,0:T(8,128)}, /*index=5...) while((s32[]{:T(128)}, f32[256,128,128]{2,1,0:T(8,128)}, ...), condition=%wide.region_25.26_spmd.clone, body=%wide.region_22.25_spmd.clone.sunk | while | flops 262799360 | bytes 220174512 | solution.py:67
  820.1 17.4 %fusion.315 = f32[4,2,128,256]{2,1,3,0:T(2,128)} fusion(f32[4,2,128,256]{2,1,3,0:T(2,128)} %get-tuple-element.2148, s32[]{:T(128)S(6)} %sub.206, f32[256,2,128]{2,1,0:T(2,128)S(1)} %fusion.314, f32[256,128,128]{2,1,0:T(8,128)} %get-tuple-element.2177, f32[4,2,128,256]{2,1,3,0:T(2,128)} %get-tuple-element.2170), kind=kOutput, calls=%fused_computation.109.clone.1 | convolution fusion | flops 100728832 | bytes 17564672 | tf_op jit(solution)/shard_map/transpose(jvp(vmap()))/while/body/eval_jaxpr/ctj,jc->tc/dot_general | solution.py:62
  841.6 5.6 fusion.313
  847.4 4.9 select_add_fusion.9
  852.4 28.3 %select_add_fusion.7 = f32[256,128,128]{2,1,0:T(8,128)S(1)} fusion(f32[256,128,128]{2,1,0:T(8,128)S(1)} %bitcast.431, pred[]{:T(512)S(6)} %compare.16, f32[4,2,128,256]{2,1,3,0:T(2,128)S(1)} %get-tuple-element.2171, s32[]{:T(128)S(6)} %sub.206, f32[4,2,128,256]{2,1,3,0:T(2,128)S(1)} %copy-done.16), kind=kOutput, calls=%fused_computation.100.clone.1 | convolution fusion | flops 109051904 | bytes 34080256 | tf_op jit(solution)/shard_map/transpose(jvp(vmap()))/while/body/eval_jaxpr/ctj,jc->tc/dot_general | solution.py:62
  880.7 5.8 copy-done.2
  888.5 17.4 %fusion.315 = f32[4,2,128,256]{2,1,3,0:T(2,128)} fusion(f32[4,2,128,256]{2,1,3,0:T(2,128)} %get-tuple-element.2148, s32[]{:T(128)S(6)} %sub.206, f32[256,2,128]{2,1,0:T(2,128)S(1)} %fusion.314, f32[256,128,128]{2,1,0:T(8,128)} %get-tuple-element.2177, f32[4,2,128,256]{2,1,3,0:T(2,128)} %get-tuple-element.2170), kind=kOutput, calls=%fused_computation.109.clone.1 | convolution fusion | flops 100728832 | bytes 17564672 | tf_op jit(solution)/shard_map/transpose(jvp(vmap()))/while/body/eval_jaxpr/ctj,jc->tc/dot_general | solution.py:62
  910.0 5.6 fusion.313
  915.8 4.9 select_add_fusion.9
  920.8 28.3 %select_add_fusion.7 = f32[256,128,128]{2,1,0:T(8,128)S(1)} fusion(f32[256,128,128]{2,1,0:T(8,128)S(1)} %bitcast.431, pred[]{:T(512)S(6)} %compare.16, f32[4,2,128,256]{2,1,3,0:T(2,128)S(1)} %get-tuple-element.2171, s32[]{:T(128)S(6)} %sub.206, f32[4,2,128,256]{2,1,3,0:T(2,128)S(1)} %copy-done.16), kind=kOutput, calls=%fused_computation.100.clone.1 | convolution fusion | flops 109051904 | bytes 34080256 | tf_op jit(solution)/shard_map/transpose(jvp(vmap()))/while/body/eval_jaxpr/ctj,jc->tc/dot_general | solution.py:62
  949.1 5.8 copy-done.2
  956.9 17.4 %fusion.315 = f32[4,2,128,256]{2,1,3,0:T(2,128)} fusion(f32[4,2,128,256]{2,1,3,0:T(2,128)} %get-tuple-element.2148, s32[]{:T(128)S(6)} %sub.206, f32[256,2,128]{2,1,0:T(2,128)S(1)} %fusion.314, f32[256,128,128]{2,1,0:T(8,128)} %get-tuple-element.2177, f32[4,2,128,256]{2,1,3,0:T(2,128)} %get-tuple-element.2170), kind=kOutput, calls=%fused_computation.109.clone.1 | convolution fusion | flops 100728832 | bytes 17564672 | tf_op jit(solution)/shard_map/transpose(jvp(vmap()))/while/body/eval_jaxpr/ctj,jc->tc/dot_general | solution.py:62
  978.4 5.6 fusion.313
  984.1 4.9 select_add_fusion.9
  989.1 28.3 %select_add_fusion.7 = f32[256,128,128]{2,1,0:T(8,128)S(1)} fusion(f32[256,128,128]{2,1,0:T(8,128)S(1)} %bitcast.431, pred[]{:T(512)S(6)} %compare.16, f32[4,2,128,256]{2,1,3,0:T(2,128)S(1)} %get-tuple-element.2171, s32[]{:T(128)S(6)} %sub.206, f32[4,2,128,256]{2,1,3,0:T(2,128)S(1)} %copy-done.16), kind=kOutput, calls=%fused_computation.100.clone.1 | convolution fusion | flops 109051904 | bytes 34080256 | tf_op jit(solution)/shard_map/transpose(jvp(vmap()))/while/body/eval_jaxpr/ctj,jc->tc/dot_general | solution.py:62
  1017.5 5.8 copy-done.2
  1025.2 17.4 %fusion.315 = f32[4,2,128,256]{2,1,3,0:T(2,128)} fusion(f32[4,2,128,256]{2,1,3,0:T(2,128)} %get-tuple-element.2148, s32[]{:T(128)S(6)} %sub.206, f32[256,2,128]{2,1,0:T(2,128)S(1)} %fusion.314, f32[256,128,128]{2,1,0:T(8,128)} %get-tuple-element.2177, f32[4,2,128,256]{2,1,3,0:T(2,128)} %get-tuple-element.2170), kind=kOutput, calls=%fused_computation.109.clone.1 | convolution fusion | flops 100728832 | bytes 17564672 | tf_op jit(solution)/shard_map/transpose(jvp(vmap()))/while/body/eval_jaxpr/ctj,jc->tc/dot_general | solution.py:62
  1046.7 5.6 fusion.313
  1052.5 4.9 select_add_fusion.9
  1057.5 28.3 %select_add_fusion.7 = f32[256,128,128]{2,1,0:T(8,128)S(1)} fusion(f32[256,128,128]{2,1,0:T(8,128)S(1)} %bitcast.431, pred[]{:T(512)S(6)} %compare.16, f32[4,2,128,256]{2,1,3,0:T(2,128)S(1)} %get-tuple-element.2171, s32[]{:T(128)S(6)} %sub.206, f32[4,2,128,256]{2,1,3,0:T(2,128)S(1)} %copy-done.16), kind=kOutput, calls=%fused_computation.100.clone.1 | convolution fusion | flops 109051904 | bytes 34080256 | tf_op jit(solution)/shard_map/transpose(jvp(vmap()))/while/body/eval_jaxpr/ctj,jc->tc/dot_general | solution.py:62
  1085.8 5.8 copy-done.2
  1112.2 7.1 convolution_bitcast_fusion.4
  1119.4 4.8 convolution_bitcast_fusion.3
  1136.4 6.4 all-reduce.5
  1151.4 11.9 select_bitcast_fusion.1
  1163.3 18.1 %copy.276 = f32[128,128,256]{2,1,0:T(8,128)} copy(f32[128,128,256]{1,0,2:T(8,128)} %select_bitcast_fusion.1) | data formatting | bytes 33554432 | tf_op jit(solution)/shard_map/transpose(jvp(vmap(jit(_where))))/select_n | solution.py:55
  1181.5 98.7 %scatter_custom_fusion = f32[256,128]{0,1:T(8,128)S(1)} fusion(s32[16384]{0:T(1024)} %maximum_bitcast_fusion.1, f32[16384,256]{1,0:T(8,128)} %bitcast.435, f32[]{:T(128)} %constant.362.clone.1), kind=kCustom, calls=%fused_computation.256 | custom fusion | flops 4194304 | bytes 131584 | tf_op jit(solution)/shard_map/transpose(jvp(vmap(jit(_take))))/scatter-add | solution.py:55
  1284.5 6.4 multiply_reduce_fusion.6
  1292.1 46.4 %all-reduce.3 = (f32[256]{0:T(256)}, f32[256]{0:T(256)}, f32[256,16]{1,0:T(8,128)S(1)}, f32[256,16]{1,0:T(8,128)S(1)}, f32[256,16]{1,0:T(8,128)S(1)}) all-reduce(f32[256]{0:T(256)S(1)} %dynamic-slice.1, f32[256]{0:T(256)S(1)} %dynamic-slice.3, f32[256,16]{1,0:T(8,128)S(1)} %get-tuple-element.1533, ...), channel_id=1, replica_groups=mesh['seq'=8,'tp'=4] {'seq'}, use_global_device_ids=true, to_apply=%region_30.31 | all-reduce | flops 12800 | bytes 102400 | tf_op jit(solution)/shard_map/psum | solution.py:284
  1343.3 225.1 %all-reduce.8.cloned.1.call-done = (f32[1024,256]{1,0:T(8,128)}, f32[1024,256]{1,0:T(8,128)}, f32[1024,256]{1,0:T(8,128)}, f32[256,1024]{1,0:T(8,128)}, f32[1024,1024]{1,0:T(8,128)}, /*index=5*/f32[1024,1024]{1,0:T(8,128)}) async-done(((f32[1024,256]{1,0:T(8,128)}, f32[1024,256]{1,0:T(8,128)}, f32[1024,256]{1,0:T(8,128)}, f32[256,1024]{1,0:T(8,128)}, f32[1024,1024]{1,0:T(8,128)}, ...) | async-done | bytes 12582928 | tf_op jit(solution)/shard_map/psum | solution.py:284
  (618 shorter events, 312.7 us)
Async XLA Ops:
  7.2 520.5 %copy-start = (bf16[1024,1024]{1,0:T(8,128)(2,1)S(1)}, bf16[1024,1024]{1,0:T(8,128)(2,1)}, u32[]{:S(2)}) copy-start(bf16[1024,1024]{1,0:T(8,128)(2,1)} %param.38) | copy-start | bytes 6291460
  7.2 145.1 %all-gather.7.cloned.1.call-start = ((), (), s32[]{:S(2)}) async-start(), calls=%async_computation.5 | async-start | bytes 2621440 | tf_op jit(solution)/shard_map/all_gather | solution.py:115
  7.9 479.8 %reduce-scatter.6.cloned.1.call-start = ((), (), s32[]{:S(2)}) async-start(), calls=%async_computation.6 | async-start | bytes 5242880 | tf_op jit(solution)/shard_map/reduce_scatter | solution.py:181
  11.4 125.5 %copy-start.56 = (f32[256,16]{1,0:T(8,128)}, f32[256,16]{1,0:T(8,128)S(1)}, u32[]{:S(2)}) copy-start(f32[256,16]{1,0:T(8,128)S(1)} %get-tuple-element.1538) | copy-start | bytes 49156
  11.4 340.4 %copy-start.81 = (f32[256,16]{0,1:T(8,128)}, f32[256,16]{0,1:T(8,128)S(1)}, u32[]{:S(2)}) copy-start(f32[256,16]{0,1:T(8,128)S(1)} %copy.213) | copy-start | bytes 49156
  101.5 38.8 %copy-start.83 = (pred[128,128]{1,0:T(8,128)(4,1)}, pred[128,128]{1,0:T(8,128)(4,1)S(1)}, u32[]{:S(2)}) copy-start(pred[128,128]{1,0:T(8,128)(4,1)S(1)} %get-tuple-element.1544) | copy-start | bytes 49156
  101.5 38.8 %copy-start.96 = (f32[2]{0:T(128)}, f32[2]{0:T(128)S(1)}, u32[]{:S(2)}) copy-start(f32[2]{0:T(128)S(1)} %broadcast_subtract_fusion) | copy-start | bytes 28
  165.4 31.6 %copy-start.32 = (f32[256,16]{1,0:T(8,128)S(1)}, f32[256,16]{1,0:T(8,128)}, u32[]{:S(2)}) copy-start(f32[256,16]{1,0:T(8,128)} %get-tuple-element.1979) | copy-start | bytes 49156 | tf_op jit(solution)/shard_map/vmap()/while
  200.7 31.6 %copy-start.32 = (f32[256,16]{1,0:T(8,128)S(1)}, f32[256,16]{1,0:T(8,128)}, u32[]{:S(2)}) copy-start(f32[256,16]{1,0:T(8,128)} %get-tuple-element.1979) | copy-start | bytes 49156 | tf_op jit(solution)/shard_map/vmap()/while
  236.0 31.6 %copy-start.32 = (f32[256,16]{1,0:T(8,128)S(1)}, f32[256,16]{1,0:T(8,128)}, u32[]{:S(2)}) copy-start(f32[256,16]{1,0:T(8,128)} %get-tuple-element.1979) | copy-start | bytes 49156 | tf_op jit(solution)/shard_map/vmap()/while
  271.3 31.6 %copy-start.32 = (f32[256,16]{1,0:T(8,128)S(1)}, f32[256,16]{1,0:T(8,128)}, u32[]{:S(2)}) copy-start(f32[256,16]{1,0:T(8,128)} %get-tuple-element.1979) | copy-start | bytes 49156 | tf_op jit(solution)/shard_map/vmap()/while
  306.5 56.4 %copy-start.11 = (f32[4,2,128,256]{2,1,3,0:T(2,128)}, f32[4,2,128,256]{2,1,3,0:T(2,128)S(1)}, u32[]{:S(2)}) copy-start(f32[4,2,128,256]{2,1,3,0:T(2,128)S(1)} %get-tuple-element.2222) | copy-start | bytes 3145732
  306.5 56.4 %copy-start.23 = (f32[256,16]{1,0:T(8,128)}, f32[256,16]{1,0:T(8,128)S(1)}, u32[]{:S(2)}) copy-start(f32[256,16]{1,0:T(8,128)S(1)} %get-tuple-element.2236) | copy-start | bytes 49156
  372.4 16.0 %collective-permute-start = (bf16[2,128,1024]{2,1,0:T(8,128)(2,1)}, bf16[2,128,1024]{2,1,0:T(8,128)(2,1)S(1)}, u32[]{:S(2)}, u32[]{:S(2)}) collective-permute-start(bf16[2,128,1024]{2,1,0:T(8,128)(2,1)} %copy.217), channel_id=1, source_target_pairs={{0,4},{4,8},{8,12},{12,16},{16,20},{20,24},{24,28},{1,5},{5,9},{9,... | collective-permute-start | bytes 1572872 | tf_op jit(solution)/shard_map/ppermute | solution.py:37
  378.2 21.3 %collective-permute-start.1 = (bf16[2,512,256]{2,1,0:T(8,128)(2,1)S(1)}, bf16[2,512,256]{2,1,0:T(8,128)(2,1)S(1)}, u32[]{:S(2)}, u32[]{:S(2)}) collective-permute-start(bf16[2,512,256]{2,1,0:T(8,128)(2,1)S(1)} %convolution_convert_fusion.3), channel_id=1, source_target_pairs={{0,4},{4,8},{8,12},{12,16},{16,20},{20,24},{24,28},{1,5},{5,9},{9,... | collective-permute-start | bytes 1572872 | tf_op jit(solution)/shard_map/ppermute | solution.py:37
  383.3 26.9 %collective-permute-start.2 = (bf16[2,512,256]{2,1,0:T(8,128)(2,1)}, bf16[2,512,256]{2,1,0:T(8,128)(2,1)}, u32[]{:S(2)}, u32[]{:S(2)}) collective-permute-start(bf16[2,512,256]{2,1,0:T(8,128)(2,1)} %convolution_convert_fusion.1), channel_id=1, source_target_pairs={{0,4},{4,8},{8,12},{12,16},{16,20},{20,24},{24,28},{1,5},{5,9},{9,... | collective-permute-start | bytes 1572872 | tf_op jit(solution)/shard_map/ppermute | solution.py:37
  441.9 85.8 %copy-start.98 = (f32[1024]{0:T(1024)S(1)}, f32[1024]{0:T(1024)}, u32[]{:S(2)}) copy-start(f32[1024]{0:T(1024)} %param.37) | copy-start | bytes 12292
  441.9 83.0 %all-gather.9.cloned.1.call-start = ((), (), s32[]{:S(2)}) async-start(), calls=%async_computation.7 | async-start | bytes 5242880 | tf_op jit(solution)/shard_map/all_gather | solution.py:183
  490.3 58.8 %all-gather.11.cloned.1.call-start = ((), (), s32[]{:S(2)}) async-start(), calls=%async_computation.9 | async-start | bytes 2621440 | tf_op jit(solution)/shard_map/all_gather | solution.py:116
  490.9 117.2 %reduce-scatter.10.cloned.1.call-start = ((), (), s32[]{:S(2)}) async-start(), calls=%async_computation.10 | async-start | bytes 5242880 | tf_op jit(solution)/shard_map/reduce_scatter | solution.py:200
  528.4 32.1 %copy-start.94 = (f32[2,512]{1,0:T(2,128)}, f32[2,512]{1,0:T(2,128)S(1)}, u32[]{:S(2)}) copy-start(f32[2,512]{1,0:T(2,128)S(1)} %fusion.182) | copy-start | bytes 12292
  563.3 47.3 %copy-start.58 = (f32[8,2,256,16]{2,3,1,0:T(8,128)S(1)}, f32[8,2,256,16]{2,3,1,0:T(8,128)}, u32[]{:S(2)}) copy-start(f32[8,2,256,16]{2,3,1,0:T(8,128)} %get-tuple-element.2260) | copy-start | bytes 786436
  563.3 49.0 %copy-start.4 = (f32[256,16,128]{2,1,0:T(8,128)S(1)}, f32[256,16,128]{2,1,0:T(8,128)}, u32[]{:S(2)}) copy-start(f32[256,16,128]{2,1,0:T(8,128)} %get-tuple-element.2219) | copy-start | bytes 6291460
  563.4 77.8 %all-gather.13.cloned.1.call-start = ((), (), s32[]{:S(2)}) async-start(), calls=%async_computation.11 | async-start | bytes 2621440 | tf_op jit(solution)/shard_map/all_gather | solution.py:204
  610.4 93.8 %reduce-scatter.12.cloned.1.call-start = ((), (), s32[]{:S(2)}) async-start(), calls=%async_computation.12 | async-start | bytes 655360 | tf_op jit(solution)/shard_map/reduce_scatter | solution.py:242
  675.9 458.4 %reduce-scatter.8.cloned.1.call-start = ((), (), s32[]{:S(2)}) async-start(), calls=%async_computation.8 | async-start | bytes 2621440 | tf_op jit(solution)/shard_map/reduce_scatter | solution.py:187
  686.8 28.2 %collective-permute-start.3 = (f32[2,512,256]{2,1,0:T(8,128)}, f32[2,512,256]{2,1,0:T(8,128)}, u32[]{:S(2)}, u32[]{:S(2)}) collective-permute-start(f32[2,512,256]{2,1,0:T(8,128)} %copy.281), channel_id=1, source_target_pairs={{4,0},{8,4},{12,8},{16,12},{20,16},{24,20},{28,24},{5,1},{9,5},{13... | collective-permute-start | bytes 3145736 | tf_op jit(solution)/shard_map/ppermute | solution.py:37
  688.1 49.4 %collective-permute-start.4 = (f32[2,512,256]{2,1,0:T(8,128)}, f32[2,512,256]{2,1,0:T(8,128)}, u32[]{:S(2)}, u32[]{:S(2)}) collective-permute-start(f32[2,512,256]{2,1,0:T(8,128)} %copy.283), channel_id=1, source_target_pairs={{4,0},{8,4},{12,8},{16,12},{20,16},{24,20},{28,24},{5,1},{9,5},{13... | collective-permute-start | bytes 3145736 | tf_op jit(solution)/shard_map/ppermute | solution.py:37
  696.3 644.2 %reduce-scatter.14.cloned.1.call-start = ((), (), s32[]{:S(2)}) async-start(), calls=%async_computation.13 | async-start | bytes 5242880 | tf_op jit(solution)/shard_map/reduce_scatter | solution.py:280
  704.2 33.3 %copy-start.43 = (f32[2,512,256]{2,1,0:T(8,128)S(1)}, f32[2,512,256]{2,1,0:T(8,128)}, u32[]{:S(2)}) copy-start(f32[2,512,256]{2,1,0:T(8,128)} %copy.282) | copy-start | bytes 3145732
  705.2 36.7 %collective-permute-start.5 = (f32[2,128,256]{2,1,0:T(8,128)S(1)}, f32[2,128,256]{2,1,0:T(8,128)S(1)}, u32[]{:S(2)}, u32[]{:S(2)}) collective-permute-start(f32[2,128,256]{2,1,0:T(8,128)S(1)} %convert_element_type.176), channel_id=1, source_target_pairs={{4,0},{8,4},{12,8},{16,12},{20,16},{24,20},{28,24},{5,1},{9,5},{13... | collective-permute-start | bytes 786440 | tf_op jit(solution)/shard_map/ppermute | solution.py:37
  744.6 47.2 %copy-start.65 = (f32[2,256,16]{1,2,0:T(8,128)S(1)}, f32[2,256,16]{1,2,0:T(8,128)}, u32[]{:S(2)}) copy-start(f32[2,256,16]{1,2,0:T(8,128)} %custom-call.2) | copy-start | bytes 98308
  744.6 55.6 %copy-start.12 = (f32[4,2,128,256]{2,1,3,0:T(2,128)S(1)}, f32[4,2,128,256]{2,1,3,0:T(2,128)}, u32[]{:S(2)}) copy-start(f32[4,2,128,256]{2,1,3,0:T(2,128)} %get-tuple-element.2223) | copy-start | bytes 3145732
  744.6 55.6 %copy-start.24 = (f32[1,256,16]{2,1,0:T(8,128)S(1)}, f32[1,256,16]{2,1,0:T(8,128)}, u32[]{:S(2)}) copy-start(f32[1,256,16]{2,1,0:T(8,128)} %get-tuple-element.2237) | copy-start | bytes 49156
  744.6 55.6 %copy-start.105 = (f32[128]{0:T(128)S(1)}, f32[128]{0:T(128)}, u32[]{:S(2)}) copy-start(f32[128]{0:T(128)} %get-tuple-element.2281) | copy-start | bytes 1540
  820.1 32.2 %slice-start = ((s8[16777216]{0:T(1024)(128)(4,1)}), s8[4194304]{0:T(1024)(128)(4,1)S(1)}, s32[]{:S(2)}) async-start(s8[16777216]{0:T(1024)(128)(4,1)} %bitcast.430), calls=%async_computation.15 | async-start | bytes 8388608 | tf_op jit(solution)/shard_map/transpose(jvp(vmap()))/while
  820.1 32.2 %slice-start.1 = ((s8[16777216]{0:T(1024)(128)(4,1)}), s8[4194304]{0:T(1024)(128)(4,1)S(1)}, s32[]{:S(2)}) async-start(s8[16777216]{0:T(1024)(128)(4,1)} %bitcast.430), calls=%async_computation.16 | async-start | bytes 8388608 | tf_op jit(solution)/shard_map/transpose(jvp(vmap()))/while
  820.1 32.2 %slice-start.2 = ((s8[16777216]{0:T(1024)(128)(4,1)}), s8[4194304]{0:T(1024)(128)(4,1)S(1)}, s32[]{:S(2)}) async-start(s8[16777216]{0:T(1024)(128)(4,1)} %bitcast.430), calls=%async_computation.17 | async-start | bytes 8388608 | tf_op jit(solution)/shard_map/transpose(jvp(vmap()))/while
  847.4 33.3 %copy-start.36 = (f32[256,16]{1,0:T(8,128)}, f32[256,16]{1,0:T(8,128)S(1)}, u32[]{:S(2)}) copy-start(f32[256,16]{1,0:T(8,128)S(1)} %get-tuple-element.2166) | copy-start | bytes 49156 | tf_op jit(solution)/shard_map/transpose(jvp(vmap()))/while
  847.4 33.3 %copy-start.39 = (f32[256,16]{1,0:T(8,128)}, f32[256,16]{1,0:T(8,128)S(1)}, u32[]{:S(2)}) copy-start(f32[256,16]{1,0:T(8,128)S(1)} %get-tuple-element.2164) | copy-start | bytes 49156 | tf_op jit(solution)/shard_map/transpose(jvp(vmap()))/while
  888.5 32.2 %slice-start = ((s8[16777216]{0:T(1024)(128)(4,1)}), s8[4194304]{0:T(1024)(128)(4,1)S(1)}, s32[]{:S(2)}) async-start(s8[16777216]{0:T(1024)(128)(4,1)} %bitcast.430), calls=%async_computation.15 | async-start | bytes 8388608 | tf_op jit(solution)/shard_map/transpose(jvp(vmap()))/while
  888.5 32.2 %slice-start.1 = ((s8[16777216]{0:T(1024)(128)(4,1)}), s8[4194304]{0:T(1024)(128)(4,1)S(1)}, s32[]{:S(2)}) async-start(s8[16777216]{0:T(1024)(128)(4,1)} %bitcast.430), calls=%async_computation.16 | async-start | bytes 8388608 | tf_op jit(solution)/shard_map/transpose(jvp(vmap()))/while
  888.5 32.2 %slice-start.2 = ((s8[16777216]{0:T(1024)(128)(4,1)}), s8[4194304]{0:T(1024)(128)(4,1)S(1)}, s32[]{:S(2)}) async-start(s8[16777216]{0:T(1024)(128)(4,1)} %bitcast.430), calls=%async_computation.17 | async-start | bytes 8388608 | tf_op jit(solution)/shard_map/transpose(jvp(vmap()))/while
  915.7 33.3 %copy-start.36 = (f32[256,16]{1,0:T(8,128)}, f32[256,16]{1,0:T(8,128)S(1)}, u32[]{:S(2)}) copy-start(f32[256,16]{1,0:T(8,128)S(1)} %get-tuple-element.2166) | copy-start | bytes 49156 | tf_op jit(solution)/shard_map/transpose(jvp(vmap()))/while
  915.8 33.3 %copy-start.39 = (f32[256,16]{1,0:T(8,128)}, f32[256,16]{1,0:T(8,128)S(1)}, u32[]{:S(2)}) copy-start(f32[256,16]{1,0:T(8,128)S(1)} %get-tuple-element.2164) | copy-start | bytes 49156 | tf_op jit(solution)/shard_map/transpose(jvp(vmap()))/while
  956.8 32.2 %slice-start = ((s8[16777216]{0:T(1024)(128)(4,1)}), s8[4194304]{0:T(1024)(128)(4,1)S(1)}, s32[]{:S(2)}) async-start(s8[16777216]{0:T(1024)(128)(4,1)} %bitcast.430), calls=%async_computation.15 | async-start | bytes 8388608 | tf_op jit(solution)/shard_map/transpose(jvp(vmap()))/while
  956.8 32.2 %slice-start.1 = ((s8[16777216]{0:T(1024)(128)(4,1)}), s8[4194304]{0:T(1024)(128)(4,1)S(1)}, s32[]{:S(2)}) async-start(s8[16777216]{0:T(1024)(128)(4,1)} %bitcast.430), calls=%async_computation.16 | async-start | bytes 8388608 | tf_op jit(solution)/shard_map/transpose(jvp(vmap()))/while
  956.8 32.2 %slice-start.2 = ((s8[16777216]{0:T(1024)(128)(4,1)}), s8[4194304]{0:T(1024)(128)(4,1)S(1)}, s32[]{:S(2)}) async-start(s8[16777216]{0:T(1024)(128)(4,1)} %bitcast.430), calls=%async_computation.17 | async-start | bytes 8388608 | tf_op jit(solution)/shard_map/transpose(jvp(vmap()))/while
  984.1 33.3 %copy-start.36 = (f32[256,16]{1,0:T(8,128)}, f32[256,16]{1,0:T(8,128)S(1)}, u32[]{:S(2)}) copy-start(f32[256,16]{1,0:T(8,128)S(1)} %get-tuple-element.2166) | copy-start | bytes 49156 | tf_op jit(solution)/shard_map/transpose(jvp(vmap()))/while
  984.1 33.3 %copy-start.39 = (f32[256,16]{1,0:T(8,128)}, f32[256,16]{1,0:T(8,128)S(1)}, u32[]{:S(2)}) copy-start(f32[256,16]{1,0:T(8,128)S(1)} %get-tuple-element.2164) | copy-start | bytes 49156 | tf_op jit(solution)/shard_map/transpose(jvp(vmap()))/while
  1025.2 32.2 %slice-start = ((s8[16777216]{0:T(1024)(128)(4,1)}), s8[4194304]{0:T(1024)(128)(4,1)S(1)}, s32[]{:S(2)}) async-start(s8[16777216]{0:T(1024)(128)(4,1)} %bitcast.430), calls=%async_computation.15 | async-start | bytes 8388608 | tf_op jit(solution)/shard_map/transpose(jvp(vmap()))/while
  1025.2 32.2 %slice-start.1 = ((s8[16777216]{0:T(1024)(128)(4,1)}), s8[4194304]{0:T(1024)(128)(4,1)S(1)}, s32[]{:S(2)}) async-start(s8[16777216]{0:T(1024)(128)(4,1)} %bitcast.430), calls=%async_computation.16 | async-start | bytes 8388608 | tf_op jit(solution)/shard_map/transpose(jvp(vmap()))/while
  1025.2 32.2 %slice-start.2 = ((s8[16777216]{0:T(1024)(128)(4,1)}), s8[4194304]{0:T(1024)(128)(4,1)S(1)}, s32[]{:S(2)}) async-start(s8[16777216]{0:T(1024)(128)(4,1)} %bitcast.430), calls=%async_computation.17 | async-start | bytes 8388608 | tf_op jit(solution)/shard_map/transpose(jvp(vmap()))/while
  1052.5 33.3 %copy-start.36 = (f32[256,16]{1,0:T(8,128)}, f32[256,16]{1,0:T(8,128)S(1)}, u32[]{:S(2)}) copy-start(f32[256,16]{1,0:T(8,128)S(1)} %get-tuple-element.2166) | copy-start | bytes 49156 | tf_op jit(solution)/shard_map/transpose(jvp(vmap()))/while
  1052.5 33.3 %copy-start.39 = (f32[256,16]{1,0:T(8,128)}, f32[256,16]{1,0:T(8,128)S(1)}, u32[]{:S(2)}) copy-start(f32[256,16]{1,0:T(8,128)S(1)} %get-tuple-element.2164) | copy-start | bytes 49156 | tf_op jit(solution)/shard_map/transpose(jvp(vmap()))/while
  1110.6 457.8 %all-reduce.8.cloned.1.call-start = ((), (), s32[]{:S(2)}) async-start(), calls=%async_computation.14 | async-start | bytes 25165824 | tf_op jit(solution)/shard_map/psum | solution.py:284
  1163.3 117.7 %copy-start.72 = (f32[256,16]{1,0:T(8,128)S(1)}, f32[256,16]{1,0:T(8,128)}, u32[]{:S(2)}) copy-start(f32[256,16]{1,0:T(8,128)} %get-tuple-element.2262) | copy-start | bytes 49156
  1163.3 117.7 %copy-start.103 = (f32[128]{0:T(128)S(1)}, f32[128]{0:T(128)}, u32[]{:S(2)}) copy-start(f32[128]{0:T(128)} %copy-done.102) | copy-start | bytes 1540
  1163.3 121.2 %copy-start.10 = (f32[256,16,128]{2,1,0:T(8,128)S(1)}, f32[256,16,128]{2,1,0:T(8,128)}, u32[]{:S(2)}) copy-start(f32[256,16,128]{2,1,0:T(8,128)} %get-tuple-element.986) | copy-start | bytes 6291460
  1181.5 109.5 %copy-start.37 = (f32[256,16]{1,0:T(8,128)S(1)}, f32[256,16]{1,0:T(8,128)}, u32[]{:S(2)}) copy-start(f32[256,16]{1,0:T(8,128)} %get-tuple-element.985) | copy-start | bytes 49156
  1181.5 109.5 %copy-start.40 = (f32[256,16]{1,0:T(8,128)S(1)}, f32[256,16]{1,0:T(8,128)}, u32[]{:S(2)}) copy-start(f32[256,16]{1,0:T(8,128)} %get-tuple-element.989) | copy-start | bytes 49156
  1181.5 109.5 %copy-start.60 = (f32[256,16]{1,0:T(8,128)S(1)}, f32[256,16]{1,0:T(8,128)}, u32[]{:S(2)}) copy-start(f32[256,16]{1,0:T(8,128)} %copy-done.59) | copy-start | bytes 49156
  1181.5 109.5 %copy-start.62 = (f32[256,16]{1,0:T(8,128)S(1)}, f32[256,16]{1,0:T(8,128)}, u32[]{:S(2)}) copy-start(f32[256,16]{1,0:T(8,128)} %copy-done.61) | copy-start | bytes 49156
  1284.5 56.0 %copy-start.34 = (bf16[2,128,1024]{2,1,0:T(8,128)(2,1)S(1)}, bf16[2,128,1024]{2,1,0:T(8,128)(2,1)}, u32[]{:S(2)}) copy-start(bf16[2,128,1024]{2,1,0:T(8,128)(2,1)} %param.31) | copy-start | bytes 1572868
  (140 other events, 1202.4 us)
Sparse Core Ops, SparseCore 0:
  9.6 25.2 all-gather.6
  442.0 45.6 reduce-scatter.5
  490.4 34.4 all-gather.8
  526.4 22.5 all-gather.10
  563.5 44.5 reduce-scatter.9
  610.5 22.5 all-gather.12
  676.0 21.6 reduce-scatter.11
  700.4 31.5 reduce-scatter.7
  1110.8 43.0 reduce-scatter.13
  1161.1 407.2 all-reduce.7
where the time goes:
time: 1600 us; the launch traced here: 1590 us
  matrix products  521 us (33%)
  waiting for transfers between devices  413 us (26%)
  local copies, waits for them, and re-layouts  222 us (14%)
  other arithmetic  213 us (13%)
  blocking collectives  158 us (10%)
  loops' own time  31 us (2%)
  between operations  16.1 us (1%)
    dot_general x12, matrix products, advance(): inner = jnp.einsum('ctj,jc->tc', toeplitz, piece, precision=highest)  297 us
    psum x1, waiting for transfers between devices, body(): lax.psum((gain_grad, query_grad, key_grad, value_grad, out_proj_grad, mid...  225 us
    scatter-add x1, other arithmetic, ssm_block(): jnp.take(kernel, lag_index, axis=1)  98.7 us
    all_gather x3, blocking collectives, entering(): pieces = jax.tree.map(lambda part: lax.all_gather(part, axis), value)  98.2 us
    gather x2, local copies, waits for them, and re-layouts, ssm_block(): jnp.take(kernel, lag_index, axis=1)  80.1 us
    dot_general x16, matrix products, advance(): jnp.einsum('cnj,jc->cn', behind, piece, precision=highest)  59 us
    dot_general x12, matrix products, advance(): jnp.einsum('cn,cnt->tc', coef_out * state, ahead, precision=highest)  54 us
    psum x1, blocking collectives, body(): lax.psum((gain_grad, query_grad, key_grad, value_grad, out_proj_grad, mid...  46.4 us
  transfers between devices with their start and end apart: 16, of which 11 were waited for; matrix products, arithmetic and copies ran while one was open for 41% of the time, Pallas kernels for 0%

commit v1 on v0

v1 whole, which is shorter than its diff:
```python
import functools

import jax
import jax.numpy as jnp
from jax import lax
from jax.experimental import pallas as pl
from jax.experimental.pallas import tpu as pltpu
from jax.sharding import PartitionSpec as P

HD = 128
NS = 16
CTX = 128


eps_norm = 1e-06
neg_big = -1e30
MESH = pl.DeviceIdType.MESH
VM = pltpu.VMEM
BF = jnp.bfloat16
F32 = jnp.float32
NT = (((1,), (1,)), ((), ()))
TN = (((0,), (0,)), ((), ()))
NN = (((1,), (0,)), ((), ()))


def dot(left, right, dims=NN):
    return lax.dot_general(left, right, dims, preferred_element_type=F32)


def vmem_specs(count):
    return [pl.BlockSpec(memory_space=VM)] * count


def tp_peers():
    me = lax.axis_index("tp")
    mate = me + 1 - 2 * lax.rem(me, 2)
    return me, mate, lax.rem(me + 2, 4), lax.rem(mate + 2, 4)


def remote(src, dst, send, recv, **where):
    return pltpu.make_async_remote_copy(
        src_ref=src,
        dst_ref=dst,
        send_sem=send,
        recv_sem=recv,
        device_id=where,
        device_id_type=MESH,
    )


def greet(n, with_seq):
    s = lax.axis_index("seq")
    barrier = pltpu.get_barrier_semaphore()
    for peer in tp_peers()[1:]:
        pl.semaphore_signal(barrier, inc=1, device_id={"tp": peer}, device_id_type=MESH)
    if with_seq:
        for k in range(1, n):
            pl.semaphore_signal(
                barrier, inc=1, device_id={"seq": lax.rem(s + k, n)}, device_id_type=MESH
            )


def greeted(n, with_seq):
    pl.semaphore_wait(pltpu.get_barrier_semaphore(), 3 + (n - 1 if with_seq else 0))


class Fetch:
    def __init__(self, names, refs, held, sems):
        self.copies = {
            name: pltpu.make_async_copy(ref, held[name], sems.at[i])
            for i, (name, ref) in enumerate(zip(names, refs))
        }
        self.ready = set()
        for c in self.copies.values():
            c.start()

    def need(self, *wanted):
        for name in wanted:
            if name not in self.ready:
                self.copies[name].wait()
                self.ready.add(name)


class Gather:
    def __init__(self, ref, send, recv):
        rows = ref.shape[0] // 4
        me, mate, across, _ = tp_peers()

        def give(slot, quarter, peer):
            part = ref.at[pl.ds(pl.multiple_of(quarter * rows, rows), rows), :]
            return remote(part, part, send.at[slot], recv.at[slot], tp=peer)

        self.cross = give(1, me, across)
        self.side = give(0, me, mate)
        self.relay = give(2, across, mate)

    def start(self):
        self.cross.start()
        self.side.start()

    def near(self):
        self.side.wait_recv()

    def pass_on(self):
        self.cross.wait_recv()
        self.relay.start()

    def far(self):
        self.relay.wait_recv()

    def finish(self):
        for c in (self.side, self.cross, self.relay):
            c.wait_send()


class Scatter:
    def __init__(self, ref, over, into, send, recv):
        self.ref, self.over, self.into = ref, over, into
        self.rows = ref.shape[0] // 4
        self.me, self.mate, self.across, self.diag = tp_peers()
        self.hop = [
            remote(self.quarter(self.diag), into.at[0], send.at[0], recv.at[0], tp=self.mate),
            remote(self.quarter(self.mate), into.at[1], send.at[1], recv.at[1], tp=self.mate),
            remote(over, into.at[2], send.at[2], recv.at[2], tp=self.across),
        ]

    def span(self, quarter):
        return pl.ds(pl.multiple_of(quarter * self.rows, self.rows), self.rows)

    def quarter(self, quarter):
        return self.ref.at[self.span(quarter), :]

    def start(self):
        self.hop[0].start()
        self.hop[1].start()

    def turn(self):
        self.hop[0].wait_recv()
        mine = self.ref[self.span(self.across), :].astype(F32)
        self.over[...] = (mine + self.into[0].astype(F32)).astype(BF)
        self.hop[2].start()

    def end(self):
        self.hop[1].wait_recv()
        value = self.ref[self.span(self.me), :].astype(F32) + self.into[1].astype(F32)
        self.hop[2].wait_recv()
        value = value + self.into[2].astype(F32)
        for c in self.hop:
            c.wait_send()
        return value


FRONT_IN = ("tok", "gain", "wq", "wk", "wv", "rate", "cin", "cout", "keep", "init")


def front_kernel(n, refs_in, outs, held, scr):
    fetch = Fetch(FRONT_IN, refs_in, held, scr["fetch"])
    nf, q_o, k_o, v_o, ctx_o, start_o, end_o = outs
    s = lax.axis_index("seq")
    me, mate, across, diag = tp_peers()
    tok, rate, keep, init = (held[x] for x in ("tok", "rate", "keep", "init"))
    wq, wk, wv = held["wq"], held["wk"], held["wv"]
    u_s, gath, pay, y_s, ctx_s = (scr[x] for x in ("u", "gath", "pay", "y", "ctx"))
    block = nf.shape[1]
    rows = block // 4
    chan = rate.shape[1]
    gath[...] = jnp.zeros_like(gath)

    @pl.when(s == 0)
    def _():
        k_o[:, 0 : CTX + block, :] = jnp.zeros((2, CTX + block, chan), BF)
        v_o[:, 0 : CTX + block, :] = jnp.zeros((2, CTX + block, chan), BF)
        ctx_o[...] = jnp.zeros_like(ctx_o)

    greet(n, True)

    def span(quarter):
        return pl.ds(pl.multiple_of(quarter * rows, rows), rows)

    def lanes(part):
        return pl.ds(pl.multiple_of(part * chan, chan), chan)

    fetch.need("tok", "gain")
    x = tok[...].astype(F32).reshape(2 * rows, -1)
    normed = x * lax.rsqrt(jnp.mean(x * x, axis=-1, keepdims=True) + eps_norm) * held["gain"][...]
    nf[:, span(me), :] = normed.astype(BF).reshape(2, rows, -1)
    greeted(n, True)

    def give(slot, quarter, peer, part=None):
        cols = slice(None) if part is None else lanes(part)
        ref = nf.at[:, span(quarter), cols]
        return remote(ref, ref, scr["ts"].at[slot], scr["tr"].at[slot], tp=peer)

    cross = [give(1 + i, me, across, part) for i, part in enumerate((across, diag, me, mate))]
    relay = [give(5 + i, across, mate, part) for i, part in enumerate((me, mate, across, diag))]
    side = give(0, me, mate)
    for c in cross:
        c.start()
    side.start()

    def pass_kv(slot, src, half):
        high = 2 * rows
        part = pl.ds(pl.multiple_of(CTX + half * high, rows), high)
        own = pl.ds(pl.multiple_of(CTX + block + half * high, rows), high)
        return remote(
            src.at[:, own, :],
            src.at[:, part, :],
            scr["kvs"].at[slot],
            scr["kvr"].at[slot],
            seq=lax.rem(s + 1, n),
        )

    def qkv(order, half):
        high = 2 * rows
        here = pl.ds(pl.multiple_of(half * high, high), high)
        part = nf[:, here, :].reshape(2 * high, -1)
        own = pl.ds(pl.multiple_of(CTX + block + half * high, rows), high)
        k_o[:, own, :] = dot(part, wk[...]).astype(BF).reshape(2, high, chan)
        v_o[:, own, :] = dot(part, wv[...]).astype(BF).reshape(2, high, chan)

        @pl.when(s < n - 1)
        def _():
            pass_kv(2 * order, k_o, half).start()
            pass_kv(2 * order + 1, v_o, half).start()

        q_o[:, here, :] = dot(part, wq[...]).astype(BF).reshape(2, high, chan)

    near = me // 2
    side.wait_recv()
    fetch.need("wk", "wv", "wq")
    qkv(0, near)
    cross[0].wait_recv()
    cross[1].wait_recv()
    relay[1].start()
    relay[0].start()
    relay[1].wait_recv()
    fetch.need("rate", "cin", "cout", "keep", "init")
    cols = lanes(me)
    for m in range(2):
        u_s[m] = nf[m, :, cols].astype(F32)
    decay = jnp.exp(-rate[...])
    drive = jnp.sqrt(1.0 - decay * decay) * held["cin"][...]

    def run(i, state):
        base = pl.multiple_of(i * 8, 8)
        state = list(state)
        for k in range(8):
            for m in range(2):
                state[m] = decay * state[m] + drive * u_s[m, pl.ds(base + k, 1), :]
        return tuple(state)

    zero = jnp.zeros((NS, chan), F32)
    late = lax.fori_loop(0, (block - CTX) // 8, run, (zero, zero))
    last_state = lax.fori_loop((block - CTX) // 8, block // 8, run, late)
    pay[0:NS] = last_state[0]
    pay[NS : 2 * NS] = last_state[1]
    pay[2 * NS : 2 * NS + 8] = keep[...]

    def spread(k):
        return remote(
            pay, gath.at[k], scr["gs"].at[k], scr["gr"].at[k], seq=lax.rem(s + k, n)
        )

    for k in range(1, n):

        @pl.when(s + k < n)
        def _():
            spread(k).start()

    for i in (2, 3):
        cross[i].wait_recv()
        relay[i].start()
    for i in (0, 2, 3):
        relay[i].wait_recv()
    qkv(1, 1 - near)

    whole = jnp.exp(-rate[...] * block)
    for k in range(1, n):

        @pl.when(s >= k)
        def _():
            spread(k).wait_recv()

    def entry(begin_keep, end, b):
        return tuple(jnp.where(b == 0, init[m], begin_keep[m] * end[m]) for m in range(2))

    def chain(b, end):
        k = jnp.maximum(s - b, 0)
        got = gath[k]
        begin = entry((got[2 * NS : 2 * NS + 1], got[2 * NS + 1 : 2 * NS + 2]), end, b)
        new = tuple(got[m * NS : (m + 1) * NS] + whole * begin[m] for m in range(2))
        return tuple(jnp.where(b < s, new[m], end[m]) for m in range(2))

    end = lax.fori_loop(0, n - 1, chain, (zero, zero))
    begin = entry((keep[0:1, :], keep[1:2, :]), end, s)
    toward = jnp.exp(-rate[...] * (block - CTX))
    state = tuple(late[m] + toward * begin[m] for m in range(2))
    out_c = held["cout"][...]

    def run_out(i, state):
        base = pl.multiple_of(block - CTX + i * 8, 8)
        row = pl.multiple_of(i * 8, 8)
        state = list(state)
        for k in range(8):
            for m in range(2):
                state[m] = decay * state[m] + drive * u_s[m, pl.ds(base + k, 1), :]
                y_s[m, pl.ds(row + k, 1), :] = jnp.sum(out_c * state[m], axis=0, keepdims=True)
        return tuple(state)

    state = lax.fori_loop(0, CTX // 8, run_out, state)
    ctx_s[...] = y_s[...].astype(BF)
    down = remote(
        ctx_s, ctx_o.at[:, :, cols], scr["cs"].at[0], scr["cr"].at[0], seq=lax.rem(s + 1, n)
    )

    @pl.when(s < n - 1)
    def _():
        down.start()

    for m in range(2):
        start_o[m] = begin[m]
        end_o[m] = last_state[m] + whole * begin[m]

    @pl.when(s > 0)
    def _():
        down.wait_recv()
        mine = ctx_o.at[:, :, cols]
        shares = [
            remote(mine, mine, scr["cs"].at[1 + i], scr["cr"].at[1 + i], tp=peer)
            for i, peer in enumerate((across, diag, mate))
        ]
        for c in shares:
            c.start()
        for c in shares:
            c.wait_recv()
        flat = ctx_o[...].reshape(2 * CTX, -1)
        k_o[:, 0:CTX, :] = dot(flat, wk[...]).astype(BF).reshape(2, CTX, chan)
        v_o[:, 0:CTX, :] = dot(flat, wv[...]).astype(BF).reshape(2, CTX, chan)
        for order, half in enumerate((near, 1 - near)):
            pass_kv(2 * order, k_o, half).wait_recv()
            pass_kv(2 * order + 1, v_o, half).wait_recv()
        for c in shares:
            c.wait_send()

    @pl.when(s < n - 1)
    def _():
        down.wait_send()
        for order, half in enumerate((near, 1 - near)):
            pass_kv(2 * order, k_o, half).wait_send()
            pass_kv(2 * order + 1, v_o, half).wait_send()

    for k in range(1, n):

        @pl.when(s + k < n)
        def _():
            spread(k).wait_send()

    for c in [side] + cross + relay:
        c.wait_send()


def launch(body, names, args, outs, out_vmem, scratch, collective_id, limit, name):
    keys = list(scratch)
    count = len(names)

    def kernel(*refs):
        refs_in, refs = refs[:count], refs[count:]
        outs_r, refs = refs[: len(outs)], refs[len(outs) :]
        held, refs = dict(zip(names, refs[:count])), refs[count:]
        body(refs_in, outs_r, held, dict(zip(keys, refs)))

    scratch = dict(scratch)
    return pl.pallas_call(
        kernel,
        out_shape=tuple(outs),
        in_specs=[pl.BlockSpec(memory_space=pl.ANY)] * count,
        out_specs=tuple(
            pl.BlockSpec(memory_space=VM if in_vmem else pl.ANY) for in_vmem in out_vmem
        ),
        scratch_shapes=[VM(a.shape, a.dtype) for a in args] + list(scratch.values()),
        compiler_params=pltpu.CompilerParams(
            collective_id=collective_id, has_side_effects=True, vmem_limit_bytes=limit << 20
        ),
        name=name,
    )(*args)


def front(*args):
    n = lax.axis_size("seq")
    micro, rows, width = args[0].shape
    block = 4 * rows
    chan = args[5].shape[1]
    sds = jax.ShapeDtypeStruct
    dma = pltpu.SemaphoreType.DMA
    outs = (
        sds((micro, block, width), BF),
        sds((micro, block, chan), BF),
        sds((micro, CTX + 2 * block, chan), BF),
        sds((micro, CTX + 2 * block, chan), BF),
        sds((micro, CTX, width), BF),
        sds((micro, NS, chan), F32),
        sds((micro, NS, chan), F32),
    )
    scratch = dict(
        fetch=dma((len(FRONT_IN),)),
        u=VM((micro, block, chan), F32),
        gath=VM((n, 2 * NS + 8, chan), F32),
        pay=VM((2 * NS + 8, chan), F32),
        y=VM((micro, CTX, chan), F32),
        ctx=VM((micro, CTX, chan), BF),
        ts=dma((9,)),
        tr=dma((9,)),
        kvs=dma((4,)),
        kvr=dma((4,)),
        gs=dma((n,)),
        gr=dma((n,)),
        cs=dma((4,)),
        cr=dma((4,)),
    )
    return launch(
        functools.partial(front_kernel, n),
        FRONT_IN,
        args,
        outs,
        [True] * 7,
        scratch,
        0,
        62,
        "front",
    )


def rms_back(x, gain, grad):
    inv = lax.rsqrt(jnp.mean(x * x, axis=-1, keepdims=True) + eps_norm)
    unit = x * inv
    scaled = grad * gain
    gain_grad = jnp.sum(grad * unit, axis=0, keepdims=True)
    return inv * (scaled - unit * jnp.mean(scaled * unit, axis=-1, keepdims=True)), gain_grad


MIDDLE_IN = ("q", "k", "v", "keep", "w_out", "tok", "gain", "w_up", "w_down", "og")


def middle_kernel(refs_in, outs, held, scr):
    fetch = Fetch(MIDDLE_IN, refs_in, held, scr["fetch"])
    mlp_o, h1_o, dh1_o, ffn_o, att, lse, gain_o = outs
    nm, pm, dm, hid, dpre = (scr[x] for x in ("nm", "pm", "dm", "hid", "dpre"))
    q, k, v, keep, w_out, tok, gain, w_up, w_down, og = (held[x] for x in MIDDLE_IN)
    me = tp_peers()[0]
    near = me // 2
    block = q.shape[1]
    rows = block // 4
    width = w_out.shape[1]
    tile = 256
    panels = w_up.shape[1] // tile
    greet(0, False)
    own = pl.ds(pl.multiple_of(me * rows, rows), rows)
    edge0 = k.shape[1] - block
    half = block // 2
    row_ids = lax.broadcasted_iota(jnp.int32, (half, half), 0)
    col_ids = lax.broadcasted_iota(jnp.int32, (half, half), 1)
    scale = HD ** (-0.5)

    def attend(m):
        def one(head, c):
            lanes = pl.ds(pl.multiple_of(head * HD, HD), HD)
            shut = (keep[m : m + 1, 0:half] - 1.0) * -neg_big
            for part in range(2):
                mine = slice(part * half, (part + 1) * half)
                edge = edge0 + part * half
                sc = dot(k[m, 0 : edge + half, lanes], q[m, mine, lanes], NT) * scale
                pieces = [sc[:edge0] + shut]
                if part:
                    pieces.append(sc[edge0:edge])
                pieces.append(jnp.where(row_ids <= col_ids, sc[edge:], neg_big))
                sc = jnp.concatenate(pieces, axis=0)
                top = jnp.max(sc, axis=0, keepdims=True)
                expo = jnp.exp(sc - top)
                total = jnp.sum(expo, axis=0, keepdims=True)
                weights = (expo * (1.0 / total)).astype(BF)
                res = dot(v[m, 0 : edge + half, lanes], weights, TN)
                att[m, mine, lanes] = res.T.astype(BF)
                lse[m, head, :, mine] = top + jnp.log(total)
            return c

        lax.fori_loop(0, q.shape[2] // HD, one, 0)

    def scatter(kind, m, ref):
        at = 2 * kind + m
        return Scatter(
            ref.at[m], scr["over"].at[at], scr["into"].at[at], scr["ss"].at[at], scr["sr"].at[at]
        )

    sums1 = [scatter(0, m, pm) for m in range(2)]
    sums2 = [scatter(1, m, dm) for m in range(2)]
    gathers = [Gather(nm.at[m], scr["gs"].at[m], scr["gr"].at[m]) for m in range(2)]

    def project(m):
        def one(j, c):
            cols = pl.ds(pl.multiple_of(j * tile, tile), tile)
            pm[m, :, cols] = dot(att[m], w_out[:, cols]).astype(BF)
            return c

        lax.fori_loop(0, width // tile, one, 0)

    def residual(m):
        h1 = tok[m].astype(F32) + sums1[m].end()
        h1_o[m] = h1
        inv = lax.rsqrt(jnp.mean(h1 * h1, axis=-1, keepdims=True) + eps_norm)
        nm[m, own, :] = (h1 * inv * gain[...]).astype(BF)
        gathers[m].start()

    def feed(m, part):
        here = pl.ds(pl.multiple_of(part * half, half), half)
        flat = pl.ds(pl.multiple_of(m * block + part * half, half), half)

        def panel(j, c):
            cols = pl.ds(pl.multiple_of(j * tile, tile), tile)
            pre = dot(nm[m, here, :], w_up[:, cols])
            sq = pre * pre
            t = jnp.tanh((0.7978845608028654 * pre) * (1.0 + 0.044715 * sq))
            hid[flat, cols] = (0.5 * pre * (1.0 + t)).astype(BF)
            slope = 0.5 * (1.0 + t) + (0.3989422804014327 * pre) * (1.0 - t * t) * (
                1.0 + 0.134145 * sq
            )
            dpre[flat, cols] = (slope * dot(og[m, here, :], w_down[cols, :], NT)).astype(BF)
            return c

        lax.fori_loop(0, panels, panel, 0)

        def back(j, c):
            cols = pl.ds(pl.multiple_of(j * tile, tile), tile)
            dm[m, here, cols] = dot(dpre[flat, :], w_up[cols, :], NT).astype(BF)
            return c

        lax.fori_loop(0, width // tile, back, 0)

    def lower(m):
        def one(j, c):
            cols = pl.ds(pl.multiple_of(j * tile, tile), tile)
            flat = slice(m * block, (m + 1) * block)
            mlp_o[m, :, cols] = dot(hid[flat, :], w_down[:, cols]).astype(BF)
            return c

        lax.fori_loop(0, width // tile, one, 0)

    fetch.need("q", "k", "v", "keep")
    attend(0)
    fetch.need("w_out")
    project(0)
    greeted(0, False)
    sums1[0].start()
    sums1[0].turn()
    attend(1)
    project(1)
    sums1[1].start()
    sums1[1].turn()
    fetch.need("tok", "gain")
    residual(0)
    fetch.need("w_up", "w_down", "og")
    gathers[0].near()
    feed(0, near)
    residual(1)
    gathers[0].pass_on()
    gathers[1].near()
    feed(1, near)
    gathers[0].far()
    feed(0, 1 - near)
    sums2[0].start()
    gathers[1].pass_on()
    sums2[0].turn()
    gathers[1].far()
    feed(1, 1 - near)
    sums2[1].start()
    sums2[1].turn()

    def down_sum(i, c):
        left = hid[:, pl.ds(pl.multiple_of(i * tile, tile), tile)]
        for j in range(width // tile):
            right = og[:, :, j * tile : (j + 1) * tile].reshape(2 * block, tile)
            at = pl.multiple_of((width // tile + j) * panels * tile + i * tile, tile)
            ffn_o[pl.ds(at, tile), :] = dot(left, right, TN).astype(BF)
        return c

    def up_sum(i, c):
        left = nm[:, :, pl.ds(pl.multiple_of(i * tile, tile), tile)].reshape(2 * block, tile)
        for j in range(panels):
            at = pl.multiple_of(j * width + i * tile, tile)
            ffn_o[pl.ds(at, tile), :] = dot(
                left, dpre[:, j * tile : (j + 1) * tile], TN
            ).astype(BF)
        return c

    lax.fori_loop(0, panels, down_sum, 0)
    lax.fori_loop(0, width // tile, up_sum, 0)
    lower(0)
    lower(1)
    total = jnp.zeros((1, width), F32)
    for m in range(2):
        back, gain_grad = rms_back(h1_o[m], gain[...], sums2[m].end())
        total = total + gain_grad
        dh1_o[m] = og[m, own, :].astype(F32) + back
    gain_o[...] = total
    for m in range(2):
        gathers[m].finish()


def middle(*args):
    q, w_out, og, w_up = args[0], args[4], args[9], args[7]
    micro, block, width = og.shape
    rows = block // 4
    units = w_up.shape[1]
    chan = q.shape[2]
    sds = jax.ShapeDtypeStruct
    dma = pltpu.SemaphoreType.DMA
    outs = (
        sds((micro, block, width), BF),
        sds((micro, rows, width), F32),
        sds((micro, rows, width), F32),
        sds((2 * units * width // 256, 256), BF),
        sds((micro, block, chan), BF),
        sds((micro, chan // HD, 1, block), F32),
        sds((1, width), F32),
    )
    scratch = dict(
        fetch=dma((len(MIDDLE_IN),)),
        nm=VM((micro, block, width), BF),
        pm=VM((micro, block, width), BF),
        dm=VM((micro, block, width), BF),
        hid=VM((micro * block, units), BF),
        dpre=VM((micro * block, units), BF),
        over=VM((4, rows, width), BF),
        into=VM((4, 3, rows, width), BF),
        ss=dma((4, 3)),
        sr=dma((4, 3)),
        gs=dma((2, 3)),
        gr=dma((2, 3)),
    )
    return launch(
        middle_kernel, MIDDLE_IN, args, outs, [True] * 7, scratch, 1, 62, "middle"
    )


class Ring:
    def __init__(self, n, x, recv, send_sem, recv_sem):
        self.n, self.x, self.recv = n, x, recv
        self.send_sem, self.recv_sem = send_sem, recv_sem
        self.subs, self.rows = recv.shape[2], recv.shape[3]
        s = lax.axis_index("seq")
        half = n // 2
        self.r = jnp.where(lax.rem(s, 2) == 0, s // 2, n - 1 - s // 2)

        def dev(q):
            q = lax.rem(q + n, n)
            return jnp.where(q < half, 2 * q, 2 * (n - 1 - q) + 1)

        self.target = (dev(self.r + 1), dev(self.r - 1))
        self.done = 0
        self.total = 2 * n - 2

    def chunk(self, d, b, off):
        sign = (1, -1)[d]
        c = lax.rem(self.r + sign * off + 2 * self.n, self.n)
        at = ((d * self.n + c) * self.subs + b) * self.rows
        return pl.ds(pl.multiple_of(at, self.rows), self.rows)

    def copy(self, d, b, src, dst, k):
        return pltpu.make_async_remote_copy(
            src_ref=src,
            dst_ref=dst,
            send_sem=self.send_sem.at[d, b, k],
            recv_sem=self.recv_sem.at[d, b, k],
            device_id={"seq": self.target[d]},
            device_id_type=MESH,
        )

    def first(self, d, b):
        return self.copy(d, b, self.x.at[self.chunk(d, b, 0)], self.recv.at[d, 0, b], 0)

    def sums(self, d, b, k):
        prior = jnp.maximum(k - 1, 0)
        return self.copy(d, b, self.recv.at[d, prior, b], self.recv.at[d, k, b], k)

    def alls(self, d, b, k):
        ref = self.x.at[self.chunk(d, b, 1 - k)]
        return self.copy(d, b, ref, ref, self.n - 1 + k)

    def each(self):
        return [(d, b) for b in range(self.subs) for d in range(2)]

    def add(self, d, b, k):
        mine = self.x[self.chunk(d, b, -k - 1)]
        return (self.recv[d, k, b].astype(F32) + mine.astype(F32)).astype(BF)

    def start(self):
        for d, b in self.each():
            self.first(d, b).start()

    def tick(self, t):
        n = self.n

        def leave():
            for d, b in self.each():
                self.first(d, b).wait_send()

        def sum_step():
            for d, b in self.each():
                self.sums(d, b, t).wait_recv()
                self.recv[d, t, b] = self.add(d, b, t)
                self.sums(d, b, t + 1).start()

        def turn():
            for d, b in self.each():
                self.sums(d, b, n - 2).wait_recv()
                self.x[self.chunk(d, b, 1)] = self.add(d, b, n - 2)
                self.alls(d, b, 0).start()

        def all_step():
            k = t - (n - 1)
            for d, b in self.each():
                self.alls(d, b, k).wait_recv()
                self.alls(d, b, k + 1).start()

        def close():
            for d, b in self.each():
                self.alls(d, b, n - 2).wait_recv()

        steps = (
            (t == 0, leave),
            (t < n - 2, sum_step),
            (t == n - 2, turn),
            ((t > n - 2) & (t < 2 * n - 3), all_step),
            (t == 2 * n - 3, close),
        )
        for when, step in steps:
            if isinstance(t, int):
                if when:
                    step()
            else:
                pl.when(when)(step)

    def go(self, fourteenths):
        upto = min(-(-fourteenths * self.total // 14), self.total)
        if upto - self.done == 1:
            self.tick(self.done)
        elif upto > self.done:

            def one(t, c):
                self.tick(t)
                return c

            lax.fori_loop(self.done, upto, one, 0)
        self.done = max(upto, self.done)

    def drain(self):
        def more(k, c):
            for d, b in self.each():
                self.sums(d, b, k + 1).wait_send()
                self.alls(d, b, k).wait_send()
            return c

        lax.fori_loop(0, self.n - 2, more, 0)
        for d, b in self.each():
            self.alls(d, b, self.n - 2).wait_send()


LAST_IN = (
    "q",
    "k",
    "v",
    "lse",
    "att",
    "w_out",
    "nf",
    "ctx",
    "wq",
    "wk",
    "wv",
    "rate",
    "cin",
    "cout",
    "start",
    "keep",
    "endg",
    "mlp",
    "h1",
    "dh1",
    "tok",
    "gain",
    "midg",
    "ffn",
)


def last_kernel(n, refs_in, outs, h, scr):
    x1, x2 = scr["x1"], scr["x2"]
    ffn_rows = refs_in[LAST_IN.index("ffn")].shape[0]
    h = dict(h, ffn=x1.at[0:ffn_rows])
    fetch = Fetch(LAST_IN, refs_in, h, scr["fetch"])
    need = fetch.need
    mixed_o, tg_o, sum1_o, sum2_o, gain_o = outs
    s = lax.axis_index("seq")
    me, mate, across, diag = tp_peers()
    peers = (mate, across, diag)
    nf, rate, tok = h["nf"], h["rate"], h["tok"]
    block = nf.shape[1]
    rows = block // 4
    width = nf.shape[2]
    chan = rate.shape[1]
    rk, rv, gath, dcr = scr["rk"], scr["rv"], scr["gath"], scr["dcr"]
    gath[...] = jnp.zeros_like(gath)
    if x1.shape[0] > ffn_rows:
        x1[ffn_rows:] = jnp.zeros((x1.shape[0] - ffn_rows, chan), BF)
    used2 = 4 * width + 3 * NS
    if x2.shape[0] > used2:
        x2[used2:] = jnp.zeros((x2.shape[0] - used2, chan), BF)

    @pl.when(s == n - 1)
    def _():
        rk[...] = jnp.zeros_like(rk)
        rv[...] = jnp.zeros_like(rv)
        dcr[...] = jnp.zeros_like(dcr)

    greet(n, True)
    before = lax.rem(s + n - 1, n)
    own = pl.ds(pl.multiple_of(me * rows, rows), rows)

    def to_before(sem, slot, src, dst):
        return remote(
            src, dst, scr["send_k"].at[sem, slot], scr["recv_k"].at[sem, slot], seq=before
        )

    ring1 = Ring(n, x1, scr["r1"], scr["s1s"], scr["s1r"])
    ring2 = Ring(n, x2, scr["r2"], scr["s2s"], scr["s2r"])
    rr, da, dh1 = scr["rr"], scr["da"], h["dh1"]
    need("dh1")
    for m in range(2):
        rr[m, own, :] = dh1[m].astype(BF)
    greeted(n, True)
    gathers = [Gather(rr.at[m], scr["rs"].at[m], scr["rrv"].at[m]) for m in range(2)]
    for g in gathers:
        g.start()
    need("ffn")
    ring1.start()
    need("w_out", "q", "k", "v", "lse", "keep")

    q, k, v, lse, keep, w_out = (h[name] for name in ("q", "k", "v", "lse", "keep", "w_out"))
    edge0 = k.shape[1] - block
    half = block // 2
    row_ids = lax.broadcasted_iota(jnp.int32, (half, half), 0)
    col_ids = lax.broadcasted_iota(jnp.int32, (half, half), 1)
    scale = HD ** (-0.5)
    dq_s, dko, dvo, dkc, dvc = (scr[x] for x in ("dq", "dko", "dvo", "dkc", "dvc"))
    dkp, dvp, ak, av = (scr[x] for x in ("dkp", "dvp", "ak", "av"))

    def attend_one(m, head):
        i = 2 * m + head
        lanes = pl.ds(pl.multiple_of(head * HD, HD), HD)
        shut = (keep[pl.ds(m, 1), 0:half] - 1.0) * -neg_big
        for part in (1, 0):
            mine = slice(part * half, (part + 1) * half)
            edge = edge0 + part * half
            qq = q[m, mine, lanes]
            kk = k[m, 0 : edge + half, lanes]
            dd = da[m, mine, lanes]
            sc = dot(kk, qq, NT) * scale
            pieces = [sc[:edge0] + shut]
            if part:
                pieces.append(sc[edge0:edge])
            pieces.append(jnp.where(row_ids <= col_ids, sc[edge:], neg_big))
            sc = jnp.concatenate(pieces, axis=0)
            probs = jnp.exp(sc - lse[m, head, :, mine])
            dp = dot(v[m, 0 : edge + half, lanes], dd, NT)
            spread_sum = jnp.sum(probs * dp, axis=0, keepdims=True)
            ds = (probs * (dp - spread_sum)).astype(BF)
            dq_s[m, mine, lanes] = (dot(kk, ds, TN) * scale).T.astype(BF)
            dk = dot(ds, qq) * scale
            dv = dot(probs.astype(BF), dd)
            if part:
                ak[...] = dk
                av[...] = dv
            else:
                ak[0 : edge + half] += dk
                av[0 : edge + half] += dv
        for acc, far, prev, own in ((ak, dkc, dkp, dko), (av, dvc, dvp, dvo)):
            far[m, :, lanes] = acc[0:CTX].astype(BF)
            prev[i] = acc[CTX:edge0].astype(BF)
            own[m, :, lanes] = acc[edge0:]

        @pl.when(s > 0)
        def _():
            to_before(0, i, dkp.at[i], rk.at[i]).start()
            to_before(1, i, dvp.at[i], rv.at[i]).start()

    def stream_back(m, c):
        g = Gather(rr.at[m], scr["rs"].at[m], scr["rrv"].at[m])
        g.near()
        g.pass_on()
        g.far()
        da[m] = dot(rr[m], w_out[...], NT).astype(BF)

        def heads(head, c):
            attend_one(m, head)
            return c

        lax.fori_loop(0, chan // HD, heads, 0)
        ring1.tick(m)
        return c

    lax.fori_loop(0, 2, stream_back, 0)
    ring1.done = 2

    cp, cr, dcs = scr["cp"], scr["cr"], scr["dcs"]
    wq, wk, wv = h["wq"], h["wk"], h["wv"]
    need("wq", "wk", "wv")
    ctx_part = dot(dkc[...].reshape(2 * CTX, chan), wk[...], NT) + dot(
        dvc[...].reshape(2 * CTX, chan), wv[...], NT
    )
    for j in range(4):
        cp[j] = ctx_part[:, j * chan : (j + 1) * chan].astype(BF).reshape(2, CTX, chan)

    def to_peer(i, src, dst, kind):
        return remote(
            src, dst, scr["send_c"].at[kind, i], scr["recv_c"].at[kind, i], tp=peers[i]
        )

    ctx_out = [to_peer(i, cp.at[peers[i]], cr.at[i], 0) for i in range(3)]
    for c in ctx_out:
        c.start()
    need("mlp", "h1")
    mlp, h1 = h["mlp"], h["h1"]

    def scatter(kind, m):
        at = 2 * kind + m
        return Scatter(
            mlp.at[m], scr["over"].at[at], scr["into"].at[at], scr["ss"].at[at], scr["sr"].at[at]
        )

    mlp_sums = [scatter(0, m) for m in range(2)]
    for c in mlp_sums:
        c.start()

    u_s, du_s, hist = scr["u"], scr["du"], scr["hist"]
    cols = pl.ds(pl.multiple_of(me * chan, chan), chan)
    need("nf", "rate", "cin", "cout", "start", "endg")
    for m in range(2):
        u_s[m] = nf[m, :, cols].astype(F32)
    decay = jnp.exp(-rate[...])
    root = jnp.sqrt(1.0 - decay * decay)
    drive = root * h["cin"][...]
    out_c = h["cout"][...]
    start, endg = h["start"], h["endg"]
    for m in range(2):
        hist[0, m] = start[m].astype(BF)

    def run(i, state):
        base = pl.multiple_of(i * 8, 8)
        state = list(state)
        for k in range(8):
            for m in range(2):
                state[m] = decay * state[m] + drive * u_s[m, pl.ds(base + k, 1), :]
                hist[base + k + 1, m] = state[m].astype(BF)
        return tuple(state)

    lax.fori_loop(0, block // 8, run, (start[0], start[1]))
    ctx_back = to_before(0, 4, dcs, dcr)
    total = cp[me].astype(F32)
    for i in range(3):
        ctx_out[i].wait_recv()
        total = total + cr[i].astype(F32)
    dcs[...] = total.astype(BF)

    @pl.when(s > 0)
    def _():
        ctx_back.start()

    for c in mlp_sums:
        c.turn()
    need("att")
    flat_att = h["att"][...].reshape(2 * block, chan)
    tile = 256

    def proj(j, c):
        cols = pl.ds(pl.multiple_of(j * tile, tile), tile)
        right = rr[:, :, cols].reshape(2 * block, tile)
        at = pl.multiple_of(3 * width + j * tile, tile)
        x2[pl.ds(at, tile), :] = dot(flat_att, right, TN).astype(BF)
        return c

    lax.fori_loop(0, width // tile, proj, 0)
    ring1.go(3)

    @pl.when(s < n - 1)
    def _():
        ctx_back.wait_recv()

    dy_s = scr["dy"]
    dy_s[...] = dcr[...].astype(F32)
    zero = jnp.zeros((NS, chan), F32)

    def early(i, grad):
        base = pl.multiple_of(CTX - 8 - i * 8, 8)
        grad = list(grad)
        for k in range(7, -1, -1):
            for m in range(2):
                grad[m] = decay * grad[m] + out_c * dy_s[m, pl.ds(base + k, 1), :]
        return tuple(grad)

    got = lax.fori_loop(0, CTX // 8, early, (zero, zero))
    reach = jnp.exp(-rate[...] * (block - CTX + 1.0))
    whole = jnp.exp(-rate[...] * block)
    pay = scr["pay"]
    for m in range(2):
        pay[m * NS : (m + 1) * NS] = reach * got[m] + whole * endg[m]
    pay[2 * NS : 2 * NS + 8] = keep[...]

    def spread(k):
        return remote(
            pay,
            gath.at[k],
            scr["send_g"].at[0, k],
            scr["recv_g"].at[0, k],
            seq=lax.rem(s + n - k, n),
        )

    for k in range(1, n):

        @pl.when(s >= k)
        def _():
            spread(k).start()

    ring1.go(4)
    for m in range(2):
        mixed_o[m] = (h1[m] + mlp_sums[m].end()).astype(BF)
    for k in range(1, n):

        @pl.when(s + k < n)
        def _():
            spread(k).wait_recv()

    def chain(i, carry):
        k = n - 1 - i
        got = gath[k]
        valid = s + k < n
        return tuple(
            jnp.where(
                valid,
                got[2 * NS + m : 2 * NS + m + 1]
                * (got[m * NS : (m + 1) * NS] + whole * carry[m]),
                carry[m],
            )
            for m in range(2)
        )

    carry = lax.fori_loop(0, n - 1, chain, (zero, zero))
    grads0 = tuple(endg[m] + carry[m] for m in range(2))

    def back_late(i, val):
        hold, d_drive, d_decay, d_out = list(val[0:2]), val[2], val[3], val[4]
        low_row = pl.multiple_of(CTX - 8 - i * 8, 8)
        base = pl.multiple_of(block - 8 - i * 8, 8)
        for k in range(7, -1, -1):
            for m in range(2):
                dy = dy_s[m, pl.ds(low_row + k, 1), :]
                grad = hold[m] + out_c * dy
                du_s[m, pl.ds(base + k, 1), :] = jnp.sum(drive * grad, axis=0, keepdims=True)
                d_drive = d_drive + grad * u_s[m, pl.ds(base + k, 1), :]
                d_decay = d_decay + grad * hist[base + k, m].astype(F32)
                d_out = d_out + dy * hist[base + k + 1, m].astype(F32)
                hold[m] = decay * grad
        return hold[0], hold[1], d_drive, d_decay, d_out

    val = lax.fori_loop(0, CTX // 8, back_late, (grads0[0], grads0[1], zero, zero, zero))

    def back_early(i, val):
        hold, d_drive, d_decay = list(val[0:2]), val[2], val[3]
        base = pl.multiple_of(block - CTX - 8 - i * 8, 8)
        for k in range(7, -1, -1):
            for m in range(2):
                grad = hold[m]
                du_s[m, pl.ds(base + k, 1), :] = jnp.sum(drive * grad, axis=0, keepdims=True)
                d_drive = d_drive + grad * u_s[m, pl.ds(base + k, 1), :]
                d_decay = d_decay + grad * hist[base + k, m].astype(F32)
                hold[m] = decay * grad
        return hold[0], hold[1], d_drive, d_decay

    _, _, d_drive, d_decay = lax.fori_loop(0, (block - CTX) // 8, back_early, val[0:4])
    at = 4 * width
    x2[at : at + NS] = (-decay * (d_decay - d_drive * h["cin"][...] * decay / root)).astype(BF)
    x2[at + NS : at + 2 * NS] = (d_drive * root).astype(BF)
    x2[at + 2 * NS : at + 3 * NS] = val[4].astype(BF)
    ring1.go(5)

    @pl.when(s < n - 1)
    def _():
        for i in range(4):
            to_before(0, i, dkp.at[i], rk.at[i]).wait_recv()
            to_before(1, i, dvp.at[i], rv.at[i]).wait_recv()

    dk_b, dv_b = scr["dkb"], scr["dvb"]
    for m in range(2):
        for head in range(chan // HD):
            lanes = slice(head * HD, (head + 1) * HD)
            i = m * (chan // HD) + head
            dk_b[m, :, lanes] = (dko[m, :, lanes] + rk[i].astype(F32)).astype(BF)
            dv_b[m, :, lanes] = (dvo[m, :, lanes] + rv[i].astype(F32)).astype(BF)

    part_s = scr["part"]

    def normed_part(i, c):
        m, part = i // 2, lax.rem(i, 2)
        here = pl.ds(pl.multiple_of(part * half, half), half)
        part_s[...] = (
            dot(dq_s[m, here, :], wq[...], NT)
            + dot(dk_b[m, here, :], wk[...], NT)
            + dot(dv_b[m, here, :], wv[...], NT)
        )
        part_s[:, cols] += du_s[m, here, :]
        mlp[m, here, :] = part_s[...].astype(BF)
        return c

    finals = [scatter(1, m) for m in range(2)]
    for m in range(2):
        lax.fori_loop(2 * m, 2 * m + 2, normed_part, 0)
        finals[m].start()
    finals[0].turn()
    need("ctx")
    ctx = h["ctx"]

    def grads(i, c):
        at = pl.multiple_of(i * tile, tile)
        here = pl.ds(at, tile)
        left = nf[:, :, here].reshape(2 * block, tile)
        left_ctx = ctx[:, :, here].reshape(2 * CTX, tile)
        x2[pl.ds(at, tile), :] = dot(left, dq_s[...].reshape(2 * block, chan), TN).astype(BF)
        for j, (own, far) in enumerate(((dk_b, dkc), (dv_b, dvc))):
            value = dot(left, own[...].reshape(2 * block, chan), TN) + dot(
                left_ctx, far[...].reshape(2 * CTX, chan), TN
            )
            x2[pl.ds((j + 1) * width + at, tile), :] = value.astype(BF)
        return c

    finals[1].turn()
    lax.fori_loop(0, width // tile, grads, 0)
    ring2.start()
    ring1.go(6)
    need("tok", "gain", "midg")
    gain_grad = jnp.zeros((1, width), F32)
    for m in range(2):
        back, one = rms_back(tok[m].astype(F32), h["gain"][...], finals[m].end())
        tg_o[m] = dh1[m] + back
        gain_grad = gain_grad + one
    gp, gr, gs, gg = scr["gp"], scr["gr"], scr["gs"], scr["gg"]
    for j in range(4):
        gp[j, 0:1] = gain_grad[:, j * chan : (j + 1) * chan]
        gp[j, 1:2] = h["midg"][:, j * chan : (j + 1) * chan]
        gp[j, 2:8] = jnp.zeros((6, chan), F32)
    gains = [to_peer(i, gp.at[peers[i]], gr.at[i], 1) for i in range(3)]
    for c in gains:
        c.start()
    ring1.go(7)
    ring2.go(1)
    total = gp[me]
    for i in range(3):
        gains[i].wait_recv()
        total = total + gr[i]
    gs[...] = total

    def gain_out(k):
        return remote(
            gs,
            gg.at[k],
            scr["send_g"].at[1, k],
            scr["recv_g"].at[1, k],
            seq=lax.rem(s + k, n),
        )

    for k in range(1, n):
        gain_out(k).start()
    for t in range(8, 15):
        ring1.go(t)
        ring2.go(t - 6)
    store1 = pltpu.make_async_copy(x1, sum1_o, scr["store"].at[0])
    store1.start()
    for k in range(1, n):
        gain_out(k).wait_recv()
        total = total + gg[k]
    gain_o[...] = total
    for t in range(9, 15):
        ring2.go(t)
    store2 = pltpu.make_async_copy(x2, sum2_o, scr["store"].at[1])
    store2.start()
    for k in range(1, n):
        gain_out(k).wait_send()
    for c in gains + ctx_out:
        c.wait_send()
    for g in gathers:
        g.finish()

    @pl.when(s > 0)
    def _():
        ctx_back.wait_send()
        for i in range(4):
            to_before(0, i, dkp.at[i], rk.at[i]).wait_send()
            to_before(1, i, dvp.at[i], rv.at[i]).wait_send()

    for k in range(1, n):

        @pl.when(s >= k)
        def _():
            spread(k).wait_send()

    ring1.drain()
    ring2.drain()
    store1.wait()
    store2.wait()


def ring_rows(n, used, subs):
    return -(-used // (2 * n * subs * 16)) * 16


def last(*args):
    n = lax.axis_size("seq")
    by = dict(zip(LAST_IN, args))
    micro, block, width = by["nf"].shape
    rows = block // 4
    chan = by["rate"].shape[1]
    keys = by["k"].shape[1]
    sds = jax.ShapeDtypeStruct
    dma = pltpu.SemaphoreType.DMA
    step1 = ring_rows(n, by["ffn"].shape[0], 2)
    step2 = ring_rows(n, 4 * width + 3 * NS, 1)
    x1 = VM((4 * n * step1, chan), BF)
    x2 = VM((2 * n * step2, chan), BF)
    scratch = dict(
        x1=x1,
        r1=VM((2, n - 1, 2, step1, chan), BF),
        x2=x2,
        r2=VM((2, n - 1, 1, step2, chan), BF),
        s1s=dma((2, 2, 2 * n - 2)),
        s1r=dma((2, 2, 2 * n - 2)),
        s2s=dma((2, 1, 2 * n - 2)),
        s2r=dma((2, 1, 2 * n - 2)),
        fetch=dma((len(LAST_IN),)),
        rr=VM((micro, block, width), BF),
        da=VM((micro, block, chan), BF),
        rs=dma((2, 3)),
        rrv=dma((2, 3)),
        rk=VM((4, block, HD), BF),
        rv=VM((4, block, HD), BF),
        dkp=VM((4, block, HD), BF),
        dvp=VM((4, block, HD), BF),
        ak=VM((keys, HD), F32),
        av=VM((keys, HD), F32),
        dq=VM((micro, block, chan), BF),
        dko=VM((micro, block, chan), F32),
        dvo=VM((micro, block, chan), F32),
        dkb=VM((micro, block, chan), BF),
        dvb=VM((micro, block, chan), BF),
        dkc=VM((micro, CTX, chan), BF),
        dvc=VM((micro, CTX, chan), BF),
        cp=VM((4, micro, CTX, chan), BF),
        cr=VM((3, micro, CTX, chan), BF),
        dcs=VM((micro, CTX, chan), BF),
        dcr=VM((micro, CTX, chan), BF),
        dy=VM((micro, CTX, chan), F32),
        u=VM((micro, block, chan), F32),
        du=VM((micro, block, chan), F32),
        hist=VM((block + 1, micro, NS, chan), BF),
        pay=VM((2 * NS + 8, chan), F32),
        gath=VM((n, 2 * NS + 8, chan), F32),
        part=VM((block // 2, width), F32),
        over=VM((4, rows, width), BF),
        into=VM((4, 3, rows, width), BF),
        ss=dma((4, 3)),
        sr=dma((4, 3)),
        gp=VM((4, 8, chan), F32),
        gr=VM((3, 8, chan), F32),
        gs=VM((8, chan), F32),
        gg=VM((n, 8, chan), F32),
        send_k=dma((2, 5)),
        recv_k=dma((2, 5)),
        send_c=dma((2, 3)),
        recv_c=dma((2, 3)),
        send_g=dma((2, n)),
        recv_g=dma((2, n)),
        store=dma((2,)),
    )
    outs = (
        sds((micro, rows, width), BF),
        sds((micro, rows, width), F32),
        sds(x1.shape, BF),
        sds(x2.shape, BF),
        sds((8, chan), F32),
    )
    return launch(
        functools.partial(last_kernel, n),
        LAST_IN,
        args,
        outs,
        [True, True, False, False, True],
        scratch,
        2,
        62,
        "last",
    )


def finish_kernel(up_i, down_i, proj_i, q_i, k_i, v_i, up, down, proj, q, k, v):
    pairs = ((up_i, up), (down_i, down), (proj_i, proj), (q_i, q), (k_i, k), (v_i, v))
    for src, dst in pairs:
        dst[...] = src[...].astype(F32)


def finish(sum1, sum2, width, units, chan):
    across = width // chan
    sds = jax.ShapeDtypeStruct
    down_at = units * width // chan
    tall = lambda high, at: pl.BlockSpec((high, chan), lambda j: (at // high + j, 0))
    wide = lambda high: pl.BlockSpec((high, chan), lambda j: (0, j))
    col = pl.BlockSpec((chan, chan), lambda j: (j, 0))
    return pl.pallas_call(
        finish_kernel,
        grid=(across,),
        out_shape=(
            sds((width, units), F32),
            sds((units, width), F32),
            sds((chan, width), F32),
            sds((width, chan), F32),
            sds((width, chan), F32),
            sds((width, chan), F32),
        ),
        in_specs=[
            tall(width, 0),
            tall(units, down_at),
            tall(chan, 3 * width),
            tall(chan, 0),
            tall(chan, width),
            tall(chan, 2 * width),
        ],
        out_specs=(wide(width), wide(units), wide(chan), col, col, col),
        compiler_params=pltpu.CompilerParams(vmem_limit_bytes=62 << 20),
        name="finish",
    )(sum1, sum1, sum2, sum2, sum2, sum2)


def body(
    tokens,
    out_grad,
    norm_gain,
    w_query,
    w_key,
    w_value,
    w_out,
    mid_gain,
    w_up,
    w_down,
    ssm_rate,
    ssm_in,
    ssm_out,
    resets,
    init_state,
    states_grad,
):
    micro, rows, width = tokens.shape
    chan = ssm_rate.shape[0]
    units = w_up.shape[1]
    og = lax.all_gather(out_grad, "tp", axis=1, tiled=True)
    rate, cin, cout = ssm_rate.T, ssm_in.T, ssm_out.T
    flags = resets[:, 0]
    keep = jnp.zeros((8, chan), F32).at[0:micro].set((1.0 - flags.astype(F32))[:, None])
    init = jnp.swapaxes(init_state, 1, 2)
    endg = jnp.swapaxes(states_grad[:, 0], 1, 2)
    gain_row, mid_row = norm_gain[None], mid_gain[None]
    nf, q, k, v, ctx, start, end = front(
        tokens, gain_row, w_query, w_key, w_value, rate, cin, cout, keep, init
    )
    mlp, h1, dh1, ffn, att, lse, mid_part = middle(
        q, k, v, keep, w_out, tokens, mid_row, w_up, w_down, og
    )
    mixed, tokens_grad, sum1, sum2, gains = last(
        *(q, k, v, lse, att, w_out, nf, ctx, w_query, w_key, w_value, rate, cin, cout),
        *(start, keep, endg, mlp, h1, dh1, tokens, gain_row, mid_part, ffn),
    )
    up_g, down_g, proj_g, query_g, key_g, value_g = finish(sum1, sum2, width, units, chan)
    small = sum2[4 * width : 4 * width + 3 * NS].astype(F32)
    rate_g, in_g, out_g = (small[i * NS : (i + 1) * NS].T for i in range(3))
    return (
        mixed,
        jnp.swapaxes(end, 1, 2)[:, None],
        tokens_grad,
        gains[0],
        query_g,
        key_g,
        value_g,
        proj_g,
        gains[1],
        up_g,
        down_g,
        rate_g,
        in_g,
        out_g,
    )


def solution(mesh):
    return jax.shard_map(
        body,
        mesh=mesh,
        in_specs=(
            P(None, ("seq", "tp"), None),
            P(None, ("seq", "tp"), None),
            P(),
            P(None, "tp"),
            P(None, "tp"),
            P(None, "tp"),
            P("tp", None),
            P(),
            P(None, "tp"),
            P("tp", None),
            P("tp", None),
            P("tp", None),
            P("tp", None),
            P(None, "seq"),
            P(None, "tp", None),
            P(None, "seq", "tp", None),
        ),
        out_specs=(
            P(None, ("seq", "tp"), None),
            P(None, "seq", "tp", None),
            P(None, ("seq", "tp"), None),
            P("tp"),
            P(None, "tp"),
            P(None, "tp"),
            P(None, "tp"),
            P("tp", None),
            P("tp"),
            P(None, "tp"),
            P("tp", None),
            P("tp", None),
            P("tp", None),
            P("tp", None),
        ),
        check_vma=False,
    )
```

time: 1600 us -> 326 us (0.20)
  matrix products: 521 us -> 0 us
  waiting for transfers between devices: 413 us -> 0.7 us
  Pallas kernels: 0 us -> 304 us
  local copies, waits for them, and re-layouts: 222 us -> 5.03 us
  other arithmetic: 213 us -> 1.4 us
  blocking collectives: 158 us -> 0 us
  loops' own time: 31 us -> 0 us
    dot_general x82 -> x0, matrix products: 521 us -> none  [the longest x12 297 us: advance(): inner = jnp.einsum('ctj,jc->tc', toeplitz, piece, precision=highest)]
    pallas_call x0 -> x4, Pallas kernels: none -> 304 us  [the longest x3 296 us: launch(): pl.pallas_call(kernel, out_shape=tuple(outs), in_specs=[pl.BlockSpec(memo...]
    psum x1 -> x0, waiting for transfers between devices: 225 us -> none  [body(): lax.psum((gain_grad, query_grad, key_grad, value_grad, out_proj_grad, mid...]
    all_gather x4 -> x0, blocking collectives: 105 us -> none  [the longest x3 98.2 us: entering(): pieces = jax.tree.map(lambda part: lax.all_gather(part, axis), value)]
    scatter-add x1 -> x0, other arithmetic: 98.7 us -> none  [ssm_block(): jnp.take(kernel, lag_index, axis=1)]
    reduce_scatter x5 -> x0, waiting for transfers between devices: 90.4 us -> none  [the longest x1 45.8 us: body(): lax.psum_scatter(project(attn_flat, w_out), 'tp', scatter_dimension=1, ti...]
    gather x2 -> x0, local copies, waits for them, and re-layouts: 80.1 us -> none  [ssm_block(): jnp.take(kernel, lag_index, axis=1)]
    all_gather x4 -> x1, waiting for transfers between devices: 49.8 us -> 0.02 us  [body(): og = lax.all_gather(out_grad, 'tp', axis=1, tiled=True)]
  transfers between devices with their start and end apart: 16 -> 1, of which waited for: 11 -> 0; matrix products, arithmetic and copies ran while one was open for 41% -> 0% of each run, Pallas kernels for 0% -> 14%
where the time goes in v1:
time: 326 us; the launch traced here: 325 us
  Pallas kernels  304 us (93%)
  between operations  14.1 us (4%)
  local copies, waits for them, and re-layouts  5.03 us (2%)
    pallas_call x3, Pallas kernels, launch(): pl.pallas_call(kernel, out_shape=tuple(outs), in_specs=[pl.BlockSpec(memo...  296 us
    pallas_call x1, Pallas kernels, finish(): pl.pallas_call(finish_kernel, grid=(across,), out_shape=(sds((width, unit...  7.62 us
  transfers between devices with their start and end apart: 1, of which 0 were waited for; matrix products, arithmetic and copies ran while one was open for 0% of the time, Pallas kernels for 14%

profile of v1, /device:TPU:0, one launch (start us, length us, event | category | flops | bytes accessed | tf_op | source)
XLA Modules:
  0.0 325.3 jit_solution(10496219478824124260)
XLA Ops:
  7.2 0.0 all-gather.2.cloned.1.call-start
  7.2 0.7 all-gather.2.cloned.1.call-update
  7.9 0.7 subtract_bitcast_fusion
  8.6 0.7 scatter.8.refs_8_.refs_3_.refs_15_
  9.2 44.7 %front.1 = (bf16[2,512,1024]{2,1,0:T(8,128)(2,1)}, bf16[2,512,256]{2,1,0:T(8,128)(2,1)}, bf16[2,1152,256]{2,1,0:T(8,128)(2,1)}, bf16[2,1152,256]{2,1,0:T(8,128)(...) custom-call(bf16[2,128,1024]{2,1,0:T(8,128)(2,1)} %refs_20_.1, ...), custom_call_target="tpu_custom_call" | custom-call | tf_op jit(solution)/shard_map/front/pallas_call | solution.py:373
  53.9 0.0 all-gather.2.cloned.1.call-done.refs_9_
  53.9 55.9 %middle.1 = (bf16[2,512,1024]{2,1,0:T(8,128)(2,1)}, f32[2,128,1024]{2,1,0:T(8,128)}, f32[2,128,1024]{2,1,0:T(8,128)}, bf16[8192,256]{1,0:T(8,128)(2,1)}, bf16[2,...) custom-call(bf16[2,512,256]{2,1,0:T(8,128)(2,1)} %get-tuple-element.51.refs_0_, ...), custom_call_target="tpu_custom_call" | custom-call | tf_op jit(solution)/shard_map/middle/pallas_call | solution.py:373
  109.8 195.9 %last.1 = (bf16[2,128,1024]{2,1,0:T(8,128)(2,1)}, f32[2,128,1024]{2,1,0:T(8,128)}, bf16[8192,256]{1,0:T(8,128)(2,1)}, bf16[4352,256]{1,0:T(8,128)(2,1)}, f32[8,256]{1,0:T(8,128)}) custom-call(bf16[2,512,256]{2,1,0:T(8,128)(2,1)} %get-tuple-element.51.refs_0_, bf16[2,1152,256]{2,1,0:T(8,128)(2,1)} %get-tuple-element.52.refs_1_, ...), custom_call_target="tpu_custom_call" | custom-call | tf_op jit(solution)/shard_map/last/pallas_call | solution.py:373
  305.7 1.3 fusion
  307.0 0.7 slice_convert_fusion
  307.8 0.6 slice_bitcast_fusion
  308.4 0.0 copy-start.1
  308.4 0.0 copy-start.2
  308.4 0.0 copy-start
  308.4 7.6 %finish.1 = (f32[1024,1024]{1,0:T(8,128)}, f32[1024,1024]{1,0:T(8,128)}, f32[256,1024]{1,0:T(8,128)}, f32[1024,256]{1,0:T(8,128)}, f32[1024,256]{1,0:T(8,128)}, /*index=5*/f32[1024,256]{1,0:T(8,128)}) custom-call(bf16[8192,256]{1,0:T(8,128)(2,1)} %get-tuple-element.68.up_i.down_i, bf16[8192,256]{1,0:T(8,128)(2,1)} %get-tuple-element.68.up_i.down_i, ...), custom_call_target="tpu_custom_call" | custom-call | tf_op jit(solution)/shard_map/finish/pallas_call | solution.py:1323
  316.0 0.0 copy-done.1
  316.0 0.8 copy.34
  316.8 0.0 copy-done.2
  316.8 0.6 copy.35
  317.4 0.0 copy-done
  317.4 1.0 copy.36
  (1 shorter events, 0.0 us)
Async XLA Ops:
  7.2 46.8 %all-gather.2.cloned.1.call-start = ((), (), s32[]{:S(2)}) async-start(), calls=%async_computation | async-start | bytes 2621440 | tf_op jit(solution)/shard_map/all_gather | solution.py:1369
  308.4 7.6 %copy-start.1 = (bf16[2,128,1024]{2,1,0:T(8,128)(2,1)S(1)}, bf16[2,128,1024]{2,1,0:T(8,128)(2,1)}, u32[]{:S(2)}) copy-start(bf16[2,128,1024]{2,1,0:T(8,128)(2,1)} %get-tuple-element.109) | copy-start | bytes 1572868
  308.4 8.4 %copy-start.2 = (f32[2,16,256]{2,1,0:T(8,128)S(1)}, f32[2,16,256]{2,1,0:T(8,128)}, u32[]{:S(2)}) copy-start(f32[2,16,256]{2,1,0:T(8,128)} %get-tuple-element.65) | copy-start | bytes 98308
  308.4 9.0 %copy-start = (f32[2,128,1024]{2,1,0:T(8,128)S(1)}, f32[2,128,1024]{2,1,0:T(8,128)}, u32[]{:S(2)}) copy-start(f32[2,128,1024]{2,1,0:T(8,128)} %get-tuple-element.111) | copy-start | bytes 3145732
Sparse Core Ops, SparseCore 0:
  9.6 31.5 all-gather.1

commit v2 on v1

--- a/solution.py
+++ b/solution.py
@@ -150,14 +150,34 @@
         return value
 
 
-FRONT_IN = ("tok", "gain", "wq", "wk", "wv", "rate", "cin", "cout", "keep", "init")
+FRONT_IN = ("tok", "gain", "wq", "wk", "wv", "rate", "cin", "cout", "keep", "init", "ogm")
+
+
+class Save:
+    def __init__(self, sems):
+        self.sems, self.copies = sems, []
+
+    def __call__(self, src, dst):
+        self.copies.append(pltpu.make_async_copy(src, dst, self.sems.at[len(self.copies)]))
+        self.copies[-1].start()
+
+    def finish(self):
+        for c in self.copies:
+            c.wait()
 
 
 def front_kernel(n, refs_in, outs, held, scr):
-    fetch = Fetch(FRONT_IN, refs_in, held, scr["fetch"])
-    nf, q_o, k_o, v_o, ctx_o, start_o, end_o = outs
     s = lax.axis_index("seq")
     me, mate, across, diag = tp_peers()
+    og = scr["og"]
+    own_rows = og.shape[1] // 4
+    own = pl.ds(pl.multiple_of(me * own_rows, own_rows), own_rows)
+    held = dict(held, ogm=og.at[:, own, :])
+    fetch = Fetch(FRONT_IN, refs_in, held, scr["fetch"])
+    nf_d, og_d, q_d, k_d, v_d, ctx_d, start_o, end_o = outs
+    nf, q_o, k_o, v_o, ctx_o = (scr[x] for x in ("nf", "q", "k", "v", "ctxa"))
+    save = Save(scr["save"])
+    grad_gathers = [Gather(og.at[m], scr["os"].at[m], scr["or"].at[m]) for m in range(2)]
     tok, rate, keep, init = (held[x] for x in ("tok", "rate", "keep", "init"))
     wq, wk, wv = held["wq"], held["wk"], held["wv"]
     u_s, gath, pay, y_s, ctx_s = (scr[x] for x in ("u", "gath", "pay", "y", "ctx"))
@@ -272,7 +292,12 @@
         relay[i].start()
     for i in (0, 2, 3):
         relay[i].wait_recv()
+    fetch.need("ogm")
+    for g in grad_gathers:
+        g.start()
     qkv(1, 1 - near)
+    save(nf, nf_d)
+    save(q_o, q_d)
 
     whole = jnp.exp(-rate[...] * block)
     for k in range(1, n):
@@ -320,6 +345,9 @@
     for m in range(2):
         start_o[m] = begin[m]
         end_o[m] = last_state[m] + whole * begin[m]
+    for g in grad_gathers:
+        g.near()
+        g.pass_on()
 
     @pl.when(s > 0)
     def _():
@@ -342,6 +370,13 @@
         for c in shares:
             c.wait_send()
 
+    save(k_o, k_d)
+    save(v_o, v_d)
+    save(ctx_o, ctx_d)
+    for g in grad_gathers:
+        g.far()
+    save(og, og_d)
+
     @pl.when(s < n - 1)
     def _():
         down.wait_send()
@@ -357,16 +392,22 @@
 
     for c in [side] + cross + relay:
         c.wait_send()
-
-
-def launch(body, names, args, outs, out_vmem, scratch, collective_id, limit, name):
+    for g in grad_gathers:
+        g.finish()
+    save.finish()
+
+
+def launch(
+    body, names, args, outs, out_vmem, scratch, collective_id, limit, name, placed=()
+):
     keys = list(scratch)
     count = len(names)
+    plain = [name for name in names if name not in placed]
 
     def kernel(*refs):
         refs_in, refs = refs[:count], refs[count:]
         outs_r, refs = refs[: len(outs)], refs[len(outs) :]
-        held, refs = dict(zip(names, refs[:count])), refs[count:]
+        held, refs = dict(zip(plain, refs)), refs[len(plain) :]
         body(refs_in, outs_r, held, dict(zip(keys, refs)))
 
     scratch = dict(scratch)
@@ -377,7 +418,8 @@
         out_specs=tuple(
             pl.BlockSpec(memory_space=VM if in_vmem else pl.ANY) for in_vmem in out_vmem
         ),
-        scratch_shapes=[VM(a.shape, a.dtype) for a in args] + list(scratch.values()),
+        scratch_shapes=[VM(a.shape, a.dtype) for x, a in zip(names, args) if x in plain]
+        + list(scratch.values()),
         compiler_params=pltpu.CompilerParams(
             collective_id=collective_id, has_side_effects=True, vmem_limit_bytes=limit << 20
         ),
@@ -394,6 +436,7 @@
     dma = pltpu.SemaphoreType.DMA
     outs = (
         sds((micro, block, width), BF),
+        sds((micro, block, width), BF),
         sds((micro, block, chan), BF),
         sds((micro, CTX + 2 * block, chan), BF),
         sds((micro, CTX + 2 * block, chan), BF),
@@ -403,6 +446,14 @@
     )
     scratch = dict(
         fetch=dma((len(FRONT_IN),)),
+        nf=VM((micro, block, width), BF),
+        og=VM((micro, block, width), BF),
+        q=VM((micro, block, chan), BF),
+        k=VM((micro, CTX + 2 * block, chan), BF),
+        v=VM((micro, CTX + 2 * block, chan), BF),
+        ctxa=VM((micro, CTX, width), BF),
+        save=dma((6,)),
+        os=dma((2, 3)),
         u=VM((micro, block, chan), F32),
         gath=VM((n, 2 * NS + 8, chan), F32),
         pay=VM((2 * NS + 8, chan), F32),
@@ -417,16 +468,18 @@
         cs=dma((4,)),
         cr=dma((4,)),
     )
+    scratch["or"] = dma((2, 3))
     return launch(
         functools.partial(front_kernel, n),
         FRONT_IN,
         args,
         outs,
-        [True] * 7,
+        [False] * 6 + [True] * 2,
         scratch,
         0,
         62,
         "front",
+        ("ogm",),
     )
 
 
@@ -443,8 +496,9 @@
 
 def middle_kernel(refs_in, outs, held, scr):
     fetch = Fetch(MIDDLE_IN, refs_in, held, scr["fetch"])
-    mlp_o, h1_o, dh1_o, ffn_o, att, lse, gain_o = outs
     nm, pm, dm, hid, dpre = (scr[x] for x in ("nm", "pm", "dm", "hid", "dpre"))
+    mlp_o, h1_o, ffn_o, att, lse = (scr[x] for x in ("mlp", "h1", "ffn", "att", "lse"))
+    save = Save(scr["save"])
     q, k, v, keep, w_out, tok, gain, w_up, w_down, og = (held[x] for x in MIDDLE_IN)
     me = tp_peers()[0]
     near = me // 2
@@ -491,8 +545,8 @@
             ref.at[m], scr["over"].at[at], scr["into"].at[at], scr["ss"].at[at], scr["sr"].at[at]
         )
 
+    mlp_d, h1_d, dm_d, ffn_d, att_d, lse_d = outs
     sums1 = [scatter(0, m, pm) for m in range(2)]
-    sums2 = [scatter(1, m, dm) for m in range(2)]
     gathers = [Gather(nm.at[m], scr["gs"].at[m], scr["gr"].at[m]) for m in range(2)]
 
     def project(m):
@@ -553,6 +607,8 @@
     sums1[0].turn()
     attend(1)
     project(1)
+    save(att, att_d)
+    save(lse, lse_d)
     sums1[1].start()
     sums1[1].turn()
     fetch.need("tok", "gain")
@@ -561,18 +617,17 @@
     gathers[0].near()
     feed(0, near)
     residual(1)
+    save(h1_o, h1_d)
     gathers[0].pass_on()
     gathers[1].near()
     feed(1, near)
     gathers[0].far()
     feed(0, 1 - near)
-    sums2[0].start()
+    save(dm.at[0], dm_d.at[0])
     gathers[1].pass_on()
-    sums2[0].turn()
     gathers[1].far()
     feed(1, 1 - near)
-    sums2[1].start()
-    sums2[1].turn()
+    save(dm.at[1], dm_d.at[1])
 
     def down_sum(i, c):
         left = hid[:, pl.ds(pl.multiple_of(i * tile, tile), tile)]
@@ -591,18 +646,17 @@
             ).astype(BF)
         return c
 
+    high = panels * tile * (width // tile)
     lax.fori_loop(0, panels, down_sum, 0)
-    lax.fori_loop(0, width // tile, up_sum, 0)
+    save(ffn_o.at[high : 2 * high], ffn_d.at[high : 2 * high])
     lower(0)
     lower(1)
-    total = jnp.zeros((1, width), F32)
-    for m in range(2):
-        back, gain_grad = rms_back(h1_o[m], gain[...], sums2[m].end())
-        total = total + gain_grad
-        dh1_o[m] = og[m, own, :].astype(F32) + back
-    gain_o[...] = total
+    save(mlp_o, mlp_d)
+    lax.fori_loop(0, width // tile, up_sum, 0)
+    save(ffn_o.at[0:high], ffn_d.at[0:high])
     for m in range(2):
         gathers[m].finish()
+    save.finish()
 
 
 def middle(*args):
@@ -616,11 +670,10 @@
     outs = (
         sds((micro, block, width), BF),
         sds((micro, rows, width), F32),
-        sds((micro, rows, width), F32),
+        sds((micro, block, width), BF),
         sds((2 * units * width // 256, 256), BF),
         sds((micro, block, chan), BF),
         sds((micro, chan // HD, 1, block), F32),
-        sds((1, width), F32),
     )
     scratch = dict(
         fetch=dma((len(MIDDLE_IN),)),
@@ -629,15 +682,21 @@
         dm=VM((micro, block, width), BF),
         hid=VM((micro * block, units), BF),
         dpre=VM((micro * block, units), BF),
-        over=VM((4, rows, width), BF),
-        into=VM((4, 3, rows, width), BF),
-        ss=dma((4, 3)),
-        sr=dma((4, 3)),
+        mlp=VM((micro, block, width), BF),
+        h1=VM((micro, rows, width), F32),
+        ffn=VM((2 * units * width // 256, 256), BF),
+        att=VM((micro, block, chan), BF),
+        lse=VM((micro, chan // HD, 1, block), F32),
+        save=dma((8,)),
+        over=VM((2, rows, width), BF),
+        into=VM((2, 3, rows, width), BF),
+        ss=dma((2, 3)),
+        sr=dma((2, 3)),
         gs=dma((2, 3)),
         gr=dma((2, 3)),
     )
     return launch(
-        middle_kernel, MIDDLE_IN, args, outs, [True] * 7, scratch, 1, 62, "middle"
+        middle_kernel, MIDDLE_IN, args, outs, [False] * 6, scratch, 1, 62, "middle"
     )
 
 
@@ -784,21 +843,22 @@
     "endg",
     "mlp",
     "h1",
-    "dh1",
+    "dm",
+    "ogm",
+    "mid",
     "tok",
     "gain",
-    "midg",
     "ffn",
 )
 
 
 def last_kernel(n, refs_in, outs, h, scr):
-    x1, x2 = scr["x1"], scr["x2"]
+    x1, x2, x3 = scr["x1"], scr["x2"], scr["x3"]
     ffn_rows = refs_in[LAST_IN.index("ffn")].shape[0]
     h = dict(h, ffn=x1.at[0:ffn_rows])
     fetch = Fetch(LAST_IN, refs_in, h, scr["fetch"])
     need = fetch.need
-    mixed_o, tg_o, sum1_o, sum2_o, gain_o = outs
+    mixed_o, tg_o, sum1_o, sum2_o, small_o = outs
     s = lax.axis_index("seq")
     me, mate, across, diag = tp_peers()
     peers = (mate, across, diag)
@@ -811,9 +871,10 @@
     gath[...] = jnp.zeros_like(gath)
     if x1.shape[0] > ffn_rows:
         x1[ffn_rows:] = jnp.zeros((x1.shape[0] - ffn_rows, chan), BF)
-    used2 = 4 * width + 3 * NS
+    used2 = 4 * width
     if x2.shape[0] > used2:
         x2[used2:] = jnp.zeros((x2.shape[0] - used2, chan), BF)
+    x3[...] = jnp.zeros_like(x3)
 
     @pl.when(s == n - 1)
     def _():
@@ -832,16 +893,34 @@
 
     ring1 = Ring(n, x1, scr["r1"], scr["s1s"], scr["s1r"])
     ring2 = Ring(n, x2, scr["r2"], scr["s2s"], scr["s2r"])
-    rr, da, dh1 = scr["rr"], scr["da"], h["dh1"]
-    need("dh1")
-    for m in range(2):
-        rr[m, own, :] = dh1[m].astype(BF)
+    ring3 = Ring(n, x3, scr["r3"], scr["s3s"], scr["s3r"])
+    rr, da, dh1, mlp, h1 = scr["rr"], scr["da"], scr["dh1"], h["mlp"], h["h1"]
+
+    def scatter(ref, at, m):
+        at = 2 * at + m
+        return Scatter(
+            ref.at[m], scr["over"].at[at], scr["into"].at[at], scr["ss"].at[at], scr["sr"].at[at]
+        )
+
+    mid_sums = [scatter(h["dm"], 0, m) for m in range(2)]
+    gathers = [Gather(rr.at[m], scr["rs"].at[m], scr["rrv"].at[m]) for m in range(2)]
+    need("dm")
     greeted(n, True)
-    gathers = [Gather(rr.at[m], scr["rs"].at[m], scr["rrv"].at[m]) for m in range(2)]
-    for g in gathers:
-        g.start()
+    for c in mid_sums:
+        c.start()
     need("ffn")
     ring1.start()
+    for c in mid_sums:
+        c.turn()
+    need("h1", "ogm", "mid")
+    mid_grad = jnp.zeros((1, width), F32)
+    for m in range(2):
+        back, one = rms_back(h1[m], h["mid"][...], mid_sums[m].end())
+        mid_grad = mid_grad + one
+        dh1[m] = h["ogm"][m].astype(F32) + back
+        rr[m, own, :] = dh1[m].astype(BF)
+        gathers[m].start()
+        ring1.go(m + 1)
     need("w_out", "q", "k", "v", "lse", "keep")
 
     q, k, v, lse, keep, w_out = (h[name] for name in ("q", "k", "v", "lse", "keep", "w_out"))
@@ -897,6 +976,7 @@
         g.near()
         g.pass_on()
         g.far()
+        ring1.tick(m + ring1.done)
         da[m] = dot(rr[m], w_out[...], NT).astype(BF)
 
         def heads(head, c):
@@ -904,11 +984,10 @@
             return c
 
         lax.fori_loop(0, chan // HD, heads, 0)
-        ring1.tick(m)
         return c
 
     lax.fori_loop(0, 2, stream_back, 0)
-    ring1.done = 2
+    ring1.done += 2
 
     cp, cr, dcs = scr["cp"], scr["cr"], scr["dcs"]
     wq, wk, wv = h["wq"], h["wk"], h["wv"]
@@ -927,18 +1006,11 @@
     ctx_out = [to_peer(i, cp.at[peers[i]], cr.at[i], 0) for i in range(3)]
     for c in ctx_out:
         c.start()
-    need("mlp", "h1")
-    mlp, h1 = h["mlp"], h["h1"]
-
-    def scatter(kind, m):
-        at = 2 * kind + m
-        return Scatter(
-            mlp.at[m], scr["over"].at[at], scr["into"].at[at], scr["ss"].at[at], scr["sr"].at[at]
-        )
-
-    mlp_sums = [scatter(0, m) for m in range(2)]
+    need("mlp")
+    mlp_sums = [scatter(mlp, 1, m) for m in range(2)]
     for c in mlp_sums:
         c.start()
+    ring1.go(5)
 
     u_s, du_s, hist = scr["u"], scr["du"], scr["hist"]
     cols = pl.ds(pl.multiple_of(me * chan, chan), chan)
@@ -985,10 +1057,13 @@
         right = rr[:, :, cols].reshape(2 * block, tile)
         at = pl.multiple_of(3 * width + j * tile, tile)
         x2[pl.ds(at, tile), :] = dot(flat_att, right, TN).astype(BF)
+        here = pl.ds(pl.multiple_of(j * tile, tile), tile)
+        left = nf[:, :, here].reshape(2 * block, tile)
+        x2[here, :] = dot(left, dq_s[...].reshape(2 * block, chan), TN).astype(BF)
         return c
 
+    ring1.go(6)
     lax.fori_loop(0, width // tile, proj, 0)
-    ring1.go(3)
 
     @pl.when(s < n - 1)
     def _():
@@ -1018,8 +1093,8 @@
         return remote(
             pay,
             gath.at[k],
-            scr["send_g"].at[0, k],
-            scr["recv_g"].at[0, k],
+            scr["send_g"].at[k],
+            scr["recv_g"].at[k],
             seq=lax.rem(s + n - k, n),
         )
 
@@ -1029,9 +1104,41 @@
         def _():
             spread(k).start()
 
-    ring1.go(4)
+    ring1.go(7)
     for m in range(2):
         mixed_o[m] = (h1[m] + mlp_sums[m].end()).astype(BF)
+    @pl.when(s < n - 1)
+    def _():
+        for i in range(4):
+            to_before(0, i, dkp.at[i], rk.at[i]).wait_recv()
+            to_before(1, i, dvp.at[i], rv.at[i]).wait_recv()
+
+    dk_b, dv_b = scr["dkb"], scr["dvb"]
+    for m in range(2):
+        for head in range(chan // HD):
+            lanes = slice(head * HD, (head + 1) * HD)
+            i = m * (chan // HD) + head
+            dk_b[m, :, lanes] = (dko[m, :, lanes] + rk[i].astype(F32)).astype(BF)
+            dv_b[m, :, lanes] = (dvo[m, :, lanes] + rv[i].astype(F32)).astype(BF)
+
+    need("ctx")
+    ctx = h["ctx"]
+
+    def kv_grads(i, c):
+        at = pl.multiple_of(i * tile, tile)
+        here = pl.ds(at, tile)
+        left = nf[:, :, here].reshape(2 * block, tile)
+        left_ctx = ctx[:, :, here].reshape(2 * CTX, tile)
+        for j, (own, far) in enumerate(((dk_b, dkc), (dv_b, dvc))):
+            value = dot(left, own[...].reshape(2 * block, chan), TN) + dot(
+                left_ctx, far[...].reshape(2 * CTX, chan), TN
+            )
+            x2[pl.ds((j + 1) * width + at, tile), :] = value.astype(BF)
+        return c
+
+    lax.fori_loop(0, width // tile, kv_grads, 0)
+    ring2.start()
+    ring1.go(8)
     for k in range(1, n):
 
         @pl.when(s + k < n)
@@ -1085,26 +1192,12 @@
         return hold[0], hold[1], d_drive, d_decay
 
     _, _, d_drive, d_decay = lax.fori_loop(0, (block - CTX) // 8, back_early, val[0:4])
-    at = 4 * width
-    x2[at : at + NS] = (-decay * (d_decay - d_drive * h["cin"][...] * decay / root)).astype(BF)
-    x2[at + NS : at + 2 * NS] = (d_drive * root).astype(BF)
-    x2[at + 2 * NS : at + 3 * NS] = val[4].astype(BF)
-    ring1.go(5)
-
-    @pl.when(s < n - 1)
-    def _():
-        for i in range(4):
-            to_before(0, i, dkp.at[i], rk.at[i]).wait_recv()
-            to_before(1, i, dvp.at[i], rv.at[i]).wait_recv()
-
-    dk_b, dv_b = scr["dkb"], scr["dvb"]
-    for m in range(2):
-        for head in range(chan // HD):
-            lanes = slice(head * HD, (head + 1) * HD)
-            i = m * (chan // HD) + head
-            dk_b[m, :, lanes] = (dko[m, :, lanes] + rk[i].astype(F32)).astype(BF)
-            dv_b[m, :, lanes] = (dvo[m, :, lanes] + rv[i].astype(F32)).astype(BF)
-
+    x3[0:NS] = (-decay * (d_decay - d_drive * h["cin"][...] * decay / root)).astype(BF)
+    x3[NS : 2 * NS] = (d_drive * root).astype(BF)
+    x3[2 * NS : 3 * NS] = val[4].astype(BF)
+    ring3.start()
+    ring1.go(9)
+    ring2.go(1)
     part_s = scr["part"]
 
     def normed_part(i, c):
@@ -1119,32 +1212,16 @@
         mlp[m, here, :] = part_s[...].astype(BF)
         return c
 
-    finals = [scatter(1, m) for m in range(2)]
+    finals = [scatter(mlp, 0, m) for m in range(2)]
     for m in range(2):
         lax.fori_loop(2 * m, 2 * m + 2, normed_part, 0)
         finals[m].start()
-    finals[0].turn()
-    need("ctx")
-    ctx = h["ctx"]
-
-    def grads(i, c):
-        at = pl.multiple_of(i * tile, tile)
-        here = pl.ds(at, tile)
-        left = nf[:, :, here].reshape(2 * block, tile)
-        left_ctx = ctx[:, :, here].reshape(2 * CTX, tile)
-        x2[pl.ds(at, tile), :] = dot(left, dq_s[...].reshape(2 * block, chan), TN).astype(BF)
-        for j, (own, far) in enumerate(((dk_b, dkc), (dv_b, dvc))):
-            value = dot(left, own[...].reshape(2 * block, chan), TN) + dot(
-                left_ctx, far[...].reshape(2 * CTX, chan), TN
-            )
-            x2[pl.ds((j + 1) * width + at, tile), :] = value.astype(BF)
-        return c
-
-    finals[1].turn()
-    lax.fori_loop(0, width // tile, grads, 0)
-    ring2.start()
-    ring1.go(6)
-    need("tok", "gain", "midg")
+    for c in finals:
+        c.turn()
+    ring1.go(10)
+    ring2.go(2)
+    ring3.go(1)
+    need("tok", "gain")
     gain_grad = jnp.zeros((1, width), F32)
     for m in range(2):
         back, one = rms_back(tok[m].astype(F32), h["gain"][...], finals[m].end())
@@ -1153,13 +1230,14 @@
     gp, gr, gs, gg = scr["gp"], scr["gr"], scr["gs"], scr["gg"]
     for j in range(4):
         gp[j, 0:1] = gain_grad[:, j * chan : (j + 1) * chan]
-        gp[j, 1:2] = h["midg"][:, j * chan : (j + 1) * chan]
+        gp[j, 1:2] = mid_grad[:, j * chan : (j + 1) * chan]
         gp[j, 2:8] = jnp.zeros((6, chan), F32)
     gains = [to_peer(i, gp.at[peers[i]], gr.at[i], 1) for i in range(3)]
     for c in gains:
         c.start()
-    ring1.go(7)
-    ring2.go(1)
+    ring1.go(11)
+    ring2.go(3)
+    ring3.go(2)
     total = gp[me]
     for i in range(3):
         gains[i].wait_recv()
@@ -1170,26 +1248,30 @@
         return remote(
             gs,
             gg.at[k],
-            scr["send_g"].at[1, k],
-            scr["recv_g"].at[1, k],
+            scr["gain_s"].at[k],
+            scr["gain_r"].at[k],
             seq=lax.rem(s + k, n),
         )
 
     for k in range(1, n):
         gain_out(k).start()
-    for t in range(8, 15):
+    for t in range(12, 15):
         ring1.go(t)
-        ring2.go(t - 6)
+        ring2.go(t - 8)
+        ring3.go(t - 9)
     store1 = pltpu.make_async_copy(x1, sum1_o, scr["store"].at[0])
     store1.start()
+    for t in range(7, 15):
+        ring2.go(t)
+        ring3.go(min(t - 1 + (t - 7) // 3, 14))
+    store2 = pltpu.make_async_copy(x2, sum2_o, scr["store"].at[1])
+    store2.start()
+    ring3.go(14)
+    small_o[0 : 3 * NS] = x3[0 : 3 * NS].astype(F32)
     for k in range(1, n):
         gain_out(k).wait_recv()
         total = total + gg[k]
-    gain_o[...] = total
-    for t in range(9, 15):
-        ring2.go(t)
-    store2 = pltpu.make_async_copy(x2, sum2_o, scr["store"].at[1])
-    store2.start()
+    small_o[3 * NS : 3 * NS + 8] = total
     for k in range(1, n):
         gain_out(k).wait_send()
     for c in gains + ctx_out:
@@ -1212,6 +1294,7 @@
 
     ring1.drain()
     ring2.drain()
+    ring3.drain()
     store1.wait()
     store2.wait()
 
@@ -1230,18 +1313,23 @@
     sds = jax.ShapeDtypeStruct
     dma = pltpu.SemaphoreType.DMA
     step1 = ring_rows(n, by["ffn"].shape[0], 2)
-    step2 = ring_rows(n, 4 * width + 3 * NS, 1)
+    step2 = ring_rows(n, 4 * width, 2)
+    step3 = ring_rows(n, 3 * NS, 1)
     x1 = VM((4 * n * step1, chan), BF)
-    x2 = VM((2 * n * step2, chan), BF)
+    x2 = VM((4 * n * step2, chan), BF)
     scratch = dict(
         x1=x1,
         r1=VM((2, n - 1, 2, step1, chan), BF),
         x2=x2,
-        r2=VM((2, n - 1, 1, step2, chan), BF),
+        r2=VM((2, n - 1, 2, step2, chan), BF),
+        x3=VM((2 * n * step3, chan), BF),
+        r3=VM((2, n - 1, 1, step3, chan), BF),
         s1s=dma((2, 2, 2 * n - 2)),
         s1r=dma((2, 2, 2 * n - 2)),
-        s2s=dma((2, 1, 2 * n - 2)),
-        s2r=dma((2, 1, 2 * n - 2)),
+        s2s=dma((2, 2, 2 * n - 2)),
+        s2r=dma((2, 2, 2 * n - 2)),
+        s3s=dma((2, 1, 2 * n - 2)),
+        s3r=dma((2, 1, 2 * n - 2)),
         fetch=dma((len(LAST_IN),)),
         rr=VM((micro, block, width), BF),
         da=VM((micro, block, chan), BF),
@@ -1271,6 +1359,7 @@
         pay=VM((2 * NS + 8, chan), F32),
         gath=VM((n, 2 * NS + 8, chan), F32),
         part=VM((block // 2, width), F32),
+        dh1=VM((micro, rows, width), F32),
         over=VM((4, rows, width), BF),
         into=VM((4, 3, rows, width), BF),
         ss=dma((4, 3)),
@@ -1279,12 +1368,14 @@
         gr=VM((3, 8, chan), F32),
         gs=VM((8, chan), F32),
         gg=VM((n, 8, chan), F32),
+        gain_s=dma((n,)),
+        gain_r=dma((n,)),
         send_k=dma((2, 5)),
         recv_k=dma((2, 5)),
         send_c=dma((2, 3)),
         recv_c=dma((2, 3)),
-        send_g=dma((2, n)),
-        recv_g=dma((2, n)),
+        send_g=dma((n,)),
+        recv_g=dma((n,)),
         store=dma((2,)),
     )
     outs = (
@@ -1292,7 +1383,7 @@
         sds((micro, rows, width), F32),
         sds(x1.shape, BF),
         sds(x2.shape, BF),
-        sds((8, chan), F32),
+        sds((3 * NS + 8, chan), F32),
     )
     return launch(
         functools.partial(last_kernel, n),
@@ -1304,22 +1395,29 @@
         2,
         62,
         "last",
-    )
-
-
-def finish_kernel(up_i, down_i, proj_i, q_i, k_i, v_i, up, down, proj, q, k, v):
-    pairs = ((up_i, up), (down_i, down), (proj_i, proj), (q_i, q), (k_i, k), (v_i, v))
-    for src, dst in pairs:
-        dst[...] = src[...].astype(F32)
-
-
-def finish(sum1, sum2, width, units, chan):
+        ("ffn",),
+    )
+
+
+def finish_kernel(*refs):
+    half = len(refs) // 2
+    for src, dst in zip(refs[:half], refs[half:]):
+        dst[...] = src[...].astype(dst.dtype)
+
+
+def finish(sum1, sum2, mixed, tokens_grad, end, width, units, chan):
     across = width // chan
     sds = jax.ShapeDtypeStruct
     down_at = units * width // chan
     tall = lambda high, at: pl.BlockSpec((high, chan), lambda j: (at // high + j, 0))
     wide = lambda high: pl.BlockSpec((high, chan), lambda j: (0, j))
     col = pl.BlockSpec((chan, chan), lambda j: (j, 0))
+    micro, rows, _ = mixed.shape
+    same = [
+        pl.BlockSpec((micro, rows // across, width), lambda j: (0, j, 0)),
+        pl.BlockSpec((micro, rows // across, width), lambda j: (0, j, 0)),
+        pl.BlockSpec(end.shape, lambda j: (0, 0, 0)),
+    ]
     return pl.pallas_call(
         finish_kernel,
         grid=(across,),
@@ -1330,6 +1428,9 @@
             sds((width, chan), F32),
             sds((width, chan), F32),
             sds((width, chan), F32),
+            sds(mixed.shape, BF),
+            sds(tokens_grad.shape, F32),
+            sds(end.shape, F32),
         ),
         in_specs=[
             tall(width, 0),
@@ -1338,11 +1439,12 @@
             tall(chan, 0),
             tall(chan, width),
             tall(chan, 2 * width),
-        ],
-        out_specs=(wide(width), wide(units), wide(chan), col, col, col),
+        ]
+        + same,
+        out_specs=tuple([wide(width), wide(units), wide(chan), col, col, col] + same),
         compiler_params=pltpu.CompilerParams(vmem_limit_bytes=62 << 20),
         name="finish",
-    )(sum1, sum1, sum2, sum2, sum2, sum2)
+    )(sum1, sum1, sum2, sum2, sum2, sum2, mixed, tokens_grad, end)
 
 
 def body(
@@ -1366,36 +1468,36 @@
     micro, rows, width = tokens.shape
     chan = ssm_rate.shape[0]
     units = w_up.shape[1]
-    og = lax.all_gather(out_grad, "tp", axis=1, tiled=True)
     rate, cin, cout = ssm_rate.T, ssm_in.T, ssm_out.T
     flags = resets[:, 0]
     keep = jnp.zeros((8, chan), F32).at[0:micro].set((1.0 - flags.astype(F32))[:, None])
     init = jnp.swapaxes(init_state, 1, 2)
     endg = jnp.swapaxes(states_grad[:, 0], 1, 2)
     gain_row, mid_row = norm_gain[None], mid_gain[None]
-    nf, q, k, v, ctx, start, end = front(
-        tokens, gain_row, w_query, w_key, w_value, rate, cin, cout, keep, init
-    )
-    mlp, h1, dh1, ffn, att, lse, mid_part = middle(
+    nf, og, q, k, v, ctx, start, end = front(
+        tokens, gain_row, w_query, w_key, w_value, rate, cin, cout, keep, init, out_grad
+    )
+    mlp, h1, dm, ffn, att, lse = middle(
         q, k, v, keep, w_out, tokens, mid_row, w_up, w_down, og
     )
-    mixed, tokens_grad, sum1, sum2, gains = last(
+    mixed, tokens_grad, sum1, sum2, small = last(
         *(q, k, v, lse, att, w_out, nf, ctx, w_query, w_key, w_value, rate, cin, cout),
-        *(start, keep, endg, mlp, h1, dh1, tokens, gain_row, mid_part, ffn),
-    )
-    up_g, down_g, proj_g, query_g, key_g, value_g = finish(sum1, sum2, width, units, chan)
-    small = sum2[4 * width : 4 * width + 3 * NS].astype(F32)
+        *(start, keep, endg, mlp, h1, dm, out_grad, mid_row, tokens, gain_row, ffn),
+    )
+    up_g, down_g, proj_g, query_g, key_g, value_g, mixed, tokens_grad, end = finish(
+        sum1, sum2, mixed, tokens_grad, end, width, units, chan
+    )
     rate_g, in_g, out_g = (small[i * NS : (i + 1) * NS].T for i in range(3))
     return (
         mixed,
         jnp.swapaxes(end, 1, 2)[:, None],
         tokens_grad,
-        gains[0],
+        small[3 * NS],
         query_g,
         key_g,
         value_g,
         proj_g,
-        gains[1],
+        small[3 * NS + 1],
         up_g,
         down_g,
         rate_g,

time: 326 us -> 300 us (0.920)
  between operations: 14.1 us -> 0.85 us
  Pallas kernels: 304 us -> 294 us
    pallas_call x3, Pallas kernels: 296 us -> 286 us  [launch(): pl.pallas_call(kernel, out_shape=tuple(outs), in_specs=[pl.BlockSpec(memo...]
  transfers between devices with their start and end apart: 1 -> 0, of which waited for: 0 -> 0; matrix products, arithmetic and copies ran while one was open for 0% -> 0% of each run, Pallas kernels for 14% -> 0%
where the time goes in v2:
time: 300 us; the launch traced here: 299 us
  Pallas kernels  294 us (98%)
  local copies, waits for them, and re-layouts  3.39 us (1%)
    pallas_call x3, Pallas kernels, launch(): pl.pallas_call(kernel, out_shape=tuple(outs), in_specs=[pl.BlockSpec(memo...  286 us
    pallas_call x1, Pallas kernels, finish(): pl.pallas_call(finish_kernel, grid=(across,), out_shape=(sds((width, unit...  8.74 us

profile of v2, /device:TPU:0, one launch (start us, length us, event | category | flops | bytes accessed | tf_op | source)
XLA Modules:
  0.0 299.4 jit_solution(9506952416395674651)
XLA Ops:
  0.6 0.7 subtract_bitcast_fusion
  1.3 0.7 scatter.8.refs_8_.refs_3_.refs_15_
  2.0 36.0 %front.1 = (bf16[2,512,1024]{2,1,0:T(8,128)(2,1)}, bf16[2,512,1024]{2,1,0:T(8,128)(2,1)}, bf16[2,512,256]{2,1,0:T(8,128)(2,1)}, bf16[2,1152,256]{2,1,0:T(8,128)(...) custom-call(bf16[2,128,1024]{2,1,0:T(8,128)(2,1)} %refs_22_.1, ...), custom_call_target="tpu_custom_call" | custom-call | tf_op jit(solution)/shard_map/front/pallas_call | solution.py:414
  38.0 50.8 %middle.1 = (bf16[2,512,1024]{2,1,0:T(8,128)(2,1)}, f32[2,128,1024]{2,1,0:T(8,128)}, bf16[2,512,1024]{2,1,0:T(8,128)(2,1)}, bf16[8192,256]{1,0:T(8,128)(2,1)}, b...) custom-call(bf16[2,512,256]{2,1,0:T(8,128)(2,1)} %get-tuple-element.54.refs_0_, ...), custom_call_target="tpu_custom_call" | custom-call | tf_op jit(solution)/shard_map/middle/pallas_call | solution.py:414
  88.7 199.0 %last.1 = (bf16[2,128,1024]{2,1,0:T(8,128)(2,1)}, f32[2,128,1024]{2,1,0:T(8,128)}, bf16[8192,256]{1,0:T(8,128)(2,1)}, bf16[4096,256]{1,0:T(8,128)(2,1)}, f32[56,256]{1,0:T(8,128)}) custom-call(bf16[2,512,256]{2,1,0:T(8,128)(2,1)} %get-tuple-element.54.refs_0_, bf16[2,1152,256]{2,1,0:T(8,128)(2,1)} %get-tuple-element.55.refs_1_, ...), custom_call_target="tpu_custom_call" | custom-call | tf_op jit(solution)/shard_map/last/pallas_call | solution.py:414
  287.7 1.3 fusion
  289.1 1.4 slice_bitcast_fusion
  290.5 8.7 %finish.1 = (f32[1024,1024]{1,0:T(8,128)}, f32[1024,1024]{1,0:T(8,128)}, f32[256,1024]{1,0:T(8,128)}, f32[1024,256]{1,0:T(8,128)}, f32[1024,256]{1,0:T(8,128)}, ...) custom-call(bf16[8192,256]{1,0:T(8,128)(2,1)} %get-tuple-element.67.refs_0, ...), custom_call_target="tpu_custom_call" | custom-call | tf_op jit(solution)/shard_map/finish/pallas_call | solution.py:1421
  (1 shorter events, 0.0 us)

commit v3 on v2

--- a/solution.py
+++ b/solution.py
@@ -150,7 +150,23 @@
         return value
 
 
-FRONT_IN = ("tok", "gain", "wq", "wk", "wv", "rate", "cin", "cout", "keep", "init", "ogm")
+FORWARD_IN = (
+    "tok",
+    "gain",
+    "wk",
+    "wv",
+    "wq",
+    "rate",
+    "cin",
+    "cout",
+    "keep",
+    "init",
+    "ogm",
+    "w_out",
+    "mid",
+    "w_up",
+    "w_down",
+)
 
 
 class Save:
@@ -166,15 +182,15 @@
             c.wait()
 
 
-def front_kernel(n, refs_in, outs, held, scr):
+def forward_kernel(n, refs_in, outs, held, scr):
     s = lax.axis_index("seq")
     me, mate, across, diag = tp_peers()
     og = scr["og"]
     own_rows = og.shape[1] // 4
     own = pl.ds(pl.multiple_of(me * own_rows, own_rows), own_rows)
     held = dict(held, ogm=og.at[:, own, :])
-    fetch = Fetch(FRONT_IN, refs_in, held, scr["fetch"])
-    nf_d, og_d, q_d, k_d, v_d, ctx_d, start_o, end_o = outs
+    fetch = Fetch(FORWARD_IN, refs_in, held, scr["fetch"])
+    nf_d, q_d, k_d, v_d, ctx_d, start_o, end_o = outs[:7]
     nf, q_o, k_o, v_o, ctx_o = (scr[x] for x in ("nf", "q", "k", "v", "ctxa"))
     save = Save(scr["save"])
     grad_gathers = [Gather(og.at[m], scr["os"].at[m], scr["or"].at[m]) for m in range(2)]
@@ -241,7 +257,8 @@
         @pl.when(s < n - 1)
         def _():
             pass_kv(2 * order, k_o, half).start()
-            pass_kv(2 * order + 1, v_o, half).start()
+            if order == 0:
+                pass_kv(1, v_o, half).start()
 
         q_o[:, here, :] = dot(part, wq[...]).astype(BF).reshape(2, high, chan)
 
@@ -341,6 +358,7 @@
     @pl.when(s < n - 1)
     def _():
         down.start()
+        pass_kv(3, v_o, 1 - near).start()
 
     for m in range(2):
         start_o[m] = begin[m]
@@ -373,9 +391,7 @@
     save(k_o, k_d)
     save(v_o, v_d)
     save(ctx_o, ctx_d)
-    for g in grad_gathers:
-        g.far()
-    save(og, og_d)
+    forward_middle(fetch, held, scr, outs[7:], save, q_o, k_o, v_o, og, grad_gathers)
 
     @pl.when(s < n - 1)
     def _():
@@ -427,62 +443,6 @@
     )(*args)
 
 
-def front(*args):
-    n = lax.axis_size("seq")
-    micro, rows, width = args[0].shape
-    block = 4 * rows
-    chan = args[5].shape[1]
-    sds = jax.ShapeDtypeStruct
-    dma = pltpu.SemaphoreType.DMA
-    outs = (
-        sds((micro, block, width), BF),
-        sds((micro, block, width), BF),
-        sds((micro, block, chan), BF),
-        sds((micro, CTX + 2 * block, chan), BF),
-        sds((micro, CTX + 2 * block, chan), BF),
-        sds((micro, CTX, width), BF),
-        sds((micro, NS, chan), F32),
-        sds((micro, NS, chan), F32),
-    )
-    scratch = dict(
-        fetch=dma((len(FRONT_IN),)),
-        nf=VM((micro, block, width), BF),
-        og=VM((micro, block, width), BF),
-        q=VM((micro, block, chan), BF),
-        k=VM((micro, CTX + 2 * block, chan), BF),
-        v=VM((micro, CTX + 2 * block, chan), BF),
-        ctxa=VM((micro, CTX, width), BF),
-        save=dma((6,)),
-        os=dma((2, 3)),
-        u=VM((micro, block, chan), F32),
-        gath=VM((n, 2 * NS + 8, chan), F32),
-        pay=VM((2 * NS + 8, chan), F32),
-        y=VM((micro, CTX, chan), F32),
-        ctx=VM((micro, CTX, chan), BF),
-        ts=dma((9,)),
-        tr=dma((9,)),
-        kvs=dma((4,)),
-        kvr=dma((4,)),
-        gs=dma((n,)),
-        gr=dma((n,)),
-        cs=dma((4,)),
-        cr=dma((4,)),
-    )
-    scratch["or"] = dma((2, 3))
-    return launch(
-        functools.partial(front_kernel, n),
-        FRONT_IN,
-        args,
-        outs,
-        [False] * 6 + [True] * 2,
-        scratch,
-        0,
-        62,
-        "front",
-        ("ogm",),
-    )
-
-
 def rms_back(x, gain, grad):
     inv = lax.rsqrt(jnp.mean(x * x, axis=-1, keepdims=True) + eps_norm)
     unit = x * inv
@@ -491,15 +451,12 @@
     return inv * (scaled - unit * jnp.mean(scaled * unit, axis=-1, keepdims=True)), gain_grad
 
 
-MIDDLE_IN = ("q", "k", "v", "keep", "w_out", "tok", "gain", "w_up", "w_down", "og")
-
-
-def middle_kernel(refs_in, outs, held, scr):
-    fetch = Fetch(MIDDLE_IN, refs_in, held, scr["fetch"])
+def forward_middle(fetch, held, scr, outs, save, q, k, v, og, grad_gathers):
     nm, pm, dm, hid, dpre = (scr[x] for x in ("nm", "pm", "dm", "hid", "dpre"))
     mlp_o, h1_o, ffn_o, att, lse = (scr[x] for x in ("mlp", "h1", "ffn", "att", "lse"))
-    save = Save(scr["save"])
-    q, k, v, keep, w_out, tok, gain, w_up, w_down, og = (held[x] for x in MIDDLE_IN)
+    keep, w_out, tok, gain, w_up, w_down = (
+        held[x] for x in ("keep", "w_out", "tok", "mid", "w_up", "w_down")
+    )
     me = tp_peers()[0]
     near = me // 2
     block = q.shape[1]
@@ -507,7 +464,6 @@
     width = w_out.shape[1]
     tile = 256
     panels = w_up.shape[1] // tile
-    greet(0, False)
     own = pl.ds(pl.multiple_of(me * rows, rows), rows)
     edge0 = k.shape[1] - block
     half = block // 2
@@ -547,7 +503,7 @@
 
     mlp_d, h1_d, dm_d, ffn_d, att_d, lse_d = outs
     sums1 = [scatter(0, m, pm) for m in range(2)]
-    gathers = [Gather(nm.at[m], scr["gs"].at[m], scr["gr"].at[m]) for m in range(2)]
+    gathers = [Gather(nm.at[m], scr["mgs"].at[m], scr["mgr"].at[m]) for m in range(2)]
 
     def project(m):
         def one(j, c):
@@ -589,20 +545,20 @@
 
         lax.fori_loop(0, width // tile, back, 0)
 
-    def lower(m):
+    def lower(m, part):
+        here = pl.ds(pl.multiple_of(part * half, half), half)
+        flat = pl.ds(pl.multiple_of(m * block + part * half, half), half)
+
         def one(j, c):
             cols = pl.ds(pl.multiple_of(j * tile, tile), tile)
-            flat = slice(m * block, (m + 1) * block)
-            mlp_o[m, :, cols] = dot(hid[flat, :], w_down[:, cols]).astype(BF)
+            mlp_o[m, here, cols] = dot(hid[flat, :], w_down[:, cols]).astype(BF)
             return c
 
         lax.fori_loop(0, width // tile, one, 0)
 
-    fetch.need("q", "k", "v", "keep")
     attend(0)
     fetch.need("w_out")
     project(0)
-    greeted(0, False)
     sums1[0].start()
     sums1[0].turn()
     attend(1)
@@ -611,9 +567,11 @@
     save(lse, lse_d)
     sums1[1].start()
     sums1[1].turn()
-    fetch.need("tok", "gain")
+    fetch.need("mid")
     residual(0)
-    fetch.need("w_up", "w_down", "og")
+    fetch.need("w_up", "w_down")
+    for g in grad_gathers:
+        g.far()
     gathers[0].near()
     feed(0, near)
     residual(1)
@@ -621,6 +579,8 @@
     gathers[0].pass_on()
     gathers[1].near()
     feed(1, near)
+    lower(0, near)
+    lower(1, near)
     gathers[0].far()
     feed(0, 1 - near)
     save(dm.at[0], dm_d.at[0])
@@ -649,54 +609,83 @@
     high = panels * tile * (width // tile)
     lax.fori_loop(0, panels, down_sum, 0)
     save(ffn_o.at[high : 2 * high], ffn_d.at[high : 2 * high])
-    lower(0)
-    lower(1)
+    lower(0, 1 - near)
+    lower(1, 1 - near)
     save(mlp_o, mlp_d)
     lax.fori_loop(0, width // tile, up_sum, 0)
     save(ffn_o.at[0:high], ffn_d.at[0:high])
     for m in range(2):
         gathers[m].finish()
-    save.finish()
-
-
-def middle(*args):
-    q, w_out, og, w_up = args[0], args[4], args[9], args[7]
-    micro, block, width = og.shape
-    rows = block // 4
-    units = w_up.shape[1]
-    chan = q.shape[2]
+
+
+def forward(*args):
+    n = lax.axis_size("seq")
+    by = dict(zip(FORWARD_IN, args))
+    micro, rows, width = by["tok"].shape
+    block = 4 * rows
+    chan = by["rate"].shape[1]
+    units = by["w_up"].shape[1]
+    keys = CTX + 2 * block
     sds = jax.ShapeDtypeStruct
     dma = pltpu.SemaphoreType.DMA
-    outs = (
-        sds((micro, block, width), BF),
-        sds((micro, rows, width), F32),
-        sds((micro, block, width), BF),
-        sds((2 * units * width // 256, 256), BF),
-        sds((micro, block, chan), BF),
-        sds((micro, chan // HD, 1, block), F32),
+    results = dict(
+        nf=sds((micro, block, width), BF),
+        q=sds((micro, block, chan), BF),
+        k=sds((micro, keys, chan), BF),
+        v=sds((micro, keys, chan), BF),
+        ctxa=sds((micro, CTX, width), BF),
+        start=sds((micro, NS, chan), F32),
+        end=sds((micro, NS, chan), F32),
+        mlp=sds((micro, block, width), BF),
+        h1=sds((micro, rows, width), F32),
+        dm=sds((micro, block, width), BF),
+        ffn=sds((2 * units * width // 256, 256), BF),
+        att=sds((micro, block, chan), BF),
+        lse=sds((micro, chan // HD, 1, block), F32),
     )
-    scratch = dict(
-        fetch=dma((len(MIDDLE_IN),)),
+    in_vmem = ("start", "end")
+    scratch = {x: VM(a.shape, a.dtype) for x, a in results.items() if x not in in_vmem}
+    scratch.update(
+        og=VM((micro, block, width), BF),
+        fetch=dma((len(FORWARD_IN),)),
+        save=dma((16,)),
+        os=dma((2, 3)),
+        u=VM((micro, block, chan), F32),
+        gath=VM((n, 2 * NS + 8, chan), F32),
+        pay=VM((2 * NS + 8, chan), F32),
+        y=VM((micro, CTX, chan), F32),
+        ctx=VM((micro, CTX, chan), BF),
+        ts=dma((9,)),
+        tr=dma((9,)),
+        kvs=dma((4,)),
+        kvr=dma((4,)),
+        gs=dma((n,)),
+        gr=dma((n,)),
+        cs=dma((4,)),
+        cr=dma((4,)),
         nm=VM((micro, block, width), BF),
         pm=VM((micro, block, width), BF),
-        dm=VM((micro, block, width), BF),
         hid=VM((micro * block, units), BF),
         dpre=VM((micro * block, units), BF),
-        mlp=VM((micro, block, width), BF),
-        h1=VM((micro, rows, width), F32),
-        ffn=VM((2 * units * width // 256, 256), BF),
-        att=VM((micro, block, chan), BF),
-        lse=VM((micro, chan // HD, 1, block), F32),
-        save=dma((8,)),
         over=VM((2, rows, width), BF),
         into=VM((2, 3, rows, width), BF),
         ss=dma((2, 3)),
         sr=dma((2, 3)),
-        gs=dma((2, 3)),
-        gr=dma((2, 3)),
+        mgs=dma((2, 3)),
+        mgr=dma((2, 3)),
     )
+    scratch["or"] = dma((2, 3))
     return launch(
-        middle_kernel, MIDDLE_IN, args, outs, [False] * 6, scratch, 1, 62, "middle"
+        functools.partial(forward_kernel, n),
+        FORWARD_IN,
+        args,
+        tuple(results.values()),
+        [x in in_vmem for x in results],
+        scratch,
+        0,
+        62,
+        "forward",
+        ("ogm",),
     )
 
 
@@ -1405,7 +1394,7 @@
         dst[...] = src[...].astype(dst.dtype)
 
 
-def finish(sum1, sum2, mixed, tokens_grad, end, width, units, chan):
+def finish(sum1, sum2, mixed, tokens_grad, end, small, width, units, chan):
     across = width // chan
     sds = jax.ShapeDtypeStruct
     down_at = units * width // chan
@@ -1418,6 +1407,8 @@
         pl.BlockSpec((micro, rows // across, width), lambda j: (0, j, 0)),
         pl.BlockSpec(end.shape, lambda j: (0, 0, 0)),
     ]
+    states = [pl.BlockSpec((NS, chan), lambda j, i=i: (i, 0)) for i in range(3)]
+    alone = [pl.BlockSpec((NS, chan), lambda j: (0, 0))] * 3
     return pl.pallas_call(
         finish_kernel,
         grid=(across,),
@@ -1431,6 +1422,9 @@
             sds(mixed.shape, BF),
             sds(tokens_grad.shape, F32),
             sds(end.shape, F32),
+            sds((NS, chan), F32),
+            sds((NS, chan), F32),
+            sds((NS, chan), F32),
         ),
         in_specs=[
             tall(width, 0),
@@ -1440,11 +1434,12 @@
             tall(chan, width),
             tall(chan, 2 * width),
         ]
-        + same,
-        out_specs=tuple([wide(width), wide(units), wide(chan), col, col, col] + same),
+        + same
+        + states,
+        out_specs=tuple([wide(width), wide(units), wide(chan), col, col, col] + same + alone),
         compiler_params=pltpu.CompilerParams(vmem_limit_bytes=62 << 20),
         name="finish",
-    )(sum1, sum1, sum2, sum2, sum2, sum2, mixed, tokens_grad, end)
+    )(sum1, sum1, sum2, sum2, sum2, sum2, mixed, tokens_grad, end, small, small, small)
 
 
 def body(
@@ -1470,24 +1465,22 @@
     units = w_up.shape[1]
     rate, cin, cout = ssm_rate.T, ssm_in.T, ssm_out.T
     flags = resets[:, 0]
-    keep = jnp.zeros((8, chan), F32).at[0:micro].set((1.0 - flags.astype(F32))[:, None])
+    keep = jnp.pad(1.0 - flags.astype(F32), (0, 8 - micro))
+    keep = jnp.broadcast_to(keep[:, None], (8, chan))
     init = jnp.swapaxes(init_state, 1, 2)
     endg = jnp.swapaxes(states_grad[:, 0], 1, 2)
     gain_row, mid_row = norm_gain[None], mid_gain[None]
-    nf, og, q, k, v, ctx, start, end = front(
-        tokens, gain_row, w_query, w_key, w_value, rate, cin, cout, keep, init, out_grad
-    )
-    mlp, h1, dm, ffn, att, lse = middle(
-        q, k, v, keep, w_out, tokens, mid_row, w_up, w_down, og
+    nf, q, k, v, ctx, start, end, mlp, h1, dm, ffn, att, lse = forward(
+        *(tokens, gain_row, w_key, w_value, w_query, rate, cin, cout, keep, init, out_grad),
+        *(w_out, mid_row, w_up, w_down),
     )
     mixed, tokens_grad, sum1, sum2, small = last(
         *(q, k, v, lse, att, w_out, nf, ctx, w_query, w_key, w_value, rate, cin, cout),
         *(start, keep, endg, mlp, h1, dm, out_grad, mid_row, tokens, gain_row, ffn),
     )
-    up_g, down_g, proj_g, query_g, key_g, value_g, mixed, tokens_grad, end = finish(
-        sum1, sum2, mixed, tokens_grad, end, width, units, chan
-    )
-    rate_g, in_g, out_g = (small[i * NS : (i + 1) * NS].T for i in range(3))
+    done = finish(sum1, sum2, mixed, tokens_grad, end, small, width, units, chan)
+    up_g, down_g, proj_g, query_g, key_g, value_g, mixed, tokens_grad, end = done[:9]
+    rate_g, in_g, out_g = (part.T for part in done[9:])
     return (
         mixed,
         jnp.swapaxes(end, 1, 2)[:, None],

time: 300 us -> 291 us (0.970)
  Pallas kernels: 294 us -> 287 us
    pallas_call x3 -> x2, Pallas kernels: 286 us -> 278 us  [launch(): pl.pallas_call(kernel, out_shape=tuple(outs), in_specs=[pl.BlockSpec(memo...]
where the time goes in v3:
time: 291 us
  Pallas kernels  287 us (99%)
    pallas_call x2, Pallas kernels, launch(): pl.pallas_call(kernel, out_shape=tuple(outs), in_specs=[pl.BlockSpec(memo...  278 us
    pallas_call x1, Pallas kernels, finish(): pl.pallas_call(finish_kernel, grid=(across,), out_shape=(sds((width, unit...  8.81 us

profile of v3, /device:TPU:0, one launch (start us, length us, event | category | flops | bytes accessed | tf_op | source)
XLA Modules:
  0.0 290.8 jit_solution(4171392834376829319)
XLA Ops:
  0.6 0.7 subtract_bitcast_fusion
  1.3 0.7 broadcast_in_dim.16.refs_8_.refs_15_
  2.0 83.6 %forward.1 = (bf16[2,512,1024]{2,1,0:T(8,128)(2,1)}, bf16[2,512,256]{2,1,0:T(8,128)(2,1)}, bf16[2,1152,256]{2,1,0:T(8,128)(2,1)}, bf16[2,1152,256]{2,1,0:T(8,128...) custom-call(bf16[2,128,1024]{2,1,0:T(8,128)(2,1)} %refs_22_.1, ...), custom_call_target="tpu_custom_call" | custom-call | tf_op jit(solution)/shard_map/forward/pallas_call | solution.py:430
  85.5 194.9 %last.1 = (bf16[2,128,1024]{2,1,0:T(8,128)(2,1)}, f32[2,128,1024]{2,1,0:T(8,128)}, bf16[8192,256]{1,0:T(8,128)(2,1)}, bf16[4096,256]{1,0:T(8,128)(2,1)}, f32[56,256]{1,0:T(8,128)}) custom-call(bf16[2,512,256]{2,1,0:T(8,128)(2,1)} %get-tuple-element.44.refs_0_, bf16[2,1152,256]{2,1,0:T(8,128)(2,1)} %get-tuple-element.45.refs_1_, ...), custom_call_target="tpu_custom_call" | custom-call | tf_op jit(solution)/shard_map/last/pallas_call | solution.py:430
  280.4 1.3 fusion
  281.8 8.8 %finish.1 = (f32[1024,1024]{1,0:T(8,128)}, f32[1024,1024]{1,0:T(8,128)}, f32[256,1024]{1,0:T(8,128)}, f32[1024,256]{1,0:T(8,128)}, f32[1024,256]{1,0:T(8,128)}, ...) custom-call(bf16[8192,256]{1,0:T(8,128)(2,1)} %get-tuple-element.56., ...), custom_call_target="tpu_custom_call" | custom-call | tf_op jit(solution)/shard_map/finish/pallas_call | solution.py:1412
  (1 shorter events, 0.0 us)

commit v4 on v3

--- a/solution.py
+++ b/solution.py
@@ -35,6 +35,11 @@
     me = lax.axis_index("tp")
     mate = me + 1 - 2 * lax.rem(me, 2)
     return me, mate, lax.rem(me + 2, 4), lax.rem(mate + 2, 4)
+
+
+def flag_rows(keep):
+    rest = jnp.zeros((NS - keep.shape[0], keep.shape[1]), F32)
+    return jnp.concatenate([keep[...], rest], axis=0).astype(BF)
 
 
 def remote(src, dst, send, recv, **where):
@@ -289,9 +294,9 @@
     zero = jnp.zeros((NS, chan), F32)
     late = lax.fori_loop(0, (block - CTX) // 8, run, (zero, zero))
     last_state = lax.fori_loop((block - CTX) // 8, block // 8, run, late)
-    pay[0:NS] = last_state[0]
-    pay[NS : 2 * NS] = last_state[1]
-    pay[2 * NS : 2 * NS + 8] = keep[...]
+    for m in range(2):
+        pay[m * NS : (m + 1) * NS] = last_state[m].astype(BF)
+    pay[2 * NS : 3 * NS] = flag_rows(keep)
 
     def spread(k):
         return remote(
@@ -328,7 +333,7 @@
 
     def chain(b, end):
         k = jnp.maximum(s - b, 0)
-        got = gath[k]
+        got = gath[k].astype(F32)
         begin = entry((got[2 * NS : 2 * NS + 1], got[2 * NS + 1 : 2 * NS + 2]), end, b)
         new = tuple(got[m * NS : (m + 1) * NS] + whole * begin[m] for m in range(2))
         return tuple(jnp.where(b < s, new[m], end[m]) for m in range(2))
@@ -370,15 +375,23 @@
     @pl.when(s > 0)
     def _():
         down.wait_recv()
-        mine = ctx_o.at[:, :, cols]
+        theirs = lanes(across)
         shares = [
-            remote(mine, mine, scr["cs"].at[1 + i], scr["cr"].at[1 + i], tp=peer)
-            for i, peer in enumerate((across, diag, mate))
+            remote(
+                ctx_o.at[:, :, part],
+                ctx_o.at[:, :, part],
+                scr["cs"].at[1 + i],
+                scr["cr"].at[1 + i],
+                tp=peer,
+            )
+            for i, (part, peer) in enumerate(((cols, across), (cols, mate), (theirs, mate)))
         ]
-        for c in shares:
-            c.start()
-        for c in shares:
-            c.wait_recv()
+        shares[0].start()
+        shares[1].start()
+        shares[0].wait_recv()
+        shares[2].start()
+        shares[1].wait_recv()
+        shares[2].wait_recv()
         flat = ctx_o[...].reshape(2 * CTX, -1)
         k_o[:, 0:CTX, :] = dot(flat, wk[...]).astype(BF).reshape(2, CTX, chan)
         v_o[:, 0:CTX, :] = dot(flat, wv[...]).astype(BF).reshape(2, CTX, chan)
@@ -651,8 +664,8 @@
         save=dma((16,)),
         os=dma((2, 3)),
         u=VM((micro, block, chan), F32),
-        gath=VM((n, 2 * NS + 8, chan), F32),
-        pay=VM((2 * NS + 8, chan), F32),
+        gath=VM((n, 3 * NS, chan), BF),
+        pay=VM((3 * NS, chan), BF),
         y=VM((micro, CTX, chan), F32),
         ctx=VM((micro, CTX, chan), BF),
         ts=dma((9,)),
@@ -847,7 +860,7 @@
     h = dict(h, ffn=x1.at[0:ffn_rows])
     fetch = Fetch(LAST_IN, refs_in, h, scr["fetch"])
     need = fetch.need
-    mixed_o, tg_o, sum1_o, sum2_o, small_o = outs
+    mixed_o, tg_o, sum1_o, sum2_o, rate_o, cin_o, cout_o, gain_o = outs
     s = lax.axis_index("seq")
     me, mate, across, diag = tp_peers()
     peers = (mate, across, diag)
@@ -1075,8 +1088,8 @@
     whole = jnp.exp(-rate[...] * block)
     pay = scr["pay"]
     for m in range(2):
-        pay[m * NS : (m + 1) * NS] = reach * got[m] + whole * endg[m]
-    pay[2 * NS : 2 * NS + 8] = keep[...]
+        pay[m * NS : (m + 1) * NS] = (reach * got[m] + whole * endg[m]).astype(BF)
+    pay[2 * NS : 3 * NS] = flag_rows(keep)
 
     def spread(k):
         return remote(
@@ -1136,7 +1149,7 @@
 
     def chain(i, carry):
         k = n - 1 - i
-        got = gath[k]
+        got = gath[k].astype(F32)
         valid = s + k < n
         return tuple(
             jnp.where(
@@ -1256,11 +1269,12 @@
     store2 = pltpu.make_async_copy(x2, sum2_o, scr["store"].at[1])
     store2.start()
     ring3.go(14)
-    small_o[0 : 3 * NS] = x3[0 : 3 * NS].astype(F32)
+    for i, small_o in enumerate((rate_o, cin_o, cout_o)):
+        small_o[...] = x3[i * NS : (i + 1) * NS].astype(F32)
     for k in range(1, n):
         gain_out(k).wait_recv()
         total = total + gg[k]
-    small_o[3 * NS : 3 * NS + 8] = total
+    gain_o[...] = total
     for k in range(1, n):
         gain_out(k).wait_send()
     for c in gains + ctx_out:
@@ -1345,8 +1359,8 @@
         u=VM((micro, block, chan), F32),
         du=VM((micro, block, chan), F32),
         hist=VM((block + 1, micro, NS, chan), BF),
-        pay=VM((2 * NS + 8, chan), F32),
-        gath=VM((n, 2 * NS + 8, chan), F32),
+        pay=VM((3 * NS, chan), BF),
+        gath=VM((n, 3 * NS, chan), BF),
         part=VM((block // 2, width), F32),
         dh1=VM((micro, rows, width), F32),
         over=VM((4, rows, width), BF),
@@ -1372,14 +1386,17 @@
         sds((micro, rows, width), F32),
         sds(x1.shape, BF),
         sds(x2.shape, BF),
-        sds((3 * NS + 8, chan), F32),
+        sds((NS, chan), F32),
+        sds((NS, chan), F32),
+        sds((NS, chan), F32),
+        sds((8, chan), F32),
     )
     return launch(
         functools.partial(last_kernel, n),
         LAST_IN,
         args,
         outs,
-        [True, True, False, False, True],
+        [True, True, False, False, True, True, True, True],
         scratch,
         2,
         62,
@@ -1395,23 +1412,43 @@
 
 
 def finish(sum1, sum2, mixed, tokens_grad, end, small, width, units, chan):
-    across = width // chan
+    steps = width // chan
     sds = jax.ShapeDtypeStruct
     down_at = units * width // chan
-    tall = lambda high, at: pl.BlockSpec((high, chan), lambda j: (at // high + j, 0))
-    wide = lambda high: pl.BlockSpec((high, chan), lambda j: (0, j))
-    col = pl.BlockSpec((chan, chan), lambda j: (j, 0))
     micro, rows, _ = mixed.shape
-    same = [
-        pl.BlockSpec((micro, rows // across, width), lambda j: (0, j, 0)),
-        pl.BlockSpec((micro, rows // across, width), lambda j: (0, j, 0)),
-        pl.BlockSpec(end.shape, lambda j: (0, 0, 0)),
+
+    def panel(rows_of, at):
+        return (
+            pl.BlockSpec((rows_of, chan), lambda j: (at // rows_of + j, 0)),
+            pl.BlockSpec((rows_of, chan), lambda j: (0, j)),
+        )
+
+    def column(at):
+        high = width // steps
+        return (
+            pl.BlockSpec((high, chan), lambda j: (at // high + j, 0)),
+            pl.BlockSpec((high, chan), lambda j: (j, 0)),
+        )
+
+    same = pl.BlockSpec((micro, rows // steps, width), lambda j: (0, j, 0))
+    whole = pl.BlockSpec(end.shape, lambda j: (0, 0, 0))
+    specs = [
+        panel(width, 0),
+        panel(units, down_at),
+        panel(chan, 3 * width),
+        column(0),
+        column(width),
+        column(2 * width),
+        (same, same),
+        (same, same),
+        (whole, whole),
+    ] + [
+        (pl.BlockSpec(a.shape, lambda j: (0, 0)), pl.BlockSpec(a.shape, lambda j: (0, 0)))
+        for a in small
     ]
-    states = [pl.BlockSpec((NS, chan), lambda j, i=i: (i, 0)) for i in range(3)]
-    alone = [pl.BlockSpec((NS, chan), lambda j: (0, 0))] * 3
     return pl.pallas_call(
         finish_kernel,
-        grid=(across,),
+        grid=(steps,),
         out_shape=(
             sds((width, units), F32),
             sds((units, width), F32),
@@ -1422,24 +1459,13 @@
             sds(mixed.shape, BF),
             sds(tokens_grad.shape, F32),
             sds(end.shape, F32),
-            sds((NS, chan), F32),
-            sds((NS, chan), F32),
-            sds((NS, chan), F32),
+            *(sds(a.shape, F32) for a in small),
         ),
-        in_specs=[
-            tall(width, 0),
-            tall(units, down_at),
-            tall(chan, 3 * width),
-            tall(chan, 0),
-            tall(chan, width),
-            tall(chan, 2 * width),
-        ]
-        + same
-        + states,
-        out_specs=tuple([wide(width), wide(units), wide(chan), col, col, col] + same + alone),
+        in_specs=[a for a, _ in specs],
+        out_specs=tuple(b for _, b in specs),
         compiler_params=pltpu.CompilerParams(vmem_limit_bytes=62 << 20),
         name="finish",
-    )(sum1, sum1, sum2, sum2, sum2, sum2, mixed, tokens_grad, end, small, small, small)
+    )(sum1, sum1, sum2, sum2, sum2, sum2, mixed, tokens_grad, end, *small)
 
 
 def body(
@@ -1464,9 +1490,7 @@
     chan = ssm_rate.shape[0]
     units = w_up.shape[1]
     rate, cin, cout = ssm_rate.T, ssm_in.T, ssm_out.T
-    flags = resets[:, 0]
-    keep = jnp.pad(1.0 - flags.astype(F32), (0, 8 - micro))
-    keep = jnp.broadcast_to(keep[:, None], (8, chan))
+    keep = jnp.broadcast_to(1.0 - resets.astype(F32), (micro, chan))
     init = jnp.swapaxes(init_state, 1, 2)
     endg = jnp.swapaxes(states_grad[:, 0], 1, 2)
     gain_row, mid_row = norm_gain[None], mid_gain[None]
@@ -1474,28 +1498,30 @@
         *(tokens, gain_row, w_key, w_value, w_query, rate, cin, cout, keep, init, out_grad),
         *(w_out, mid_row, w_up, w_down),
     )
-    mixed, tokens_grad, sum1, sum2, small = last(
+    mixed, tokens_grad, sum1, sum2, rate_g, in_g, out_g, gains = last(
         *(q, k, v, lse, att, w_out, nf, ctx, w_query, w_key, w_value, rate, cin, cout),
         *(start, keep, endg, mlp, h1, dm, out_grad, mid_row, tokens, gain_row, ffn),
     )
-    done = finish(sum1, sum2, mixed, tokens_grad, end, small, width, units, chan)
+    done = finish(
+        sum1, sum2, mixed, tokens_grad, end, (rate_g, in_g, out_g), width, units, chan
+    )
     up_g, down_g, proj_g, query_g, key_g, value_g, mixed, tokens_grad, end = done[:9]
-    rate_g, in_g, out_g = (part.T for part in done[9:])
+    rate_g, in_g, out_g = done[9:]
     return (
         mixed,
         jnp.swapaxes(end, 1, 2)[:, None],
         tokens_grad,
-        small[3 * NS],
+        gains[0],
         query_g,
         key_g,
         value_g,
         proj_g,
-        small[3 * NS + 1],
+        gains[1],
         up_g,
         down_g,
-        rate_g,
-        in_g,
-        out_g,
+        rate_g.T,
+        in_g.T,
+        out_g.T,
     )
 
 

time: 291 us -> 284 us (0.976)
  Pallas kernels: 287 us -> 280 us
    pallas_call x2, Pallas kernels: 278 us -> 271 us  [launch(): pl.pallas_call(kernel, out_shape=tuple(outs), in_specs=[pl.BlockSpec(memo...]
where the time goes in v4:
time: 284 us; the launch traced here: 283 us
  Pallas kernels  280 us (99%)
    pallas_call x2, Pallas kernels, launch(): pl.pallas_call(kernel, out_shape=tuple(outs), in_specs=[pl.BlockSpec(memo...  271 us
    pallas_call x1, Pallas kernels, finish(): pl.pallas_call(finish_kernel, grid=(steps,), out_shape=(sds((width, units...  8.81 us

profile of v4, /device:TPU:0, one launch (start us, length us, event | category | flops | bytes accessed | tf_op | source)
XLA Modules:
  0.0 283.4 jit_solution(15624453399578738604)
XLA Ops:
  0.6 0.7 subtract_bitcast_fusion
  1.3 0.6 broadcast_in_dim.18.refs_8_.refs_15_
  2.0 83.6 %forward.1 = (bf16[2,512,1024]{2,1,0:T(8,128)(2,1)}, bf16[2,512,256]{2,1,0:T(8,128)(2,1)}, bf16[2,1152,256]{2,1,0:T(8,128)(2,1)}, bf16[2,1152,256]{2,1,0:T(8,128...) custom-call(bf16[2,128,1024]{2,1,0:T(8,128)(2,1)} %refs_22_.1, ...), custom_call_target="tpu_custom_call" | custom-call | tf_op jit(solution)/shard_map/forward/pallas_call | solution.py:443
  85.6 187.5 %last.1 = (bf16[2,128,1024]{2,1,0:T(8,128)(2,1)}, f32[2,128,1024]{2,1,0:T(8,128)}, bf16[8192,256]{1,0:T(8,128)(2,1)}, bf16[4096,256]{1,0:T(8,128)(2,1)}, f32[16,...) custom-call(bf16[2,512,256]{2,1,0:T(8,128)(2,1)} %get-tuple-element.47.refs_0_, ...), custom_call_target="tpu_custom_call" | custom-call | tf_op jit(solution)/shard_map/last/pallas_call | solution.py:443
  273.1 1.3 fusion
  274.4 8.8 %finish.1 = (f32[1024,1024]{1,0:T(8,128)}, f32[1024,1024]{1,0:T(8,128)}, f32[256,1024]{1,0:T(8,128)}, f32[1024,256]{1,0:T(8,128)}, f32[1024,256]{1,0:T(8,128)}, ...) custom-call(bf16[8192,256]{1,0:T(8,128)(2,1)} %get-tuple-element.59., ...), custom_call_target="tpu_custom_call" | custom-call | tf_op jit(solution)/shard_map/finish/pallas_call | solution.py:1449

commit v5 on v4

--- a/solution.py
+++ b/solution.py
@@ -14,6 +14,7 @@
 
 eps_norm = 1e-06
 neg_big = -1e30
+LOG2E = 1.4426950408889634
 MESH = pl.DeviceIdType.MESH
 VM = pltpu.VMEM
 BF = jnp.bfloat16
@@ -164,7 +165,7 @@
     "rate",
     "cin",
     "cout",
-    "keep",
+    "flag",
     "init",
     "ogm",
     "w_out",
@@ -195,11 +196,12 @@
     own = pl.ds(pl.multiple_of(me * own_rows, own_rows), own_rows)
     held = dict(held, ogm=og.at[:, own, :])
     fetch = Fetch(FORWARD_IN, refs_in, held, scr["fetch"])
-    nf_d, q_d, k_d, v_d, ctx_d, start_o, end_o = outs[:7]
+    nf_d, q_d, k_d, v_d, ctx_d, keep_d, start_o, end_o = outs[:8]
     nf, q_o, k_o, v_o, ctx_o = (scr[x] for x in ("nf", "q", "k", "v", "ctxa"))
     save = Save(scr["save"])
     grad_gathers = [Gather(og.at[m], scr["os"].at[m], scr["or"].at[m]) for m in range(2)]
-    tok, rate, keep, init = (held[x] for x in ("tok", "rate", "keep", "init"))
+    tok, rate, flag, init = (held[x] for x in ("tok", "rate", "flag", "init"))
+    keep = scr["keep"]
     wq, wk, wv = held["wq"], held["wk"], held["wv"]
     u_s, gath, pay, y_s, ctx_s = (scr[x] for x in ("u", "gath", "pay", "y", "ctx"))
     block = nf.shape[1]
@@ -276,7 +278,10 @@
     relay[1].start()
     relay[0].start()
     relay[1].wait_recv()
-    fetch.need("rate", "cin", "cout", "keep", "init")
+    fetch.need("rate", "cin", "cout", "flag", "init")
+    for m in range(2):
+        keep[m : m + 1, :] = jnp.broadcast_to(1.0 - flag[m : m + 1, :].astype(F32), (1, chan))
+    save(keep, keep_d)
     cols = lanes(me)
     for m in range(2):
         u_s[m] = nf[m, :, cols].astype(F32)
@@ -404,7 +409,7 @@
     save(k_o, k_d)
     save(v_o, v_d)
     save(ctx_o, ctx_d)
-    forward_middle(fetch, held, scr, outs[7:], save, q_o, k_o, v_o, og, grad_gathers)
+    forward_middle(fetch, held, scr, outs[8:], save, q_o, k_o, v_o, og, grad_gathers)
 
     @pl.when(s < n - 1)
     def _():
@@ -467,9 +472,10 @@
 def forward_middle(fetch, held, scr, outs, save, q, k, v, og, grad_gathers):
     nm, pm, dm, hid, dpre = (scr[x] for x in ("nm", "pm", "dm", "hid", "dpre"))
     mlp_o, h1_o, ffn_o, att, lse = (scr[x] for x in ("mlp", "h1", "ffn", "att", "lse"))
-    keep, w_out, tok, gain, w_up, w_down = (
-        held[x] for x in ("keep", "w_out", "tok", "mid", "w_up", "w_down")
+    w_out, tok, gain, w_up, w_down = (
+        held[x] for x in ("w_out", "tok", "mid", "w_up", "w_down")
     )
+    keep = scr["keep"]
     me = tp_peers()[0]
     near = me // 2
     block = q.shape[1]
@@ -482,7 +488,7 @@
     half = block // 2
     row_ids = lax.broadcasted_iota(jnp.int32, (half, half), 0)
     col_ids = lax.broadcasted_iota(jnp.int32, (half, half), 1)
-    scale = HD ** (-0.5)
+    scale = HD ** (-0.5) * LOG2E
 
     def attend(m):
         def one(head, c):
@@ -498,12 +504,11 @@
                 pieces.append(jnp.where(row_ids <= col_ids, sc[edge:], neg_big))
                 sc = jnp.concatenate(pieces, axis=0)
                 top = jnp.max(sc, axis=0, keepdims=True)
-                expo = jnp.exp(sc - top)
+                expo = jnp.exp2(sc - top)
                 total = jnp.sum(expo, axis=0, keepdims=True)
-                weights = (expo * (1.0 / total)).astype(BF)
-                res = dot(v[m, 0 : edge + half, lanes], weights, TN)
+                res = dot(v[m, 0 : edge + half, lanes], expo.astype(BF), TN) * (1.0 / total)
                 att[m, mine, lanes] = res.T.astype(BF)
-                lse[m, head, :, mine] = top + jnp.log(total)
+                lse[m, head, :, mine] = top + LOG2E * jnp.log(total)
             return c
 
         lax.fori_loop(0, q.shape[2] // HD, one, 0)
@@ -603,20 +608,18 @@
     save(dm.at[1], dm_d.at[1])
 
     def down_sum(i, c):
-        left = hid[:, pl.ds(pl.multiple_of(i * tile, tile), tile)]
+        left = hid[:, pl.ds(pl.multiple_of(i * tile, tile), tile)].T
         for j in range(width // tile):
             right = og[:, :, j * tile : (j + 1) * tile].reshape(2 * block, tile)
             at = pl.multiple_of((width // tile + j) * panels * tile + i * tile, tile)
-            ffn_o[pl.ds(at, tile), :] = dot(left, right, TN).astype(BF)
+            ffn_o[pl.ds(at, tile), :] = dot(left, right).astype(BF)
         return c
 
     def up_sum(i, c):
-        left = nm[:, :, pl.ds(pl.multiple_of(i * tile, tile), tile)].reshape(2 * block, tile)
+        left = nm[:, :, pl.ds(pl.multiple_of(i * tile, tile), tile)].reshape(2 * block, tile).T
         for j in range(panels):
             at = pl.multiple_of(j * width + i * tile, tile)
-            ffn_o[pl.ds(at, tile), :] = dot(
-                left, dpre[:, j * tile : (j + 1) * tile], TN
-            ).astype(BF)
+            ffn_o[pl.ds(at, tile), :] = dot(left, dpre[:, j * tile : (j + 1) * tile]).astype(BF)
         return c
 
     high = panels * tile * (width // tile)
@@ -647,6 +650,7 @@
         k=sds((micro, keys, chan), BF),
         v=sds((micro, keys, chan), BF),
         ctxa=sds((micro, CTX, width), BF),
+        keep=sds((micro, chan), F32),
         start=sds((micro, NS, chan), F32),
         end=sds((micro, NS, chan), F32),
         mlp=sds((micro, block, width), BF),
@@ -860,7 +864,7 @@
     h = dict(h, ffn=x1.at[0:ffn_rows])
     fetch = Fetch(LAST_IN, refs_in, h, scr["fetch"])
     need = fetch.need
-    mixed_o, tg_o, sum1_o, sum2_o, rate_o, cin_o, cout_o, gain_o = outs
+    mixed_o, tg_o, sum1_o, sum2_o, rate_o, cin_o, cout_o, norm_o, mid_o = outs
     s = lax.axis_index("seq")
     me, mate, across, diag = tp_peers()
     peers = (mate, across, diag)
@@ -944,13 +948,13 @@
             qq = q[m, mine, lanes]
             kk = k[m, 0 : edge + half, lanes]
             dd = da[m, mine, lanes]
-            sc = dot(kk, qq, NT) * scale
+            sc = dot(kk, qq, NT) * (scale * LOG2E)
             pieces = [sc[:edge0] + shut]
             if part:
                 pieces.append(sc[edge0:edge])
             pieces.append(jnp.where(row_ids <= col_ids, sc[edge:], neg_big))
             sc = jnp.concatenate(pieces, axis=0)
-            probs = jnp.exp(sc - lse[m, head, :, mine])
+            probs = jnp.exp2(sc - lse[m, head, :, mine])
             dp = dot(v[m, 0 : edge + half, lanes], dd, NT)
             spread_sum = jnp.sum(probs * dp, axis=0, keepdims=True)
             ds = (probs * (dp - spread_sum)).astype(BF)
@@ -1051,14 +1055,14 @@
     for c in mlp_sums:
         c.turn()
     need("att")
-    flat_att = h["att"][...].reshape(2 * block, chan)
+    flat_att = h["att"][...].reshape(2 * block, chan).T
     tile = 256
 
     def proj(j, c):
         cols = pl.ds(pl.multiple_of(j * tile, tile), tile)
         right = rr[:, :, cols].reshape(2 * block, tile)
         at = pl.multiple_of(3 * width + j * tile, tile)
-        x2[pl.ds(at, tile), :] = dot(flat_att, right, TN).astype(BF)
+        x2[pl.ds(at, tile), :] = dot(flat_att, right).astype(BF)
         here = pl.ds(pl.multiple_of(j * tile, tile), tile)
         left = nf[:, :, here].reshape(2 * block, tile)
         x2[here, :] = dot(left, dq_s[...].reshape(2 * block, chan), TN).astype(BF)
@@ -1129,11 +1133,11 @@
     def kv_grads(i, c):
         at = pl.multiple_of(i * tile, tile)
         here = pl.ds(at, tile)
-        left = nf[:, :, here].reshape(2 * block, tile)
-        left_ctx = ctx[:, :, here].reshape(2 * CTX, tile)
+        left = nf[:, :, here].reshape(2 * block, tile).T
+        left_ctx = ctx[:, :, here].reshape(2 * CTX, tile).T
         for j, (own, far) in enumerate(((dk_b, dkc), (dv_b, dvc))):
-            value = dot(left, own[...].reshape(2 * block, chan), TN) + dot(
-                left_ctx, far[...].reshape(2 * CTX, chan), TN
+            value = dot(left, own[...].reshape(2 * block, chan)) + dot(
+                left_ctx, far[...].reshape(2 * CTX, chan)
             )
             x2[pl.ds((j + 1) * width + at, tile), :] = value.astype(BF)
         return c
@@ -1274,7 +1278,8 @@
     for k in range(1, n):
         gain_out(k).wait_recv()
         total = total + gg[k]
-    gain_o[...] = total
+    norm_o[...] = total[0:1]
+    mid_o[...] = total[1:2]
     for k in range(1, n):
         gain_out(k).wait_send()
     for c in gains + ctx_out:
@@ -1389,14 +1394,15 @@
         sds((NS, chan), F32),
         sds((NS, chan), F32),
         sds((NS, chan), F32),
-        sds((8, chan), F32),
+        sds((1, chan), F32),
+        sds((1, chan), F32),
     )
     return launch(
         functools.partial(last_kernel, n),
         LAST_IN,
         args,
         outs,
-        [True, True, False, False, True, True, True, True],
+        [True, True, False, False, True, True, True, True, True],
         scratch,
         2,
         62,
@@ -1490,33 +1496,31 @@
     chan = ssm_rate.shape[0]
     units = w_up.shape[1]
     rate, cin, cout = ssm_rate.T, ssm_in.T, ssm_out.T
-    keep = jnp.broadcast_to(1.0 - resets.astype(F32), (micro, chan))
+    flag = jnp.broadcast_to(resets, (micro, chan))
     init = jnp.swapaxes(init_state, 1, 2)
     endg = jnp.swapaxes(states_grad[:, 0], 1, 2)
     gain_row, mid_row = norm_gain[None], mid_gain[None]
-    nf, q, k, v, ctx, start, end, mlp, h1, dm, ffn, att, lse = forward(
-        *(tokens, gain_row, w_key, w_value, w_query, rate, cin, cout, keep, init, out_grad),
+    nf, q, k, v, ctx, keep, start, end, mlp, h1, dm, ffn, att, lse = forward(
+        *(tokens, gain_row, w_key, w_value, w_query, rate, cin, cout, flag, init, out_grad),
         *(w_out, mid_row, w_up, w_down),
     )
-    mixed, tokens_grad, sum1, sum2, rate_g, in_g, out_g, gains = last(
+    mixed, tokens_grad, sum1, sum2, *small = last(
         *(q, k, v, lse, att, w_out, nf, ctx, w_query, w_key, w_value, rate, cin, cout),
         *(start, keep, endg, mlp, h1, dm, out_grad, mid_row, tokens, gain_row, ffn),
     )
-    done = finish(
-        sum1, sum2, mixed, tokens_grad, end, (rate_g, in_g, out_g), width, units, chan
-    )
+    done = finish(sum1, sum2, mixed, tokens_grad, end, small, width, units, chan)
     up_g, down_g, proj_g, query_g, key_g, value_g, mixed, tokens_grad, end = done[:9]
-    rate_g, in_g, out_g = done[9:]
+    rate_g, in_g, out_g, norm_g, mid_g = done[9:]
     return (
         mixed,
         jnp.swapaxes(end, 1, 2)[:, None],
         tokens_grad,
-        gains[0],
+        norm_g[0],
         query_g,
         key_g,
         value_g,
         proj_g,
-        gains[1],
+        mid_g[0],
         up_g,
         down_g,
         rate_g.T,

time: 284 us -> 281 us (0.989)
  no operation moved by 1% of the time
where the time goes in v5:
time: 281 us
  Pallas kernels  279 us (99%)
    pallas_call x2, Pallas kernels, launch(): pl.pallas_call(kernel, out_shape=tuple(outs), in_specs=[pl.BlockSpec(memo...  270 us
    pallas_call x1, Pallas kernels, finish(): pl.pallas_call(finish_kernel, grid=(steps,), out_shape=(sds((width, units...  8.88 us

profile of v5, /device:TPU:0, one launch (start us, length us, event | category | flops | bytes accessed | tf_op | source)
XLA Modules:
  0.0 280.8 jit_solution(8703560093861485119)
XLA Ops:
  0.6 1.3 broadcast_in_dim.18.refs_8_
  1.9 82.8 %forward.1 = (bf16[2,512,1024]{2,1,0:T(8,128)(2,1)}, bf16[2,512,256]{2,1,0:T(8,128)(2,1)}, bf16[2,1152,256]{2,1,0:T(8,128)(2,1)}, bf16[2,1152,256]{2,1,0:T(8,128...) custom-call(bf16[2,128,1024]{2,1,0:T(8,128)(2,1)} %refs_22_.1, ...), custom_call_target="tpu_custom_call" | custom-call | tf_op jit(solution)/shard_map/forward/pallas_call | solution.py:448
  84.8 187.0 %last.1 = (bf16[2,128,1024]{2,1,0:T(8,128)(2,1)}, f32[2,128,1024]{2,1,0:T(8,128)}, bf16[8192,256]{1,0:T(8,128)(2,1)}, bf16[4096,256]{1,0:T(8,128)(2,1)}, f32[16,...) custom-call(bf16[2,512,256]{2,1,0:T(8,128)(2,1)} %get-tuple-element.51.refs_0_, ...), custom_call_target="tpu_custom_call" | custom-call | tf_op jit(solution)/shard_map/last/pallas_call | solution.py:448
  271.8 8.9 %finish.1 = (f32[1024,1024]{1,0:T(8,128)}, f32[1024,1024]{1,0:T(8,128)}, f32[256,1024]{1,0:T(8,128)}, f32[1024,256]{1,0:T(8,128)}, f32[1024,256]{1,0:T(8,128)}, ...) custom-call(bf16[8192,256]{1,0:T(8,128)(2,1)} %get-tuple-element.64., ...), custom_call_target="tpu_custom_call" | custom-call | tf_op jit(solution)/shard_map/finish/pallas_call | solution.py:1455

commit v6 on v5

--- a/solution.py
+++ b/solution.py
@@ -830,31 +830,31 @@
 
 
 LAST_IN = (
+    "dm",
+    "ffn",
+    "nf",
+    "rate",
+    "cin",
+    "cout",
+    "start",
+    "endg",
+    "h1",
+    "ogm",
+    "mid",
+    "w_out",
+    "keep",
     "q",
     "k",
     "v",
     "lse",
     "att",
-    "w_out",
-    "nf",
     "ctx",
     "wq",
     "wk",
     "wv",
-    "rate",
-    "cin",
-    "cout",
-    "start",
-    "keep",
-    "endg",
     "mlp",
-    "h1",
-    "dm",
-    "ogm",
-    "mid",
     "tok",
     "gain",
-    "ffn",
 )
 
 
@@ -918,6 +918,29 @@
     ring1.start()
     for c in mid_sums:
         c.turn()
+    u_s, du_s, hist = scr["u"], scr["du"], scr["hist"]
+    cols = pl.ds(pl.multiple_of(me * chan, chan), chan)
+    need("nf", "rate", "cin", "cout", "start", "endg")
+    for m in range(2):
+        u_s[m] = nf[m, :, cols].astype(F32)
+    decay = jnp.exp(-rate[...])
+    root = jnp.sqrt(1.0 - decay * decay)
+    drive = root * h["cin"][...]
+    out_c = h["cout"][...]
+    start, endg = h["start"], h["endg"]
+    for m in range(2):
+        hist[0, m] = start[m].astype(BF)
+
+    def run(i, state):
+        base = pl.multiple_of(i * 8, 8)
+        state = list(state)
+        for k in range(8):
+            for m in range(2):
+                state[m] = decay * state[m] + drive * u_s[m, pl.ds(base + k, 1), :]
+                hist[base + k + 1, m] = state[m].astype(BF)
+        return tuple(state)
+
+    lax.fori_loop(0, block // 8, run, (start[0], start[1]))
     need("h1", "ogm", "mid")
     mid_grad = jnp.zeros((1, width), F32)
     for m in range(2):
@@ -979,19 +1002,25 @@
 
     def stream_back(m, c):
         g = Gather(rr.at[m], scr["rs"].at[m], scr["rrv"].at[m])
-        g.near()
-        g.pass_on()
         g.far()
         ring1.tick(m + ring1.done)
         da[m] = dot(rr[m], w_out[...], NT).astype(BF)
 
         def heads(head, c):
             attend_one(m, head)
+
+            @pl.when((m == 0) & (head == 0))
+            def _():
+                gathers[1].near()
+                gathers[1].pass_on()
+
             return c
 
         lax.fori_loop(0, chan // HD, heads, 0)
         return c
 
+    gathers[0].near()
+    gathers[0].pass_on()
     lax.fori_loop(0, 2, stream_back, 0)
     ring1.done += 2
 
@@ -1009,51 +1038,21 @@
             src, dst, scr["send_c"].at[kind, i], scr["recv_c"].at[kind, i], tp=peers[i]
         )
 
-    ctx_out = [to_peer(i, cp.at[peers[i]], cr.at[i], 0) for i in range(3)]
-    for c in ctx_out:
-        c.start()
+    ctx_out = [
+        remote(cp.at[q], cr.at[i], scr["send_c"].at[0, i], scr["recv_c"].at[0, i], tp=peer)
+        for i, (q, peer) in enumerate(((diag, mate), (mate, mate), (across, across)))
+    ]
+    ctx_out[0].start()
+    ctx_out[1].start()
     need("mlp")
     mlp_sums = [scatter(mlp, 1, m) for m in range(2)]
     for c in mlp_sums:
         c.start()
+    ctx_out[0].wait_recv()
+    cp[across] = (cp[across].astype(F32) + cr[0].astype(F32)).astype(BF)
+    ctx_out[2].start()
     ring1.go(5)
 
-    u_s, du_s, hist = scr["u"], scr["du"], scr["hist"]
-    cols = pl.ds(pl.multiple_of(me * chan, chan), chan)
-    need("nf", "rate", "cin", "cout", "start", "endg")
-    for m in range(2):
-        u_s[m] = nf[m, :, cols].astype(F32)
-    decay = jnp.exp(-rate[...])
-    root = jnp.sqrt(1.0 - decay * decay)
-    drive = root * h["cin"][...]
-    out_c = h["cout"][...]
-    start, endg = h["start"], h["endg"]
-    for m in range(2):
-        hist[0, m] = start[m].astype(BF)
-
-    def run(i, state):
-        base = pl.multiple_of(i * 8, 8)
-        state = list(state)
-        for k in range(8):
-            for m in range(2):
-                state[m] = decay * state[m] + drive * u_s[m, pl.ds(base + k, 1), :]
-                hist[base + k + 1, m] = state[m].astype(BF)
-        return tuple(state)
-
-    lax.fori_loop(0, block // 8, run, (start[0], start[1]))
-    ctx_back = to_before(0, 4, dcs, dcr)
-    total = cp[me].astype(F32)
-    for i in range(3):
-        ctx_out[i].wait_recv()
-        total = total + cr[i].astype(F32)
-    dcs[...] = total.astype(BF)
-
-    @pl.when(s > 0)
-    def _():
-        ctx_back.start()
-
-    for c in mlp_sums:
-        c.turn()
     need("att")
     flat_att = h["att"][...].reshape(2 * block, chan).T
     tile = 256
@@ -1068,8 +1067,21 @@
         x2[here, :] = dot(left, dq_s[...].reshape(2 * block, chan), TN).astype(BF)
         return c
 
+    lax.fori_loop(0, width // tile, proj, 0)
+    ctx_back = to_before(0, 4, dcs, dcr)
+    total = cp[me].astype(F32)
+    for i in (1, 2):
+        ctx_out[i].wait_recv()
+        total = total + cr[i].astype(F32)
+    dcs[...] = total.astype(BF)
+
+    @pl.when(s > 0)
+    def _():
+        ctx_back.start()
+
+    for c in mlp_sums:
+        c.turn()
     ring1.go(6)
-    lax.fori_loop(0, width // tile, proj, 0)
 
     @pl.when(s < n - 1)
     def _():
@@ -1505,8 +1517,8 @@
         *(w_out, mid_row, w_up, w_down),
     )
     mixed, tokens_grad, sum1, sum2, *small = last(
-        *(q, k, v, lse, att, w_out, nf, ctx, w_query, w_key, w_value, rate, cin, cout),
-        *(start, keep, endg, mlp, h1, dm, out_grad, mid_row, tokens, gain_row, ffn),
+        *(dm, ffn, nf, rate, cin, cout, start, endg, h1, out_grad, mid_row, w_out),
+        *(keep, q, k, v, lse, att, ctx, w_query, w_key, w_value, mlp, tokens, gain_row),
     )
     done = finish(sum1, sum2, mixed, tokens_grad, end, small, width, units, chan)
     up_g, down_g, proj_g, query_g, key_g, value_g, mixed, tokens_grad, end = done[:9]

time: 281 us -> 276 us (0.982)
  Pallas kernels: 279 us -> 274 us
    pallas_call x2, Pallas kernels: 270 us -> 265 us  [launch(): pl.pallas_call(kernel, out_shape=tuple(outs), in_specs=[pl.BlockSpec(memo...]
where the time goes in v6:
time: 276 us
  Pallas kernels  274 us (99%)
    pallas_call x2, Pallas kernels, launch(): pl.pallas_call(kernel, out_shape=tuple(outs), in_specs=[pl.BlockSpec(memo...  265 us
    pallas_call x1, Pallas kernels, finish(): pl.pallas_call(finish_kernel, grid=(steps,), out_shape=(sds((width, units...  8.88 us

profile of v6, /device:TPU:0, one launch (start us, length us, event | category | flops | bytes accessed | tf_op | source)
XLA Modules:
  0.0 276.1 jit_solution(8063920868683896330)
XLA Ops:
  0.6 1.3 broadcast_in_dim.18.refs_8_
  1.9 82.8 %forward.1 = (bf16[2,512,1024]{2,1,0:T(8,128)(2,1)}, bf16[2,512,256]{2,1,0:T(8,128)(2,1)}, bf16[2,1152,256]{2,1,0:T(8,128)(2,1)}, bf16[2,1152,256]{2,1,0:T(8,128...) custom-call(bf16[2,128,1024]{2,1,0:T(8,128)(2,1)} %refs_23_.1, ...), custom_call_target="tpu_custom_call" | custom-call | tf_op jit(solution)/shard_map/forward/pallas_call | solution.py:448
  84.8 182.3 %last.1 = (bf16[2,128,1024]{2,1,0:T(8,128)(2,1)}, f32[2,128,1024]{2,1,0:T(8,128)}, bf16[8192,256]{1,0:T(8,128)(2,1)}, bf16[4096,256]{1,0:T(8,128)(2,1)}, f32[16,...) custom-call(bf16[2,512,1024]{2,1,0:T(8,128)(2,1)} %get-tuple-element.51.refs_0_,, ...), custom_call_target="tpu_custom_call" | custom-call | tf_op jit(solution)/shard_map/last/pallas_call | solution.py:448
  267.1 8.9 %finish.1 = (f32[1024,1024]{1,0:T(8,128)}, f32[1024,1024]{1,0:T(8,128)}, f32[256,1024]{1,0:T(8,128)}, f32[1024,256]{1,0:T(8,128)}, f32[1024,256]{1,0:T(8,128)}, ...) custom-call(bf16[8192,256]{1,0:T(8,128)(2,1)} %get-tuple-element.64., ...), custom_call_target="tpu_custom_call" | custom-call | tf_op jit(solution)/shard_map/finish/pallas_call | solution.py:1467
